TPU v7x, 768 devices: a whole 4x8x12 slice. The times are simulated.
768 devices in a mesh: wide: 64 (over y, x, z_hi), narrow: 12 (over z_lo, core).
Axes of the slice: x: 4, y: 8, z: 12 (z_hi: 2, z_lo: 6; z = z_hi * 6 + z_lo), core: 2. Of those that a mesh axis runs over, the one named last changes fastest.
Arguments:
- hidden: bfloat16 [12, 16384, 5120], P('narrow', 'wide'), may hold values from -28 to 28
- segment: int32 [12, 16384], P('narrow', 'wide'), may hold values from 0 to 19, as said below
- grades: int32 [12, 4, 20], P('narrow'), may hold values from 0 to 4
- value_codes: bfloat16 [5120, 128], P('wide'), may hold values from -0.078125 to 0.078125
- value_scale: float32 [128], replicated, may hold values from 0.25 to 1.75
- output_codes: bfloat16 [5120, 128], P('wide'), may hold values from -0.5 to 0.5
- output_scale: bfloat16 [5120], P('wide'), may hold values from 0.25 to 1.75
- norm_gain: bfloat16 [5120], P('wide'), may hold values from 0.5 to 1.5
- final_gain: bfloat16 [5120], P('wide'), may hold values from 0.5 to 1.5
- score_vector: bfloat16 [5120], P('wide'), may hold values from -1 to 1
Outputs:
- value_grad: float32 [5120, 128], P('wide')
- output_grad: float32 [5120, 128], P('wide')
- list_loss: float32 [12, 4], P('narrow')
Inputs may be any that keep to these rules, and one draw needn't show every extreme that they name: `segment`: within each list the candidate numbers never fall, and every candidate 0 to 19 holds 1 to 2048 tokens; one candidate of every list holds exactly 2048.
All inputs are finite; a program needn't handle non-finite values.
Results may differ from a plain program's by a relative error of at most 0.025.
Values may be sent and summed in bfloat16 or wider, within the bound.
No kernel may reach another device: no remote copies, remote signals or barrier semaphores. Data moves between devices by JAX's collectives and lax.ppermute only.
A program may use at most 64 MiB of HBM per device.

v0:
```python
import jax
import jax.numpy as jnp
from jax import lax
from jax.sharding import PartitionSpec as P

EPSILON = 1e-06
SOFT_CAP = 30.0


def contract_rows(left, right):
    return lax.dot_general(
        left, right, (((0,), (0,)), ((), ())), preferred_element_type=jnp.float32
    )


def shards(
    hidden,
    segment,
    grades,
    value_codes,
    value_scale,
    output_codes,
    output_scale,
    norm_gain,
    final_gain,
    score_vector,
):
    head_size = value_codes.shape[1]
    tokens32 = hidden[0].astype(jnp.float32)
    seg_local = segment[0]
    grade_rows = grades[0]
    group_lists, cand_count = grade_rows.shape
    span = lax.axis_size("wide") // group_lists
    list_pick = (jnp.arange(group_lists, dtype=jnp.int32) == lax.axis_index("wide") // span).astype(
        jnp.float32
    )
    root_mean = jnp.sqrt(jnp.mean(tokens32 * tokens32, axis=-1, keepdims=True) + EPSILON)
    value_full, out_full, scale_full, gain_full, final_full, score_full = (
        lax.all_gather(value_codes, "wide", axis=0, tiled=True),
        lax.all_gather(output_codes, "wide", axis=0, tiled=True),
        lax.all_gather(output_scale, "wide", axis=0, tiled=True),
        lax.all_gather(norm_gain, "wide", axis=0, tiled=True),
        lax.all_gather(final_gain, "wide", axis=0, tiled=True),
        lax.all_gather(score_vector, "wide", axis=0, tiled=True),
    )
    normed = (tokens32 / root_mean * gain_full.astype(jnp.float32)).astype(jnp.bfloat16)
    mixed = jnp.dot(normed, value_full, preferred_element_type=jnp.float32)
    value_half = (mixed * value_scale).astype(jnp.bfloat16)
    scale32 = scale_full.astype(jnp.float32)
    branch = lax.dot_general(
        value_half, out_full, (((1,), (1,)), ((), ())), preferred_element_type=jnp.float32
    )
    residual = (tokens32 + branch * scale32).astype(jnp.bfloat16)
    resid32 = residual.astype(jnp.float32)
    width = resid32.shape[1]
    final_root = jnp.sqrt(jnp.mean(resid32 * resid32, axis=-1) + EPSILON)
    weighted = final_full.astype(jnp.float32) * score_full.astype(jnp.float32)
    raw_score = jnp.sum(resid32 * weighted, axis=-1) / final_root
    capped = jnp.tanh(raw_score / SOFT_CAP)
    token_score = SOFT_CAP * capped
    member = (seg_local[:, None] == jnp.arange(cand_count, dtype=jnp.int32)).astype(jnp.float32)
    local_sums = jnp.dot(token_score, member)
    local_counts = jnp.sum(member, axis=0)
    sums, counts = lax.psum(
        (list_pick[:, None] * local_sums[None, :], list_pick[:, None] * local_counts[None, :]),
        "wide",
    )
    cand_score = sums / counts
    teacher = grade_rows.astype(jnp.float32)
    log_teacher = teacher - jnp.log(jnp.sum(jnp.exp(teacher), axis=-1, keepdims=True))
    log_student = cand_score - jnp.log(jnp.sum(jnp.exp(cand_score), axis=-1, keepdims=True))
    list_loss = jnp.sum(jnp.exp(log_teacher) * (log_teacher - log_student), axis=-1)
    grad_cand = (jnp.exp(log_student) - jnp.exp(log_teacher)) / counts
    own_grad = jnp.dot(list_pick, grad_cand)
    grad_token = jnp.dot(member, own_grad) * (1.0 - capped * capped)
    grad_resid = grad_token[:, None] * (
        weighted[None, :] / final_root[:, None]
        - resid32 * (raw_score / (width * final_root * final_root))[:, None]
    )
    grad_branch = (grad_resid * scale32).astype(jnp.bfloat16)
    grad_values = (
        jnp.dot(grad_branch, out_full, preferred_element_type=jnp.float32) * value_scale
    ).astype(jnp.bfloat16)
    terms = jnp.concatenate(
        [contract_rows(grad_branch, value_half), contract_rows(normed, grad_values)], axis=1
    )
    shard = lax.psum_scatter(terms, "wide", scatter_dimension=0, tiled=True)
    total = lax.psum(shard, "narrow")
    return (total[:, head_size:], total[:, :head_size], list_loss[None, :])


def solution(mesh):
    in_specs = (
        P("narrow", "wide", None),
        P("narrow", "wide"),
        P("narrow", None, None),
        P("wide", None),
        P(),
        P("wide", None),
        P("wide"),
        P("wide"),
        P("wide"),
        P("wide"),
    )
    out_specs = (P("wide", None), P("wide", None), P("narrow", None))
    return jax.shard_map(shards, mesh=mesh, in_specs=in_specs, out_specs=out_specs, check_vma=False)
```

profile of v0, /device:TPU:1, one launch (start us, length us, event | category | flops | bytes accessed | tf_op | source)
XLA Modules:
  0.0 1621.5 jit_solution(9391585526408328512)
XLA Ops:
  7.2 0.0 all-gather.3.cloned.1.call-start
  7.2 0.7 all-gather.3.cloned.1.call-update
  7.9 0.0 all-gather.5.cloned.1.call-start
  7.9 0.7 all-gather.5.cloned.1.call-update
  8.7 0.0 reduce-scatter.4.cloned.1.call-start
  8.7 0.8 fusion.16
  9.5 1.3 dynamic-slice
  11.5 0.9 dynamic-update-slice.3
  12.3 0.8 dynamic-update-slice.1
  13.2 0.8 dynamic-update-slice
  14.0 0.8 dynamic-update-slice.2
  14.9 480.4 %all-reduce.5 = (bf16[5120]{0:T(1024)(128)(2,1)S(1)}, bf16[5120]{0:T(1024)(128)(2,1)S(1)}, bf16[5120]{0:T(1024)(128)(2,1)S(1)}, bf16[5120]{0:T(1024)(128)(2,1)S(1)}) all-reduce(bf16[5120]{0:T(1024)(128)(2,1)S(1)} %dynamic-update-slice, bf16[5120]{0:T(1024)(128)(2,1)S(1)} %dynamic-update-slice.1, ...), channel_id=1, replica_groups=mesh['wide'=64,'narrow'=12] {'wide'}, use_global_device_ids=true, to_apply=%add | all-reduce | flops 20480 | bytes 81920
  495.2 0.0 copy-start.1
  495.3 0.9 convert_reduce_fusion
  496.2 2.3 fusion.6
  498.6 0.0 copy-done.1
  498.6 0.0 copy-start.3
  498.6 0.8 fusion.8
  499.4 0.0 copy-start
  499.4 0.0 all-gather.3.cloned.1.call-done
  499.4 0.0 copy-done.3
  499.4 3.1 fusion.9
  502.5 0.0 copy-start.4
  502.5 0.0 copy-start.2
  502.5 0.0 all-gather.5.cloned.1.call-done
  502.6 5.3 fusion.4
  507.8 0.0 copy-done
  507.9 0.0 copy-done.4
  507.9 0.1 convolution_bitcast_fusion.1
  508.0 0.1 broadcast_multiply_fusion.1
  508.1 226.2 %all-reduce.4 = (f32[4,20]{1,0:T(4,128)S(1)}, f32[4,20]{1,0:T(4,128)S(1)}) all-reduce(f32[4,20]{1,0:T(4,128)S(1)} %get-tuple-element.28, f32[4,20]{1,0:T(4,128)S(1)} %get-tuple-element.27), channel_id=1, replica_groups=mesh['wide'=64,'narrow'=12] {'wide'}, use_global_device_ids=true, to_apply=%region_5.6 | all-reduce | flops 160 | bytes 1280 | tf_op jit(solution)/shard_map/psum | solution.py:64
  734.3 0.1 exponential_reduce_fusion
  734.4 0.0 copy-done.2
  734.4 0.3 fusion.12
  734.8 3.5 fusion.5
  738.2 2.1 fusion.37
  740.4 5.0 fusion.11
  745.3 5.4 pad_maximum_fusion
  750.7 6.0 copy.19
  756.7 0.0 reduce-scatter.4.cloned.1.call-update
  756.7 0.0 all-reduce.8.cloned.1.call-start
  756.8 647.6 %reduce-scatter.4.cloned.1.call-done = f32[80,256]{1,0:T(8,128)} async-done(((f32[5120,256]{1,0:T(8,128)}), f32[80,256]{1,0:T(8,128)}) %reduce-scatter.4.cloned.1.call-update) | async-done | bytes 81936
  1404.4 1.6 copy.20
  1406.0 0.0 all-reduce.8.cloned.1.call-update
  1406.1 0.7 multiply_reduce_fusion
  1406.8 205.9 %all-reduce.8.cloned.1.call-done = f32[80,256]{0,1:T(8,128)} async-done(((f32[80,256]{0,1:T(8,128)}), f32[80,256]{0,1:T(8,128)}) %all-reduce.8.cloned.1.call-update) | async-done | bytes 81936 | tf_op jit(solution)/shard_map/psum | solution.py:88
  1612.6 0.9 fusion.36
  1613.5 0.7 copy.18
  1614.2 0.7 copy.17
  (13 shorter events, 0.1 us)
Async XLA Ops:
  7.2 492.3 %all-gather.3.cloned.1.call-start = ((), (), s32[]{:S(2)}) async-start(), calls=%async_computation.1 | async-start | bytes 1331200 | tf_op jit(solution)/shard_map/all_gather | solution.py:39
  7.9 494.6 %all-gather.5.cloned.1.call-start = ((), (), s32[]{:S(2)}) async-start(), calls=%async_computation.2 | async-start | bytes 1331200 | tf_op jit(solution)/shard_map/all_gather | solution.py:40
  8.7 1395.8 %reduce-scatter.4.cloned.1.call-start = ((), (), s32[]{:S(2)}) async-start(), calls=%async_computation.4 | async-start | bytes 5324800
  495.2 3.3 copy-start.1
  498.6 0.8 copy-start.3
  499.4 8.5 copy-start
  502.5 5.4 copy-start.4
  502.5 231.9 %copy-start.2 = (s32[1,4,20]{2,1,0:T(4,128)S(1)}, s32[1,4,20]{2,1,0:T(4,128)}, u32[]{:S(2)}) copy-start(s32[1,4,20]{2,1,0:T(4,128)} %param.12) | copy-start | bytes 964
  756.7 855.9 %all-reduce.8.cloned.1.call-start = ((), (), s32[]{:S(2)}) async-start(), calls=%async_computation.3 | async-start | bytes 262144 | tf_op jit(solution)/shard_map/psum | solution.py:88
Sparse Core Ops, SparseCore 0:
  13.4 153.3 all-gather.2
  172.2 140.6 all-gather.4
  756.8 647.5 reduce-scatter.3
  1407.5 205.1 all-reduce.7
where the time goes:
time: 1620 us
  waiting for transfers between devices  855 us (53%)
  blocking collectives  707 us (44%)
    unnamed x5, waiting for transfers between devices  649 us
    unnamed x1, blocking collectives  480 us
    psum x1, blocking collectives, shards(): lax.psum((list_pick[:, None] * local_sums[None, :], list_pick[:, None] *...  226 us
    psum x1, waiting for transfers between devices, shards(): total = lax.psum(shard, 'narrow')  206 us
  transfers between devices with their start and end apart: 4, of which 2 were waited for; matrix products, arithmetic and copies ran while one was open for 1% of the time, Pallas kernels for 0%

commit v1 on v0

v1 whole, which is shorter than its diff:
```python
import jax
import jax.numpy as jnp
from jax import lax
from jax.sharding import Mesh, PartitionSpec as P

EPSILON = 1e-06
SOFT_CAP = 30.0
YX = ("yh", "yl", "x")
WIDE = ("yh", "yl", "x", "zh")
NARROW = ("zl", "c")
Z = ("zh", "zl")
SWAP = [(0, 1), (1, 0)]


def half_partner():
    pairs = []
    for z in range(12):
        to = (z + 3) % 12 if z % 6 >= 3 else (z - 3) % 12
        pairs.append((z, to))
    return pairs


def contract_rows(left, right):
    return lax.dot_general(
        left, right, (((0,), (0,)), ((), ())), preferred_element_type=jnp.float32
    )


def shards(
    hidden,
    segment,
    grades,
    value_codes,
    value_scale,
    output_codes,
    output_scale,
    norm_gain,
    final_gain,
    score_vector,
):
    rows, head_size = value_codes.shape
    core = lax.axis_index("c")
    z_half = lax.axis_index("zh")
    first = core == 0
    tokens32 = hidden[0].astype(jnp.float32)
    width = tokens32.shape[1]
    seg_local = segment[0]
    grade_rows = grades[0]
    group_lists, cand_count = grade_rows.shape

    with jax.named_scope("gather"):
        vectors = jnp.where(
            first, jnp.stack([norm_gain, output_scale]), jnp.stack([final_gain, score_vector])
        )
        vectors = jnp.pad(vectors, ((0, 6), (0, head_size - rows)))
        mine = jnp.concatenate([jnp.where(first, value_codes, output_codes), vectors], axis=0)
        other = lax.ppermute(mine, Z, half_partner())
        low = jnp.where(z_half == 0, mine, other)
        high = jnp.where(z_half == 0, other, mine)
        block = jnp.concatenate([low[:rows], high[:rows], low[rows : rows + 2], high[rows : rows + 6]], axis=0)
        spread = jnp.broadcast_to(block, (32,) + block.shape)
        own = lax.all_to_all(spread, YX, 0, 0)
        beside = lax.ppermute(own, "c", SWAP)
        value_block = jnp.where(first, own, beside)
        out_block = jnp.where(first, beside, own)
        value_full = value_block[:, : 2 * rows].reshape(width, head_size)
        out_full = out_block[:, : 2 * rows].reshape(width, head_size)

        def vector(block, which):
            parts = block[:, 2 * rows : 2 * rows + 4, :rows].reshape(32, 2, 2, rows)
            return parts[:, :, which].reshape(width).astype(jnp.float32)

        gain32 = vector(value_block, 0)
        scale32 = vector(value_block, 1)
        weighted = vector(out_block, 0) * vector(out_block, 1)

    root_mean = jnp.sqrt(jnp.mean(tokens32 * tokens32, axis=-1, keepdims=True) + EPSILON)
    normed = (tokens32 / root_mean * gain32).astype(jnp.bfloat16)
    mixed = jnp.dot(normed, value_full, preferred_element_type=jnp.float32)
    value_half = (mixed * value_scale).astype(jnp.bfloat16)
    branch = lax.dot_general(
        value_half, out_full, (((1,), (1,)), ((), ())), preferred_element_type=jnp.float32
    )
    residual = (tokens32 + branch * scale32).astype(jnp.bfloat16)
    resid32 = residual.astype(jnp.float32)
    final_root = jnp.sqrt(jnp.mean(resid32 * resid32, axis=-1) + EPSILON)
    raw_score = jnp.sum(resid32 * weighted, axis=-1) / final_root
    capped = jnp.tanh(raw_score / SOFT_CAP)
    token_score = SOFT_CAP * capped
    member = (seg_local[:, None] == jnp.arange(cand_count, dtype=jnp.int32)).astype(jnp.float32)

    with jax.named_scope("stats"):
        local = jnp.stack(
            [jnp.sum(token_score[:, None] * member, axis=0), jnp.sum(member, axis=0)]
        )
        local = jnp.pad(local, ((0, 6), (0, 128 - cand_count)))
        pair = local + lax.ppermute(local, "zh", SWAP)

    slope = 1.0 - capped * capped
    unit_resid = slope[:, None] * (
        weighted[None, :] / final_root[:, None]
        - resid32 * (raw_score / (width * final_root * final_root))[:, None]
    )
    unit_branch = (unit_resid * scale32).astype(jnp.bfloat16)
    unit_values = jnp.dot(unit_branch, out_full, preferred_element_type=jnp.float32) * value_scale

    with jax.named_scope("stats2"):
        spread = jnp.broadcast_to(pair, (8,) + pair.shape)
        stats = jnp.sum(lax.all_to_all(spread, ("yl", "x"), 0, 0), axis=0)
        sums, counts = stats[0, :cand_count], stats[1, :cand_count]
        cand_score = sums / counts
        teacher = lax.dynamic_index_in_dim(grade_rows, lax.axis_index("yh"), 0, keepdims=False)
        teacher = teacher.astype(jnp.float32)
        log_teacher = teacher - jnp.log(jnp.sum(jnp.exp(teacher)))
        log_student = cand_score - jnp.log(jnp.sum(jnp.exp(cand_score)))
        own_loss = jnp.sum(jnp.exp(log_teacher) * (log_teacher - log_student))
        grad_cand = (jnp.exp(log_student) - jnp.exp(log_teacher)) / counts
        factor = jnp.sum(member * grad_cand, axis=-1, keepdims=True)

    half_scaled = (factor * value_half.astype(jnp.float32)).astype(jnp.bfloat16)
    grad_values = (factor * unit_values).astype(jnp.bfloat16)
    output_term = contract_rows(unit_branch, half_scaled)
    value_term = contract_rows(normed, grad_values)

    with jax.named_scope("reduce"):
        keep = jnp.where(first, value_term, output_term)
        give = jnp.where(first, output_term, value_term).astype(jnp.bfloat16)
        got = lax.ppermute(give, "c", SWAP)
        both = (keep + got.astype(jnp.float32)).astype(jnp.bfloat16)
        loss_hi = own_loss.astype(jnp.bfloat16)
        loss_mid = own_loss - loss_hi.astype(jnp.float32)
        loss_lo = loss_mid.astype(jnp.bfloat16)
        loss_row = jnp.pad(jnp.stack([loss_hi, loss_lo])[None, :], ((0, 7), (0, head_size - 2)))
        sent = jnp.concatenate(
            [both.reshape(32, 2 * rows, head_size), jnp.broadcast_to(loss_row, (32, 8, head_size))],
            axis=1,
        )
        came = lax.all_to_all(sent, YX, 0, 0)
        part = jnp.sum(came[:, : 2 * rows].astype(jnp.float32), axis=0)
        losses = came.reshape(4, 8, 2 * rows + 8, head_size)[:, 0, 2 * rows, :2]
        list_loss = jnp.sum(losses.astype(jnp.float32), axis=-1)
        part = jnp.broadcast_to(part.reshape(2, 1, rows, head_size), (2, 6, rows, head_size))
        part = part.reshape(12, rows, head_size)
        total = jnp.sum(lax.all_to_all(part, Z, 0, 0), axis=0)
        pair = lax.all_gather(total, "c")
    return (pair[0], pair[1], list_loss[None, :])


def solution(mesh):
    grid = Mesh(mesh.devices.reshape(4, 2, 4, 2, 6, 2), WIDE + NARROW)
    in_specs = (
        P(NARROW, WIDE, None),
        P(NARROW, WIDE),
        P(NARROW, None, None),
        P(WIDE, None),
        P(),
        P(WIDE, None),
        P(WIDE),
        P(WIDE),
        P(WIDE),
        P(WIDE),
    )
    out_specs = (P(WIDE, None), P(WIDE, None), P(NARROW, None))
    return jax.shard_map(shards, mesh=grid, in_specs=in_specs, out_specs=out_specs, check_vma=False)
```

time: 1620 us -> 195 us (0.12)
  waiting for transfers between devices: 855 us -> 27 us
  blocking collectives: 707 us -> 89.2 us
  starting transfers between devices: 0.16 us -> 41.8 us
    unnamed x5 -> x0, waiting for transfers between devices: 649 us -> none
    unnamed x1 -> x0, blocking collectives: 480 us -> none
    psum x1 -> x0, blocking collectives: 226 us -> none  [shards(): lax.psum((list_pick[:, None] * local_sums[None, :], list_pick[:, None] *...]
    psum x1 -> x0, waiting for transfers between devices: 206 us -> none  [shards(): total = lax.psum(shard, 'narrow')]
    all_to_all x0 -> x2, blocking collectives: none -> 85 us  [the longest x1 43.4 us: shards(): own = lax.all_to_all(spread, YX, 0, 0)]
    ppermute x0 -> x4, starting transfers between devices: none -> 32.1 us  [the longest x1 15.1 us: shards(): other = lax.ppermute(mine, Z, half_partner())]
    all_to_all x0 -> x2, waiting for transfers between devices: none -> 20.3 us  [the longest x1 20.2 us: shards(): total = jnp.sum(lax.all_to_all(part, Z, 0, 0), axis=0)]
  transfers between devices with their start and end apart: 4 -> 6, of which waited for: 2 -> 6; matrix products, arithmetic and copies ran while one was open for 1% -> 4% of each run, Pallas kernels for 0% -> 0%
where the time goes in v1:
time: 195 us
  blocking collectives  89.2 us (46%)
  starting transfers between devices  41.8 us (21%)
  waiting for transfers between devices  27 us (14%)
  matrix products  14.9 us (8%)
  other arithmetic  13.4 us (7%)
  local copies, waits for them, and re-layouts  4.96 us (3%)
  between operations  3.61 us (2%)
    all_to_all x1, blocking collectives, shards(): own = lax.all_to_all(spread, YX, 0, 0)  43.4 us
    all_to_all x1, blocking collectives, shards(): came = lax.all_to_all(sent, YX, 0, 0)  41.6 us
    all_to_all x1, waiting for transfers between devices, shards(): total = jnp.sum(lax.all_to_all(part, Z, 0, 0), axis=0)  20.2 us
    ppermute x1, starting transfers between devices, shards(): other = lax.ppermute(mine, Z, half_partner())  15.1 us
    dot_general x2, matrix products, contract_rows(): lax.dot_general(left, right, (((0,), (0,)), ((), ())), preferred_element_...  9.35 us
    ppermute x1, starting transfers between devices, shards(): pair = local + lax.ppermute(local, 'zh', SWAP)  6.91 us
    all_to_all x1, starting transfers between devices, shards(): total = jnp.sum(lax.all_to_all(part, Z, 0, 0), axis=0)  6.3 us
    ppermute x1, starting transfers between devices, shards(): beside = lax.ppermute(own, 'c', SWAP)  5.56 us
  transfers between devices with their start and end apart: 6, of which 6 were waited for; matrix products, arithmetic and copies ran while one was open for 4% of the time, Pallas kernels for 0%

profile of v1, /device:TPU:1, one launch (start us, length us, event | category | flops | bytes accessed | tf_op | source)
XLA Modules:
  0.0 194.8 jit_solution(9941775513647773724)
XLA Ops:
  0.6 0.0 copy-start
  0.6 0.9 broadcast_select_fusion.4
  1.5 0.7 broadcast_select_fusion.5
  2.3 15.1 %collective-permute-start = (bf16[88,128]{1,0:T(8,128)(2,1)S(1)}, bf16[88,128]{1,0:T(8,128)(2,1)S(1)}, u32[]{:S(2)}, u32[]{:S(2)}) collective-permute-start(bf16[88,128]{1,0:T(8,128)(2,1)S(1)} %fusion.36), channel_id=1, source_target_pairs={{0,18},{2,20},{4,22},{6,12},{8,14},{10,16},{12,6},{14,8},{16,10},{... | collective-permute-start | bytes 67592 | tf_op jit(solution)/shard_map/gather/ppermute | solution.py:57
  17.4 1.2 collective-permute-done
  18.7 0.2 broadcast_in_dim.14
  18.9 43.4 %all_to_all.20 = bf16[32,168,128]{2,1,0:T(8,128)(2,1)S(1)} all-to-all(bf16[32,168,128]{2,1,0:T(8,128)(2,1)S(1)} %broadcast_in_dim.14), channel_id=1, replica_groups=mesh['yh'=4,'yl'=2,'x'=4,'zh'=2,'zl'=6,'c'=2] {'yh','yl','x'}, dimensions={0} | all-to-all | bytes 2752512 | tf_op jit(solution)/shard_map/gather/all_to_all | solution.py:62
  62.3 5.6 %collective-permute-start.1 = (bf16[32,168,128]{2,1,0:T(8,128)(2,1)S(1)}, bf16[32,168,128]{2,1,0:T(8,128)(2,1)S(1)}, u32[]{:S(2)}, u32[]{:S(2)}) collective-permute-start(bf16[32,168,128]{2,1,0:T(8,128)(2,1)S(1)} %all_to_all.20), channel_id=1, source_target_pairs={{0,1},{1,0},{2,3},{3,2},{4,5},{5,4},{6,7},{7,6},{8,9},{9,8},{10,11... | collective-permute-start | bytes 4128776 | tf_op jit(solution)/shard_map/gather/ppermute | solution.py:63
  67.9 0.0 copy-done
  67.9 0.6 fusion.6
  68.5 2.1 %collective-permute-done.1 = bf16[32,168,128]{2,1,0:T(8,128)(2,1)S(1)} collective-permute-done((bf16[32,168,128]{2,1,0:T(8,128)(2,1)S(1)}, bf16[32,168,128]{2,1,0:T(8,128)(2,1)S(1)}, u32[]{:S(2)}, u32[]{:S(2)}) %collective-permute-start.1) | collective-permute-done | bytes 1376288 | tf_op jit(solution)/shard_map/gather/ppermute | solution.py:63
  70.6 0.2 broadcast_select_fusion
  70.8 0.0 copy-start.4
  70.8 1.1 slice.82
  72.0 1.2 slice.83
  73.2 0.3 fusion.34
  73.5 0.1 reshape.153
  73.6 0.1 mul.154
  73.7 0.1 reshape.154
  73.8 0.0 copy-done.4
  73.8 0.0 copy-start.1
  73.8 2.4 %fusion.23 = bf16[256,128]{1,0:T(8,128)(2,1)S(1)} fusion(bf16[5120,128]{1,0:T(8,128)(2,1)} %bitcast.73, bf16[1,256,5120]{2,1,0:T(8,128)(2,1)S(1)} %copy-done, f32[5120]{0:T(1024)S(1)} %reshape.153, f32[256]{0:T(256)S(1)} %add_sqrt_fusion, f32[128]{0:T(128)S(1)} %copy-done.4), kind=kOutput, calls=%fused_computation.33 | convolution fusion | flops 340852736 | bytes 4019712 | tf_op jit(solution)/shard_map/dot_general | solution.py:79
  76.2 0.0 copy-done.1
  76.3 0.0 copy-start.2
  76.3 0.0 copy-start.3
  76.3 3.1 %fusion.12 = (f32[256]{0:T(256)S(1)}, f32[256]{0:T(256)S(1)}, bf16[256,5120]{1,0:T(8,128)(2,1)}) fusion(f32[5120]{0:T(1024)S(1)} %mul.154, f32[5120]{0:T(1024)S(1)} %reshape.154, bf16[256,128]{1,0:T(8,128)(2,1)S(1)} %fusion.23, bf16[5120,128]{1,0:T(8,128)(2,1)S(1)} %bitcast.72, bf16[1,256,5120]{2,1,0:T(8,128)(2,1)S(1)} %copy-done), kind=kOutput, calls=%fused_computation.19 | convolution fusion | flops 347340288 | bytes 6662144 | tf_op jit(solution)/shard_map/dot_general | solution.py:81
  79.5 0.0 copy-done.2
  79.5 0.1 select_reduce_fusion.1
  79.6 6.9 %collective-permute-start.2 = (f32[8,128]{1,0:T(8,128)S(1)}, f32[8,128]{1,0:T(8,128)S(1)}, u32[]{:S(2)}, u32[]{:S(2)}) collective-permute-start(f32[8,128]{1,0:T(8,128)S(1)} %select_maximum_fusion), channel_id=1, source_target_pairs={{0,12},{12,0},{1,13},{13,1},{2,14},{14,2},{3,15},{15,3},{4,16},{16... | collective-permute-start | bytes 12296 | tf_op jit(solution)/shard_map/stats/ppermute | solution.py:97
  86.5 0.0 copy-done.3
  86.5 0.6 exponential_reduce_fusion
  87.8 2.4 %collective-permute-done.2 = f32[8,128]{1,0:T(8,128)S(1)} collective-permute-done((f32[8,128]{1,0:T(8,128)S(1)}, f32[8,128]{1,0:T(8,128)S(1)}, u32[]{:S(2)}, u32[]{:S(2)}) %collective-permute-start.2) | collective-permute-done | bytes 4128 | tf_op jit(solution)/shard_map/stats/ppermute | solution.py:97
  90.3 0.6 broadcast_in_dim.15
  90.9 3.3 %all-to-all-start.1 = ((f32[8,8,128]{2,1,0:T(8,128)}), f32[8,8,128]{2,1,0:T(8,128)S(1)}, u32[]{:S(2)}, u32[]{:S(2)}) async-start(f32[8,8,128]{2,1,0:T(8,128)} %broadcast_in_dim.15), calls=%async_computation.1 | async-start | bytes 65536 | tf_op jit(solution)/shard_map/stats2/all_to_all | solution.py:109
  94.2 5.0 %fusion.13 = bf16[256,5120]{1,0:T(8,128)(2,1)} fusion(bf16[256,5120]{1,0:T(8,128)(2,1)} %get-tuple-element.21, f32[256]{0:T(256)S(1)} %get-tuple-element.19, f32[256]{0:T(256)S(1)} %get-tuple-element.20, f32[256]{0:T(256)S(1)} %get-tuple-element.9, f32[5120]{0:T(1024)S(1)} %mul.154, f32[5120]{0:T(1024)S(1)} %reshape.154), kind=kLoop, calls=%fused_computation.20 | loop fusion | flops 9175040 | bytes 5286912 | tf_op jit(solution)/shard_map/convert_element_type | solution.py:104
  99.2 0.1 all-to-all-done.1
  99.3 0.6 exponential_reduce_fusion.1
  100.6 0.1 select_reduce_fusion
  100.7 4.7 %fusion.15 = f32[5120,128]{1,0:T(8,128)S(1)} fusion(bf16[1,256,5120]{2,1,0:T(8,128)(2,1)} %param.10, f32[5120]{0:T(1024)S(1)} %reshape.153, f32[256]{0:T(256)S(1)} %add_sqrt_fusion, bf16[256,5120]{1,0:T(8,128)(2,1)} %fusion.13, bf16[5120,128]{1,0:T(8,128)(2,1)} %bitcast.71, f32[256]{0:T(256)S(1)} %select_reduce_fusion, f32[128]{0:T(128)S(1)} %copy-done.4), kind=kOutput, calls=%fused_computation.25 | convolution fusion | flops 676429824 | bytes 9198080 | tf_op jit(solution)/shard_map/dot_general | solution.py:24
  105.4 4.6 %select_convert_fusion = (bf16[5120,128]{1,0:T(8,128)(2,1)}, f32[5120,128]{1,0:T(8,128)}) fusion(f32[5120,128]{1,0:T(8,128)S(1)} %fusion.15, pred[]{:T(512)S(6)} %eq.22, bf16[256,5120]{1,0:T(8,128)(2,1)} %fusion.13, bf16[256,128]{1,0:T(8,128)(2,1)S(1)} %fusion.23, f32[256]{0:T(256)S(1)} %select_reduce_fusion), kind=kOutput, calls=%fused_computation.24 | convolution fusion | flops 336297984 | bytes 9241601 | tf_op jit(solution)/shard_map/dot_general | solution.py:24
  110.1 4.6 %collective-permute-start.3 = (bf16[5120,128]{1,0:T(8,128)(2,1)}, bf16[5120,128]{1,0:T(8,128)(2,1)}, u32[]{:S(2)}, u32[]{:S(2)}) collective-permute-start(bf16[5120,128]{1,0:T(8,128)(2,1)} %get-tuple-element.22), channel_id=1, source_target_pairs={{0,1},{1,0},{2,3},{3,2},{4,5},{5,4},{6,7},{7,6},{8,9},{9,8},{10,11... | collective-permute-start | bytes 3932168 | tf_op jit(solution)/shard_map/reduce/ppermute | solution.py:128
  114.7 0.6 fusion.41
  116.6 0.1 maximum_bitcast_fusion
  116.7 1.0 collective-permute-done.3
  117.6 2.5 %add_convert_fusion = bf16[5120,128]{1,0:T(8,128)(2,1)S(1)} fusion(bf16[5120,128]{1,0:T(8,128)(2,1)} %collective-permute-done.3, f32[5120,128]{1,0:T(8,128)S(1)} %fusion.15, f32[5120,128]{1,0:T(8,128)} %get-tuple-element.23, pred[]{:T(512)S(6)} %eq.22), kind=kLoop, calls=%fused_computation.23 | loop fusion | flops 2621440 | bytes 7864321 | tf_op jit(solution)/shard_map/reduce/convert_element_type | solution.py:129
  120.1 0.1 pad_maximum_fusion
  120.2 41.6 %all_to_all.21 = bf16[32,168,128]{2,1,0:T(8,128)(2,1)S(1)} all-to-all(bf16[32,168,128]{2,1,0:T(8,128)(2,1)S(1)} %pad_maximum_fusion), channel_id=1, replica_groups=mesh['yh'=4,'yl'=2,'x'=4,'zh'=2,'zl'=6,'c'=2] {'yh','yl','x'}, dimensions={0} | all-to-all | bytes 2752512 | tf_op jit(solution)/shard_map/reduce/all_to_all | solution.py:138
  161.8 0.2 convert_reduce_fusion
  162.0 0.8 broadcast_in_dim.19
  162.8 6.3 %all-to-all-start.3 = ((f32[12,80,128]{2,1,0:T(8,128)}), f32[12,80,128]{2,1,0:T(8,128)S(1)}, u32[]{:S(2)}, u32[]{:S(2)}) async-start(f32[12,80,128]{2,1,0:T(8,128)} %bitcast.22), calls=%async_computation.3 | async-start | bytes 983040 | tf_op jit(solution)/shard_map/reduce/all_to_all | solution.py:144
  169.1 0.6 fusion.37
  169.7 20.2 %all-to-all-done.3 = f32[12,80,128]{2,1,0:T(8,128)S(1)} async-done(((f32[12,80,128]{2,1,0:T(8,128)}), f32[12,80,128]{2,1,0:T(8,128)S(1)}, u32[]{:S(2)}, u32[]{:S(2)}) %all-to-all-start.3) | async-done | bytes 491552 | tf_op jit(solution)/shard_map/reduce/all_to_all | solution.py:144
  189.9 4.2 %all-gather = f32[160,128]{1,0:T(8,128)S(1)} all-gather(f32[80,128]{1,0:T(8,128)S(1)} %reduce_sum.128), channel_id=2, replica_groups=mesh['yh'=4,'yl'=2,'x'=4,'zh'=2,'zl'=6,'c'=2] {'c'}, dimensions={0}, use_global_device_ids=true | all-gather | bytes 122880 | tf_op jit(solution)/shard_map/reduce/all_gather | solution.py:145
  194.2 0.6 fusion.45
  (19 shorter events, 0.2 us)
Async XLA Ops:
  0.6 67.2 %copy-start = (bf16[1,256,5120]{2,1,0:T(8,128)(2,1)S(1)}, bf16[1,256,5120]{2,1,0:T(8,128)(2,1)}, u32[]{:S(2)}) copy-start(bf16[1,256,5120]{2,1,0:T(8,128)(2,1)} %param.10) | copy-start | bytes 7864324
  2.3 16.3 %collective-permute-start = (bf16[88,128]{1,0:T(8,128)(2,1)S(1)}, bf16[88,128]{1,0:T(8,128)(2,1)S(1)}, u32[]{:S(2)}, u32[]{:S(2)}) collective-permute-start(bf16[88,128]{1,0:T(8,128)(2,1)S(1)} %fusion.36), channel_id=1, source_target_pairs={{0,18},{2,20},{4,22},{6,12},{8,14},{10,16},{12,6},{14,8},{16,10},{... | collective-permute-start | bytes 67592 | tf_op jit(solution)/shard_map/gather/ppermute | solution.py:57
  62.3 8.3 %collective-permute-start.1 = (bf16[32,168,128]{2,1,0:T(8,128)(2,1)S(1)}, bf16[32,168,128]{2,1,0:T(8,128)(2,1)S(1)}, u32[]{:S(2)}, u32[]{:S(2)}) collective-permute-start(bf16[32,168,128]{2,1,0:T(8,128)(2,1)S(1)} %all_to_all.20), channel_id=1, source_target_pairs={{0,1},{1,0},{2,3},{3,2},{4,5},{5,4},{6,7},{7,6},{8,9},{9,8},{10,11... | collective-permute-start | bytes 4128776 | tf_op jit(solution)/shard_map/gather/ppermute | solution.py:63
  70.8 3.0 %copy-start.4 = (f32[128]{0:T(128)S(1)}, f32[128]{0:T(128)}, u32[]{:S(2)}) copy-start(f32[128]{0:T(128)} %param.14) | copy-start | bytes 1540
  73.8 2.4 %copy-start.1 = (bf16[32,160,128]{2,1,0:T(8,128)(2,1)S(1)}, bf16[32,160,128]{2,1,0:T(8,128)(2,1)}, u32[]{:S(2)}) copy-start(bf16[32,160,128]{2,1,0:T(8,128)(2,1)} %slice.83) | copy-start | bytes 3932164
  76.3 3.2 %copy-start.2 = (s32[1,256]{1,0:T(1,128)S(1)}, s32[1,256]{1,0:T(1,128)}, u32[]{:S(2)}) copy-start(s32[1,256]{1,0:T(1,128)} %param.11) | copy-start | bytes 3076
  76.3 10.2 %copy-start.3 = (s32[1,4,20]{2,1,0:T(4,128)S(1)}, s32[1,4,20]{2,1,0:T(4,128)}, u32[]{:S(2)}) copy-start(s32[1,4,20]{2,1,0:T(4,128)} %param.12) | copy-start | bytes 964
  79.6 10.7 %collective-permute-start.2 = (f32[8,128]{1,0:T(8,128)S(1)}, f32[8,128]{1,0:T(8,128)S(1)}, u32[]{:S(2)}, u32[]{:S(2)}) collective-permute-start(f32[8,128]{1,0:T(8,128)S(1)} %select_maximum_fusion), channel_id=1, source_target_pairs={{0,12},{12,0},{1,13},{13,1},{2,14},{14,2},{3,15},{15,3},{4,16},{16... | collective-permute-start | bytes 12296 | tf_op jit(solution)/shard_map/stats/ppermute | solution.py:97
  90.9 8.4 %all-to-all-start.1 = ((f32[8,8,128]{2,1,0:T(8,128)}), f32[8,8,128]{2,1,0:T(8,128)S(1)}, u32[]{:S(2)}, u32[]{:S(2)}) async-start(f32[8,8,128]{2,1,0:T(8,128)} %broadcast_in_dim.15), calls=%async_computation.1 | async-start | bytes 65536 | tf_op jit(solution)/shard_map/stats2/all_to_all | solution.py:109
  110.1 7.6 %collective-permute-start.3 = (bf16[5120,128]{1,0:T(8,128)(2,1)}, bf16[5120,128]{1,0:T(8,128)(2,1)}, u32[]{:S(2)}, u32[]{:S(2)}) collective-permute-start(bf16[5120,128]{1,0:T(8,128)(2,1)} %get-tuple-element.22), channel_id=1, source_target_pairs={{0,1},{1,0},{2,3},{3,2},{4,5},{5,4},{6,7},{7,6},{8,9},{9,8},{10,11... | collective-permute-start | bytes 3932168 | tf_op jit(solution)/shard_map/reduce/ppermute | solution.py:128
  162.8 27.1 %all-to-all-start.3 = ((f32[12,80,128]{2,1,0:T(8,128)}), f32[12,80,128]{2,1,0:T(8,128)S(1)}, u32[]{:S(2)}, u32[]{:S(2)}) async-start(f32[12,80,128]{2,1,0:T(8,128)} %bitcast.22), calls=%async_computation.3 | async-start | bytes 983040 | tf_op jit(solution)/shard_map/reduce/all_to_all | solution.py:144

commit v2 on v1

--- a/solution.py
+++ b/solution.py
@@ -94,7 +94,8 @@
             [jnp.sum(token_score[:, None] * member, axis=0), jnp.sum(member, axis=0)]
         )
         local = jnp.pad(local, ((0, 6), (0, 128 - cand_count)))
-        pair = local + lax.ppermute(local, "zh", SWAP)
+        spread = jnp.broadcast_to(local, (16,) + local.shape)
+        arrived = lax.all_to_all(spread, ("yl", "x", "zh"), 0, 0)
 
     slope = 1.0 - capped * capped
     unit_resid = slope[:, None] * (
@@ -105,8 +106,7 @@
     unit_values = jnp.dot(unit_branch, out_full, preferred_element_type=jnp.float32) * value_scale
 
     with jax.named_scope("stats2"):
-        spread = jnp.broadcast_to(pair, (8,) + pair.shape)
-        stats = jnp.sum(lax.all_to_all(spread, ("yl", "x"), 0, 0), axis=0)
+        stats = jnp.sum(arrived, axis=0)
         sums, counts = stats[0, :cand_count], stats[1, :cand_count]
         cand_score = sums / counts
         teacher = lax.dynamic_index_in_dim(grade_rows, lax.axis_index("yh"), 0, keepdims=False)
@@ -139,9 +139,9 @@
         part = jnp.sum(came[:, : 2 * rows].astype(jnp.float32), axis=0)
         losses = came.reshape(4, 8, 2 * rows + 8, head_size)[:, 0, 2 * rows, :2]
         list_loss = jnp.sum(losses.astype(jnp.float32), axis=-1)
-        part = jnp.broadcast_to(part.reshape(2, 1, rows, head_size), (2, 6, rows, head_size))
-        part = part.reshape(12, rows, head_size)
-        total = jnp.sum(lax.all_to_all(part, Z, 0, 0), axis=0)
+        part = part.astype(jnp.bfloat16).reshape(2, 1, rows, head_size)
+        part = jnp.broadcast_to(part, (2, 6, rows, head_size)).reshape(12, rows, head_size)
+        total = jnp.sum(lax.all_to_all(part, Z, 0, 0).astype(jnp.float32), axis=0)
         pair = lax.all_gather(total, "c")
     return (pair[0], pair[1], list_loss[None, :])
 

time: 195 us -> 188 us (0.964)
  waiting for transfers between devices: 27 us -> 23.4 us
  starting transfers between devices: 41.8 us -> 38.3 us
  blocking collectives: 89.2 us -> 87.1 us
    ppermute x1 -> x0, starting transfers between devices: 6.91 us -> none  [shards(): pair = local + lax.ppermute(local, 'zh', SWAP)]
    all_to_all x2, starting transfers between devices: 9.64 us -> 14.4 us  [the longest x1 7.58 us: shards(): arrived = lax.all_to_all(spread, ('yl', 'x', 'zh'), 0, 0)]
    ppermute x1 -> x0, waiting for transfers between devices: 2.43 us -> none  [shards(): pair = local + lax.ppermute(local, 'zh', SWAP)]
    ppermute x1, waiting for transfers between devices: 2.11 us -> 0.01 us  [shards(): beside = lax.ppermute(own, 'c', SWAP)]
  transfers between devices with their start and end apart: 6 -> 5, of which waited for: 6 -> 4; matrix products, arithmetic and copies ran while one was open for 4% -> 5% of each run, Pallas kernels for 0% -> 0%
where the time goes in v2:
time: 188 us; the launch traced here: 187 us
  blocking collectives  87.1 us (46%)
  starting transfers between devices  38.3 us (20%)
  waiting for transfers between devices  23.4 us (12%)
  other arithmetic  15 us (8%)
  matrix products  14.9 us (8%)
  local copies, waits for them, and re-layouts  4.87 us (3%)
  between operations  3.61 us (2%)
    all_to_all x1, blocking collectives, shards(): own = lax.all_to_all(spread, YX, 0, 0)  43.4 us
    all_to_all x1, blocking collectives, shards(): came = lax.all_to_all(sent, YX, 0, 0)  40.3 us
    ppermute x1, starting transfers between devices, shards(): other = lax.ppermute(mine, Z, half_partner())  15.1 us
    all_to_all x1, waiting for transfers between devices, shards(): total = jnp.sum(lax.all_to_all(part, Z, 0, 0).astype(jnp.float32), axis=0)  13.8 us
    dot_general x2, matrix products, contract_rows(): lax.dot_general(left, right, (((0,), (0,)), ((), ())), preferred_element_...  9.36 us
    all_to_all x1, starting transfers between devices, shards(): arrived = lax.all_to_all(spread, ('yl', 'x', 'zh'), 0, 0)  7.58 us
    all_to_all x1, waiting for transfers between devices, shards(): arrived = lax.all_to_all(spread, ('yl', 'x', 'zh'), 0, 0)  7.37 us
    all_to_all x1, starting transfers between devices, shards(): total = jnp.sum(lax.all_to_all(part, Z, 0, 0).astype(jnp.float32), axis=0)  6.78 us
  transfers between devices with their start and end apart: 5, of which 4 were waited for; matrix products, arithmetic and copies ran while one was open for 5% of the time, Pallas kernels for 0%

profile of v2, /device:TPU:1, one launch (start us, length us, event | category | flops | bytes accessed | tf_op | source)
XLA Modules:
  0.0 187.2 jit_solution(13504979007180398628)
XLA Ops:
  0.6 0.0 copy-start.3
  0.6 0.7 broadcast_select_fusion.4
  1.4 0.7 broadcast_select_fusion.5
  2.1 15.1 %collective-permute-start = (bf16[88,128]{1,0:T(8,128)(2,1)S(1)}, bf16[88,128]{1,0:T(8,128)(2,1)S(1)}, u32[]{:S(2)}, u32[]{:S(2)}) collective-permute-start(bf16[88,128]{1,0:T(8,128)(2,1)S(1)} %fusion.36), channel_id=1, source_target_pairs={{0,18},{2,20},{4,22},{6,12},{8,14},{10,16},{12,6},{14,8},{16,10},{... | collective-permute-start | bytes 67592 | tf_op jit(solution)/shard_map/gather/ppermute | solution.py:57
  17.3 1.2 collective-permute-done
  18.5 0.2 broadcast_in_dim.14
  18.7 43.4 %all_to_all.20 = bf16[32,168,128]{2,1,0:T(8,128)(2,1)S(1)} all-to-all(bf16[32,168,128]{2,1,0:T(8,128)(2,1)S(1)} %broadcast_in_dim.14), channel_id=1, replica_groups=mesh['yh'=4,'yl'=2,'x'=4,'zh'=2,'zl'=6,'c'=2] {'yh','yl','x'}, dimensions={0} | all-to-all | bytes 2752512 | tf_op jit(solution)/shard_map/gather/all_to_all | solution.py:62
  62.1 5.6 %collective-permute-start.1 = (bf16[32,168,128]{2,1,0:T(8,128)(2,1)S(1)}, bf16[32,168,128]{2,1,0:T(8,128)(2,1)S(1)}, u32[]{:S(2)}, u32[]{:S(2)}) collective-permute-start(bf16[32,168,128]{2,1,0:T(8,128)(2,1)S(1)} %all_to_all.20), channel_id=1, source_target_pairs={{0,1},{1,0},{2,3},{3,2},{4,5},{5,4},{6,7},{7,6},{8,9},{9,8},{10,11... | collective-permute-start | bytes 4128776 | tf_op jit(solution)/shard_map/gather/ppermute | solution.py:63
  67.7 0.0 copy-done.3
  67.7 0.6 exponential_reduce_fusion
  69.0 2.3 %fusion.6 = f32[256]{0:T(256)S(1)} fusion(bf16[1,256,5120]{2,1,0:T(8,128)(2,1)} %param.10), kind=kLoop, calls=%fused_computation.13 | loop fusion | flops 3931904 | bytes 2622464 | tf_op jit(solution)/shard_map/reduce_sum | solution.py:77
  71.4 0.0 collective-permute-done.1
  71.4 0.2 broadcast_select_fusion
  71.6 0.0 copy-start
  71.6 0.0 copy-start.4
  71.6 1.1 slice.82
  72.8 1.2 slice.83
  74.0 0.3 fusion.34
  74.3 0.1 reshape.153
  74.4 0.1 mul.154
  74.5 0.1 reshape.154
  74.6 0.0 copy-done
  74.6 0.0 copy-done.4
  74.6 0.0 copy-start.1
  74.7 2.4 %fusion.23 = bf16[256,128]{1,0:T(8,128)(2,1)S(1)} fusion(bf16[5120,128]{1,0:T(8,128)(2,1)} %bitcast.73, bf16[1,256,5120]{2,1,0:T(8,128)(2,1)S(1)} %copy-done, f32[5120]{0:T(1024)S(1)} %reshape.153, f32[256]{0:T(256)S(1)} %add_sqrt_fusion, f32[128]{0:T(128)S(1)} %copy-done.4), kind=kOutput, calls=%fused_computation.33 | convolution fusion | flops 340852736 | bytes 4019712 | tf_op jit(solution)/shard_map/dot_general | solution.py:79
  77.1 0.0 copy-done.1
  77.1 0.0 copy-start.2
  77.1 3.2 %fusion.12 = (f32[256]{0:T(256)S(1)}, f32[256]{0:T(256)S(1)}, bf16[256,5120]{1,0:T(8,128)(2,1)}) fusion(f32[5120]{0:T(1024)S(1)} %mul.154, f32[5120]{0:T(1024)S(1)} %reshape.154, bf16[256,128]{1,0:T(8,128)(2,1)S(1)} %fusion.23, bf16[5120,128]{1,0:T(8,128)(2,1)S(1)} %bitcast.72, bf16[1,256,5120]{2,1,0:T(8,128)(2,1)S(1)} %copy-done), kind=kOutput, calls=%fused_computation.19 | convolution fusion | flops 347340288 | bytes 6662144 | tf_op jit(solution)/shard_map/dot_general | solution.py:81
  80.3 0.0 copy-done.2
  80.3 0.1 select_reduce_fusion.1
  80.4 0.6 broadcast_in_dim.15
  81.0 7.6 %all-to-all-start.1 = ((f32[16,8,128]{2,1,0:T(8,128)}), f32[16,8,128]{2,1,0:T(8,128)S(1)}, u32[]{:S(2)}, u32[]{:S(2)}) async-start(f32[16,8,128]{2,1,0:T(8,128)} %broadcast_in_dim.15), calls=%async_computation.1 | async-start | bytes 131072 | tf_op jit(solution)/shard_map/stats/all_to_all | solution.py:98
  88.6 5.0 %fusion.13 = bf16[256,5120]{1,0:T(8,128)(2,1)} fusion(bf16[256,5120]{1,0:T(8,128)(2,1)} %get-tuple-element.21, f32[256]{0:T(256)S(1)} %get-tuple-element.19, f32[256]{0:T(256)S(1)} %get-tuple-element.20, f32[256]{0:T(256)S(1)} %get-tuple-element.9, f32[5120]{0:T(1024)S(1)} %mul.154, f32[5120]{0:T(1024)S(1)} %reshape.154), kind=kLoop, calls=%fused_computation.20 | loop fusion | flops 9175040 | bytes 5286912 | tf_op jit(solution)/shard_map/convert_element_type | solution.py:105
  93.6 7.4 %all-to-all-done.1 = f32[16,8,128]{2,1,0:T(8,128)S(1)} async-done(((f32[16,8,128]{2,1,0:T(8,128)}), f32[16,8,128]{2,1,0:T(8,128)S(1)}, u32[]{:S(2)}, u32[]{:S(2)}) %all-to-all-start.1) | async-done | bytes 65568 | tf_op jit(solution)/shard_map/stats/all_to_all | solution.py:98
  101.0 0.6 exponential_reduce_fusion.1
  102.3 0.1 select_reduce_fusion
  102.4 4.7 %fusion.15 = f32[5120,128]{1,0:T(8,128)S(1)} fusion(bf16[1,256,5120]{2,1,0:T(8,128)(2,1)} %param.10, f32[5120]{0:T(1024)S(1)} %reshape.153, f32[256]{0:T(256)S(1)} %add_sqrt_fusion, bf16[256,5120]{1,0:T(8,128)(2,1)} %fusion.13, bf16[5120,128]{1,0:T(8,128)(2,1)} %bitcast.71, f32[256]{0:T(256)S(1)} %select_reduce_fusion, f32[128]{0:T(128)S(1)} %copy-done.4), kind=kOutput, calls=%fused_computation.24 | convolution fusion | flops 676429824 | bytes 9198080 | tf_op jit(solution)/shard_map/dot_general | solution.py:24
  107.1 4.6 %select_convert_fusion = (bf16[5120,128]{1,0:T(8,128)(2,1)}, f32[5120,128]{1,0:T(8,128)}) fusion(f32[5120,128]{1,0:T(8,128)S(1)} %fusion.15, pred[]{:T(512)S(6)} %eq.22, bf16[256,5120]{1,0:T(8,128)(2,1)} %fusion.13, bf16[256,128]{1,0:T(8,128)(2,1)S(1)} %fusion.23, f32[256]{0:T(256)S(1)} %select_reduce_fusion), kind=kOutput, calls=%fused_computation.23 | convolution fusion | flops 336297984 | bytes 9241601 | tf_op jit(solution)/shard_map/dot_general | solution.py:24
  111.8 3.3 %collective-permute-start.2 = (bf16[5120,128]{1,0:T(8,128)(2,1)}, bf16[5120,128]{1,0:T(8,128)(2,1)}, u32[]{:S(2)}, u32[]{:S(2)}) collective-permute-start(bf16[5120,128]{1,0:T(8,128)(2,1)} %get-tuple-element.22), channel_id=1, source_target_pairs={{0,1},{1,0},{2,3},{3,2},{4,5},{5,4},{6,7},{7,6},{8,9},{9,8},{10,11... | collective-permute-start | bytes 3932168 | tf_op jit(solution)/shard_map/reduce/ppermute | solution.py:128
  115.0 0.6 fusion.41
  117.0 0.1 maximum_bitcast_fusion
  117.0 1.0 collective-permute-done.2
  118.0 2.5 %add_convert_fusion = bf16[5120,128]{1,0:T(8,128)(2,1)S(1)} fusion(bf16[5120,128]{1,0:T(8,128)(2,1)} %collective-permute-done.2, f32[5120,128]{1,0:T(8,128)S(1)} %fusion.15, f32[5120,128]{1,0:T(8,128)} %get-tuple-element.23, pred[]{:T(512)S(6)} %eq.22), kind=kLoop, calls=%fused_computation.22 | loop fusion | flops 2621440 | bytes 7864321 | tf_op jit(solution)/shard_map/reduce/convert_element_type | solution.py:129
  120.5 0.1 pad_maximum_fusion
  120.6 40.3 %all_to_all.21 = bf16[32,168,128]{2,1,0:T(8,128)(2,1)S(1)} all-to-all(bf16[32,168,128]{2,1,0:T(8,128)(2,1)S(1)} %pad_maximum_fusion), channel_id=1, replica_groups=mesh['yh'=4,'yl'=2,'x'=4,'zh'=2,'zl'=6,'c'=2] {'yh','yl','x'}, dimensions={0} | all-to-all | bytes 2752512 | tf_op jit(solution)/shard_map/reduce/all_to_all | solution.py:138
  161.0 0.2 slice_reduce_fusion
  161.1 0.7 broadcast_in_dim.19
  161.9 6.8 %all-to-all-start.3 = ((bf16[12,80,128]{2,1,0:T(8,128)(2,1)}), bf16[12,80,128]{2,1,0:T(8,128)(2,1)S(1)}, u32[]{:S(2)}, u32[]{:S(2)}) async-start(bf16[12,80,128]{2,1,0:T(8,128)(2,1)} %bitcast.22), calls=%async_computation.3 | async-start | bytes 491520 | tf_op jit(solution)/shard_map/reduce/all_to_all | solution.py:144
  168.7 0.6 fusion.37
  169.3 13.8 %all-to-all-done.3 = bf16[12,80,128]{2,1,0:T(8,128)(2,1)S(1)} async-done(((bf16[12,80,128]{2,1,0:T(8,128)(2,1)}), bf16[12,80,128]{2,1,0:T(8,128)(2,1)S(1)}, u32[]{:S(2)}, u32[]{:S(2)}) %all-to-all-start.3) | async-done | bytes 245792 | tf_op jit(solution)/shard_map/reduce/all_to_all | solution.py:144
  183.1 3.4 %all-gather = f32[160,128]{1,0:T(8,128)S(1)} all-gather(f32[80,128]{1,0:T(8,128)S(1)} %convert_reduce_fusion), channel_id=2, replica_groups=mesh['yh'=4,'yl'=2,'x'=4,'zh'=2,'zl'=6,'c'=2] {'c'}, dimensions={0}, use_global_device_ids=true | all-gather | bytes 122880 | tf_op jit(solution)/shard_map/reduce/all_gather | solution.py:145
  186.5 0.6 fusion.44
  (18 shorter events, 0.2 us)
Async XLA Ops:
  0.6 67.1 %copy-start.3 = (s32[1,4,20]{2,1,0:T(4,128)S(1)}, s32[1,4,20]{2,1,0:T(4,128)}, u32[]{:S(2)}) copy-start(s32[1,4,20]{2,1,0:T(4,128)} %param.12) | copy-start | bytes 964
  2.1 16.3 %collective-permute-start = (bf16[88,128]{1,0:T(8,128)(2,1)S(1)}, bf16[88,128]{1,0:T(8,128)(2,1)S(1)}, u32[]{:S(2)}, u32[]{:S(2)}) collective-permute-start(bf16[88,128]{1,0:T(8,128)(2,1)S(1)} %fusion.36), channel_id=1, source_target_pairs={{0,18},{2,20},{4,22},{6,12},{8,14},{10,16},{12,6},{14,8},{16,10},{... | collective-permute-start | bytes 67592 | tf_op jit(solution)/shard_map/gather/ppermute | solution.py:57
  62.1 9.2 %collective-permute-start.1 = (bf16[32,168,128]{2,1,0:T(8,128)(2,1)S(1)}, bf16[32,168,128]{2,1,0:T(8,128)(2,1)S(1)}, u32[]{:S(2)}, u32[]{:S(2)}) collective-permute-start(bf16[32,168,128]{2,1,0:T(8,128)(2,1)S(1)} %all_to_all.20), channel_id=1, source_target_pairs={{0,1},{1,0},{2,3},{3,2},{4,5},{5,4},{6,7},{7,6},{8,9},{9,8},{10,11... | collective-permute-start | bytes 4128776 | tf_op jit(solution)/shard_map/gather/ppermute | solution.py:63
  71.6 3.1 %copy-start = (bf16[1,256,5120]{2,1,0:T(8,128)(2,1)S(1)}, bf16[1,256,5120]{2,1,0:T(8,128)(2,1)}, u32[]{:S(2)}) copy-start(bf16[1,256,5120]{2,1,0:T(8,128)(2,1)} %param.10) | copy-start | bytes 7864324
  71.6 3.1 %copy-start.4 = (f32[128]{0:T(128)S(1)}, f32[128]{0:T(128)}, u32[]{:S(2)}) copy-start(f32[128]{0:T(128)} %param.14) | copy-start | bytes 1540
  74.6 2.4 %copy-start.1 = (bf16[32,160,128]{2,1,0:T(8,128)(2,1)S(1)}, bf16[32,160,128]{2,1,0:T(8,128)(2,1)}, u32[]{:S(2)}) copy-start(bf16[32,160,128]{2,1,0:T(8,128)(2,1)} %slice.83) | copy-start | bytes 3932164
  77.1 3.2 %copy-start.2 = (s32[1,256]{1,0:T(1,128)S(1)}, s32[1,256]{1,0:T(1,128)}, u32[]{:S(2)}) copy-start(s32[1,256]{1,0:T(1,128)} %param.11) | copy-start | bytes 3076
  81.0 19.9 %all-to-all-start.1 = ((f32[16,8,128]{2,1,0:T(8,128)}), f32[16,8,128]{2,1,0:T(8,128)S(1)}, u32[]{:S(2)}, u32[]{:S(2)}) async-start(f32[16,8,128]{2,1,0:T(8,128)} %broadcast_in_dim.15), calls=%async_computation.1 | async-start | bytes 131072 | tf_op jit(solution)/shard_map/stats/all_to_all | solution.py:98
  111.8 6.2 %collective-permute-start.2 = (bf16[5120,128]{1,0:T(8,128)(2,1)}, bf16[5120,128]{1,0:T(8,128)(2,1)}, u32[]{:S(2)}, u32[]{:S(2)}) collective-permute-start(bf16[5120,128]{1,0:T(8,128)(2,1)} %get-tuple-element.22), channel_id=1, source_target_pairs={{0,1},{1,0},{2,3},{3,2},{4,5},{5,4},{6,7},{7,6},{8,9},{9,8},{10,11... | collective-permute-start | bytes 3932168 | tf_op jit(solution)/shard_map/reduce/ppermute | solution.py:128
  161.9 21.2 %all-to-all-start.3 = ((bf16[12,80,128]{2,1,0:T(8,128)(2,1)}), bf16[12,80,128]{2,1,0:T(8,128)(2,1)S(1)}, u32[]{:S(2)}, u32[]{:S(2)}) async-start(bf16[12,80,128]{2,1,0:T(8,128)(2,1)} %bitcast.22), calls=%async_computation.3 | async-start | bytes 491520 | tf_op jit(solution)/shard_map/reduce/all_to_all | solution.py:144

commit v3 on v2

v3 whole, which is shorter than its diff:
```python
import jax
import jax.numpy as jnp
from jax import lax
from jax.experimental import pallas as pl
from jax.experimental.pallas import tpu as pltpu
from jax.sharding import Mesh, PartitionSpec as P

EPSILON = 1e-06
SOFT_CAP = 30.0
YX = ("yh", "yl", "x")
WIDE = ("yh", "yl", "x", "zh")
NARROW = ("zl", "c")
Z = ("zh", "zl")
SWAP = [(0, 1), (1, 0)]
LIST_DEVICES = 16
VMEM_LIMIT = 48 * 1024 * 1024
F32 = jnp.float32
BF16 = jnp.bfloat16


def half_partner():
    pairs = []
    for z in range(12):
        to = (z + 3) % 12 if z % 6 >= 3 else (z - 3) % 12
        pairs.append((z, to))
    return pairs


def lane_fold(x):
    total = x[:, :128]
    for k in range(1, x.shape[1] // 128):
        total = total + x[:, 128 * k : 128 * (k + 1)]
    return total


def forward_kernel(
    core_ref,
    hidden_ref,
    root_ref,
    own_ref,
    beside_ref,
    gain_ref,
    scale_ref,
    weighted_ref,
    value_scale_ref,
    segment_ref,
    normed_ref,
    resid_ref,
    out_ref,
    half_ref,
    columns_ref,
    stats_ref,
    value_ref,
):
    blocks, _, _ = own_ref.shape
    tokens, width = hidden_ref.shape
    per = width // blocks
    tile = 4 * per

    def place(value_from, out_from):
        for k in range(blocks):
            value_ref[per * k : per * (k + 1), :] = value_from[k, :per, :]
            out_ref[per * k : per * (k + 1), :] = out_from[k, :per, :]

    @pl.when(core_ref[0] == 0)
    def _():
        place(own_ref, beside_ref)

    @pl.when(core_ref[0] != 0)
    def _():
        place(beside_ref, own_ref)

    inverse = 1.0 / root_ref[...]
    mixed = jnp.zeros((tokens, value_ref.shape[1]), F32)
    for j in range(width // tile):
        span = slice(tile * j, tile * (j + 1))
        scaled = hidden_ref[:, span].astype(F32) * inverse
        normed = (scaled * gain_ref[:, span]).astype(BF16)
        normed_ref[:, span] = normed
        mixed = mixed + jnp.dot(normed, value_ref[span, :], preferred_element_type=F32)
    value_half = (mixed * value_scale_ref[...]).astype(BF16)
    half_ref[...] = value_half
    squares = jnp.zeros((tokens, 128), F32)
    scores = jnp.zeros((tokens, 128), F32)
    for j in range(width // tile):
        span = slice(tile * j, tile * (j + 1))
        branch = lax.dot_general(
            value_half, out_ref[span, :], (((1,), (1,)), ((), ())), preferred_element_type=F32
        )
        residual = (hidden_ref[:, span].astype(F32) + branch * scale_ref[:, span]).astype(BF16)
        resid_ref[:, span] = residual
        resid32 = residual.astype(F32)
        squares = squares + lane_fold(resid32 * resid32)
        scores = scores + lane_fold(resid32 * weighted_ref[:, span])
    final_root = jnp.sqrt(jnp.sum(squares, axis=1, keepdims=True) / width + EPSILON)
    raw_score = jnp.sum(scores, axis=1, keepdims=True) / final_root
    capped = jnp.tanh(raw_score / SOFT_CAP)
    slope = 1.0 - capped * capped
    lead = slope / final_root
    pull = slope * raw_score / (width * final_root * final_root)
    lanes = lax.broadcasted_iota(jnp.int32, (tokens, 128), 1)
    columns_ref[...] = jnp.where(lanes == 0, lead, pull)
    member = segment_ref[...] == lanes
    sums = jnp.sum(jnp.where(member, SOFT_CAP * capped, 0.0), axis=0, keepdims=True)
    counts = jnp.sum(jnp.where(member, 1.0, 0.0), axis=0, keepdims=True)
    row = lax.broadcasted_iota(jnp.int32, (8, 128), 0)
    packed = jnp.where(row == 0, sums, counts)
    for k in range(stats_ref.shape[0]):
        stats_ref[k] = packed


def backward_kernel(
    resid_ref, out_ref, columns_ref, scale_ref, weighted_ref, value_scale_ref, unit_ref, values_ref
):
    tokens, width = resid_ref.shape
    tile = 640
    lead = columns_ref[:, 0:1]
    pull = columns_ref[:, 1:2]
    total = jnp.zeros(values_ref.shape, F32)
    for j in range(width // tile):
        span = slice(tile * j, tile * (j + 1))
        slope = lead * weighted_ref[:, span] - pull * resid_ref[:, span].astype(F32)
        unit = (slope * scale_ref[:, span]).astype(BF16)
        unit_ref[:, span] = unit
        total = total + jnp.dot(unit, out_ref[span, :], preferred_element_type=F32)
    values_ref[...] = total * value_scale_ref[...]


def term_kernel(pick_ref, normed_ref, unit_ref, values_ref, half_ref, factor_ref, term_ref, small_ref):
    @pl.when(pl.program_id(0) == 0)
    def _():
        side = jnp.where(pick_ref[0] == 0, values_ref[...], half_ref[...].astype(F32))
        small_ref[...] = (factor_ref[...] * side).T.astype(BF16)

    def fill(tall_ref):
        term = jnp.dot(small_ref[...], tall_ref[...], preferred_element_type=F32)
        term_ref[...] = term.T.astype(term_ref.dtype)

    @pl.when(pick_ref[0] == 0)
    def _():
        fill(normed_ref)

    @pl.when(pick_ref[0] != 0)
    def _():
        fill(unit_ref)


def run_forward(core, hidden, root, own, beside, gain, scale, weighted, value_scale, segment):
    tokens, width = hidden.shape
    head = value_scale.shape[1]
    shape = jax.ShapeDtypeStruct
    vmem = pl.BlockSpec(memory_space=pltpu.VMEM)
    return pl.pallas_call(
        forward_kernel,
        out_shape=(
            shape((tokens, width), BF16),
            shape((tokens, width), BF16),
            shape((width, head), BF16),
            shape((tokens, head), BF16),
            shape((tokens, 128), F32),
            shape((LIST_DEVICES, 8, 128), F32),
        ),
        in_specs=[pl.BlockSpec(memory_space=pltpu.SMEM)] + [vmem] * 9,
        out_specs=(vmem,) * 6,
        scratch_shapes=[pltpu.VMEM((width, head), BF16)],
        compiler_params=pltpu.CompilerParams(vmem_limit_bytes=VMEM_LIMIT),
        cost_estimate=pl.CostEstimate(
            flops=4 * tokens * width * head, bytes_accessed=12 * width * tokens, transcendentals=tokens
        ),
        name="forward",
    )(core, hidden, root, own, beside, gain, scale, weighted, value_scale, segment)


def run_backward(resid, out_full, columns, scale, weighted, value_scale):
    tokens, width = resid.shape
    head = value_scale.shape[1]
    vmem = pl.BlockSpec(memory_space=pltpu.VMEM)
    return pl.pallas_call(
        backward_kernel,
        out_shape=(
            jax.ShapeDtypeStruct((tokens, width), BF16),
            jax.ShapeDtypeStruct((tokens, head), F32),
        ),
        in_specs=[vmem] * 6,
        out_specs=(vmem,) * 2,
        compiler_params=pltpu.CompilerParams(vmem_limit_bytes=VMEM_LIMIT),
        cost_estimate=pl.CostEstimate(
            flops=2 * tokens * width * head, bytes_accessed=8 * width * tokens, transcendentals=0
        ),
        name="backward",
    )(resid, out_full, columns, scale, weighted, value_scale)


def run_term(pick, normed, unit, values, half, factor, dtype):
    tokens, width = normed.shape
    head = values.shape[1]
    tile = 1280
    whole = lambda j, pick: (0, 0)
    return pl.pallas_call(
        term_kernel,
        out_shape=jax.ShapeDtypeStruct((width, head), dtype),
        grid_spec=pltpu.PrefetchScalarGridSpec(
            num_scalar_prefetch=1,
            grid=(width // tile,),
            in_specs=[
                pl.BlockSpec((tokens, tile), lambda j, pick: (0, j * (1 - pick[0]))),
                pl.BlockSpec((tokens, tile), lambda j, pick: (0, j * pick[0])),
                pl.BlockSpec((tokens, head), whole),
                pl.BlockSpec((tokens, head), whole),
                pl.BlockSpec((tokens, 1), whole),
            ],
            out_specs=pl.BlockSpec((tile, head), lambda j, pick: (j, 0)),
            scratch_shapes=[pltpu.VMEM((head, tokens), BF16)],
        ),
        compiler_params=pltpu.CompilerParams(vmem_limit_bytes=VMEM_LIMIT),
        cost_estimate=pl.CostEstimate(
            flops=2 * tokens * width * head, bytes_accessed=4 * width * tokens, transcendentals=0
        ),
        name="term",
    )(pick, normed, unit, values, half, factor)


def shards(
    hidden,
    segment,
    grades,
    value_codes,
    value_scale,
    output_codes,
    output_scale,
    norm_gain,
    final_gain,
    score_vector,
):
    rows, head_size = value_codes.shape
    core = lax.axis_index("c")
    z_half = lax.axis_index("zh")
    first = core == 0
    tokens = hidden[0]
    width = tokens.shape[1]
    seg_local = segment[0][:, None]
    grade_rows = grades[0]
    cand_count = grade_rows.shape[1]

    with jax.named_scope("gather"):
        vectors = jnp.where(
            first, jnp.stack([norm_gain, output_scale]), jnp.stack([final_gain, score_vector])
        )
        vectors = jnp.pad(vectors, ((0, 6), (0, head_size - rows)))
        mine = jnp.concatenate([jnp.where(first, value_codes, output_codes), vectors], axis=0)
        other = lax.ppermute(mine, Z, half_partner())
        low = jnp.where(z_half == 0, mine, other)
        high = jnp.where(z_half == 0, other, mine)
        block = jnp.concatenate([low[:rows], high[:rows], low[rows : rows + 2], high[rows : rows + 6]], axis=0)
        spread = jnp.broadcast_to(block, (32,) + block.shape)
        own = lax.all_to_all(spread, YX, 0, 0)
        tokens32 = tokens.astype(F32)
        root = jnp.sqrt(jnp.mean(tokens32 * tokens32, axis=-1, keepdims=True) + EPSILON)
        own, root = lax.optimization_barrier((own, root))
        beside = lax.ppermute(own, "c", SWAP)

        def vector(block, which):
            parts = block[:, 2 * rows : 2 * rows + 4, :rows].reshape(32, 2, 2, rows)
            return parts[:, :, which].reshape(1, width).astype(F32)

        gain32 = jnp.where(first, vector(own, 0), vector(beside, 0))
        scale32 = jnp.where(first, vector(own, 1), vector(beside, 1))
        final32 = jnp.where(first, vector(beside, 0), vector(own, 0))
        score32 = jnp.where(first, vector(beside, 1), vector(own, 1))
        weighted = final32 * score32

    value_row = value_scale[None, :]
    pick = core.astype(jnp.int32)[None]
    normed, resid, out_full, value_half, columns, stats = run_forward(
        pick, tokens, root, own, beside, gain32, scale32, weighted, value_row, seg_local
    )
    with jax.named_scope("stats"):
        arrived = lax.all_to_all(stats, ("yl", "x", "zh"), 0, 0)

    unit, values = run_backward(resid, out_full, columns, scale32, weighted, value_row)

    with jax.named_scope("factor"):
        stats = jnp.sum(arrived, axis=0)
        sums, counts = stats[0, :cand_count], stats[1, :cand_count]
        cand_score = sums / counts
        teacher = lax.dynamic_index_in_dim(grade_rows, lax.axis_index("yh"), 0, keepdims=False)
        teacher = teacher.astype(F32)
        log_teacher = teacher - jnp.log(jnp.sum(jnp.exp(teacher)))
        log_student = cand_score - jnp.log(jnp.sum(jnp.exp(cand_score)))
        own_loss = jnp.sum(jnp.exp(log_teacher) * (log_teacher - log_student))
        grad_cand = (jnp.exp(log_student) - jnp.exp(log_teacher)) / counts
        member = (seg_local == jnp.arange(cand_count, dtype=jnp.int32)).astype(F32)
        factor = jnp.sum(member * grad_cand, axis=-1, keepdims=True)

    give = run_term(1 - pick, normed, unit, values, value_half, factor, BF16)
    with jax.named_scope("reduce"):
        got = lax.ppermute(give, "c", SWAP)
        keep = run_term(pick, normed, unit, values, value_half, factor, F32)
        both = (keep + got.astype(F32)).astype(BF16)
        loss_hi = own_loss.astype(BF16)
        loss_lo = (own_loss - loss_hi.astype(F32)).astype(BF16)
        loss_row = jnp.pad(jnp.stack([loss_hi, loss_lo])[None, :], ((0, 7), (0, head_size - 2)))
        sent = jnp.concatenate(
            [both.reshape(32, 2 * rows, head_size), jnp.broadcast_to(loss_row, (32, 8, head_size))],
            axis=1,
        )
        came = lax.all_to_all(sent, YX, 0, 0)
        part = jnp.sum(came[:, : 2 * rows].astype(F32), axis=0)
        losses = came.reshape(4, 8, 2 * rows + 8, head_size)[:, 0, 2 * rows, :2]
        list_loss = jnp.sum(losses.astype(F32), axis=-1)
        part = part.astype(BF16).reshape(2, 1, rows, head_size)
        part = jnp.broadcast_to(part, (2, 6, rows, head_size)).reshape(12, rows, head_size)
        total = jnp.sum(lax.all_to_all(part, Z, 0, 0).astype(F32), axis=0)
        pair = lax.all_gather(total, "c")
    return (pair[0], pair[1], list_loss[None, :])


def solution(mesh):
    grid = Mesh(mesh.devices.reshape(4, 2, 4, 2, 6, 2), WIDE + NARROW)
    in_specs = (
        P(NARROW, WIDE, None),
        P(NARROW, WIDE),
        P(NARROW, None, None),
        P(WIDE, None),
        P(),
        P(WIDE, None),
        P(WIDE),
        P(WIDE),
        P(WIDE),
        P(WIDE),
    )
    out_specs = (P(WIDE, None), P(WIDE, None), P(NARROW, None))
    return jax.shard_map(shards, mesh=grid, in_specs=in_specs, out_specs=out_specs, check_vma=False)
```

time: 188 us -> 183 us (0.973)
  blocking collectives: 87.1 us -> 43.3 us
  waiting for transfers between devices: 23.4 us -> 51.8 us
  Pallas kernels: 0 us -> 17.1 us
  matrix products: 14.9 us -> 0 us
  starting transfers between devices: 38.3 us -> 50.9 us
  other arithmetic: 15 us -> 8.47 us
  local copies, waits for them, and re-layouts: 4.87 us -> 7.46 us
    all_to_all x1 -> x0, blocking collectives: 43.4 us -> none  [shards(): own = lax.all_to_all(spread, YX, 0, 0)]
    all_to_all x2 -> x3, waiting for transfers between devices: 21.2 us -> 48.2 us  [the longest x1 29.4 us: shards(): own = lax.all_to_all(spread, YX, 0, 0)]
    pallas_call x0 -> x4, Pallas kernels: none -> 17.1 us  [the longest x2 7.69 us: run_term(): pl.pallas_call(term_kernel, out_shape=jax.ShapeDtypeStruct((width, head),...]
    dot_general x4 -> x0, matrix products: 14.9 us -> none  [the longest x2 9.36 us: contract_rows(): lax.dot_general(left, right, (((0,), (0,)), ((), ())), preferred_element_...]
    all_to_all x2 -> x3, starting transfers between devices: 14.4 us -> 25.5 us  [the longest x1 9.67 us: shards(): own = lax.all_to_all(spread, YX, 0, 0)]
    convert_element_type x3 -> x1, other arithmetic: 7.79 us -> 1.57 us  [shards(): both = (keep + got.astype(F32)).astype(BF16)]
    unnamed x10 -> x14, local copies, waits for them, and re-layouts: 0.03 us -> 3.93 us
    ppermute x1, waiting for transfers between devices: 0.01 us -> 2.42 us  [shards(): beside = lax.ppermute(own, 'c', SWAP)]
  transfers between devices with their start and end apart: 5 -> 6, of which waited for: 4 -> 5; matrix products, arithmetic and copies ran while one was open for 5% -> 3% of each run, Pallas kernels for 0% -> 4%
where the time goes in v3:
time: 183 us
  waiting for transfers between devices  51.8 us (28%)
  starting transfers between devices  50.9 us (28%)
  blocking collectives  43.3 us (24%)
  Pallas kernels  17.1 us (9%)
  other arithmetic  8.47 us (5%)
  local copies, waits for them, and re-layouts  7.46 us (4%)
  between operations  3.63 us (2%)
    all_to_all x1, blocking collectives, shards(): came = lax.all_to_all(sent, YX, 0, 0)  39.9 us
    all_to_all x1, waiting for transfers between devices, shards(): own = lax.all_to_all(spread, YX, 0, 0)  29.4 us
    ppermute x1, starting transfers between devices, shards(): other = lax.ppermute(mine, Z, half_partner())  15.1 us
    all_to_all x1, waiting for transfers between devices, shards(): total = jnp.sum(lax.all_to_all(part, Z, 0, 0).astype(F32), axis=0)  13.9 us
    all_to_all x1, starting transfers between devices, shards(): own = lax.all_to_all(spread, YX, 0, 0)  9.67 us
    all_to_all x1, starting transfers between devices, shards(): arrived = lax.all_to_all(stats, ('yl', 'x', 'zh'), 0, 0)  9.26 us
    pallas_call x2, Pallas kernels, run_term(): pl.pallas_call(term_kernel, out_shape=jax.ShapeDtypeStruct((width, head),...  7.69 us
    all_to_all x1, starting transfers between devices, shards(): total = jnp.sum(lax.all_to_all(part, Z, 0, 0).astype(F32), axis=0)  6.55 us
  transfers between devices with their start and end apart: 6, of which 5 were waited for; matrix products, arithmetic and copies ran while one was open for 3% of the time, Pallas kernels for 4%

profile of v3, /device:TPU:1, one launch (start us, length us, event | category | flops | bytes accessed | tf_op | source)
XLA Modules:
  0.0 182.6 jit_solution(13216199465078038100)
XLA Ops:
  0.6 0.7 broadcast_select_fusion.2
  1.4 0.7 broadcast_select_fusion.3
  2.1 15.1 %collective-permute-start = (bf16[88,128]{1,0:T(8,128)(2,1)S(1)}, bf16[88,128]{1,0:T(8,128)(2,1)S(1)}, u32[]{:S(2)}, u32[]{:S(2)}) collective-permute-start(bf16[88,128]{1,0:T(8,128)(2,1)S(1)} %fusion.2), channel_id=1, source_target_pairs={{0,18},{2,20},{4,22},{6,12},{8,14},{10,16},{12,6},{14,8},{16,10},{... | collective-permute-start | bytes 67592 | tf_op jit(solution)/shard_map/gather/ppermute | solution.py:251
  17.2 1.2 collective-permute-done
  18.5 1.3 broadcast_in_dim.32
  19.8 9.7 %all-to-all-start = ((bf16[32,168,128]{2,1,0:T(8,128)(2,1)}), bf16[32,168,128]{2,1,0:T(8,128)(2,1)S(1)}, u32[]{:S(2)}, u32[]{:S(2)}) async-start(bf16[32,168,128]{2,1,0:T(8,128)(2,1)} %broadcast_in_dim.32), calls=%async_computation | async-start | bytes 2752512 | tf_op jit(solution)/shard_map/gather/all_to_all | solution.py:256
  29.5 0.0 copy-start.5
  29.5 0.0 copy-start.4
  29.5 2.3 %multiply_reduce_fusion = f32[256]{0:T(256)S(1)} fusion(bf16[1,256,5120]{2,1,0:T(8,128)(2,1)} %param.10), kind=kLoop, calls=%fused_computation | loop fusion | flops 3931904 | bytes 2622464 | tf_op jit(solution)/shard_map/gather/reduce_sum | solution.py:258
  31.9 29.4 %all-to-all-done.own_ref = bf16[32,168,128]{2,1,0:T(8,128)(2,1)S(1)} async-done(((bf16[32,168,128]{2,1,0:T(8,128)(2,1)}), bf16[32,168,128]{2,1,0:T(8,128)(2,1)S(1)}, u32[]{:S(2)}, u32[]{:S(2)}) %all-to-all-start) | async-done | bytes 1376288 | tf_op jit(solution)/shard_map/gather/all_to_all | solution.py:256
  61.3 6.0 %collective-permute-start.1 = (bf16[32,168,128]{2,1,0:T(8,128)(2,1)S(1)}, bf16[32,168,128]{2,1,0:T(8,128)(2,1)S(1)}, u32[]{:S(2)}, u32[]{:S(2)}) collective-permute-start(bf16[32,168,128]{2,1,0:T(8,128)(2,1)S(1)} %all-to-all-done.own_ref), channel_id=1, source_target_pairs={{0,1},{1,0},{2,3},{3,2},{4,5},{5,4},{6,7},{7,6},{8,9},{9,8},{10,11... | collective-permute-start | bytes 4128776 | tf_op jit(solution)/shard_map/gather/ppermute | solution.py:260
  67.3 0.0 copy-done.5
  67.3 0.1 copy.30.segment_ref
  67.5 0.1 copy.29.root_ref
  67.6 2.4 %collective-permute-done.1.beside_ref = bf16[32,168,128]{2,1,0:T(8,128)(2,1)S(1)} collective-permute-done((bf16[32,168,128]{2,1,0:T(8,128)(2,1)S(1)}, bf16[32,168,128]{2,1,0:T(8,128)(2,1)S(1)}, u32[]{:S(2)}, u32[]{:S(2)}) %collective-permute-start.1) | collective-permute-done | bytes 1376288 | tf_op jit(solution)/shard_map/gather/ppermute | solution.py:260
  70.0 0.1 fusion.9
  70.2 0.1 mul.23.weighted_ref
  70.3 0.1 select_n.83.gain_ref
  70.5 0.1 select_n.85.scale_ref
  70.6 0.0 copy-done.4
  70.6 0.0 copy-start.6
  70.6 6.1 %forward.1 = (bf16[256,5120]{1,0:T(8,128)(2,1)}, bf16[256,5120]{1,0:T(8,128)(2,1)}, bf16[5120,128]{1,0:T(8,128)(2,1)S(1)}, bf16[256,128]{1,0:T(8,128)(2,1)S(1)},...) custom-call(s32[1]{0:T(128)} %bitcast.core_ref.pick_ref, bf16[256,5120]{1,0:T(8,128)(2,1)} %bitcast.50, ...), custom_call_target="tpu_custom_call" | custom-call | flops 671088640 | bytes 15728640 | tf_op jit(solution)/shard_map/forward/pallas_call | solution.py:153
  76.7 0.0 copy-start.2
  76.7 1.1 copy-done.2
  77.8 9.3 %all-to-all-start.1 = ((f32[16,8,128]{2,1,0:T(8,128)}), f32[16,8,128]{2,1,0:T(8,128)S(1)}, u32[]{:S(2)}, u32[]{:S(2)}) async-start(f32[16,8,128]{2,1,0:T(8,128)} %get-tuple-element.22), calls=%async_computation.1 | async-start | bytes 131072 | tf_op jit(solution)/shard_map/stats/all_to_all | solution.py:278
  87.1 0.0 copy-done.6
  87.1 0.6 exponential_reduce_fusion
  88.4 0.0 copy-start.3
  88.4 1.3 copy-done.3
  89.7 0.0 copy-start
  89.7 3.3 %backward.1 = (bf16[256,5120]{1,0:T(8,128)(2,1)S(1)}, f32[256,128]{1,0:T(8,128)S(1)}) custom-call(bf16[256,5120]{1,0:T(8,128)(2,1)} %get-tuple-element.16.resid_ref, bf16[5120,128]{1,0:T(8,128)(2,1)S(1)} %copy-done.3, f32[256,128]{1,0:T(8,128)S(1)} %get-tuple-element.18.columns_ref, f32[1,5120]{1,0:T(1,128)S(1)} %select_n.85.scale_ref, ...), custom_call_target="tpu_custom_call" | custom-call | flops 335544320 | bytes 10485760 | tf_op jit(solution)/shard_map/backward/pallas_call | solution.py:178
  93.0 0.0 copy-start.1
  93.0 1.5 copy-done.1
  94.5 4.9 %all-to-all-done.1 = f32[16,8,128]{2,1,0:T(8,128)S(1)} async-done(((f32[16,8,128]{2,1,0:T(8,128)}), f32[16,8,128]{2,1,0:T(8,128)S(1)}, u32[]{:S(2)}, u32[]{:S(2)}) %all-to-all-start.1) | async-done | bytes 65568 | tf_op jit(solution)/shard_map/stats/all_to_all | solution.py:278
  99.4 0.6 exponential_reduce_fusion.1
  100.7 0.1 select_reduce_fusion
  100.8 0.1 copy.31.factor_ref
  101.0 0.0 copy-done
  101.0 3.9 %term.3 = bf16[5120,128]{1,0:T(8,128)(2,1)} custom-call(s32[1]{0:T(128)S(6)} %sub.45.pick_ref, bf16[256,5120]{1,0:T(8,128)(2,1)S(1)} %copy-done, bf16[256,5120]{1,0:T(8,128)(2,1)} %copy-done.1, f32[256,128]{1,0:T(8,128)S(1)} %get-tuple-element.20.values_ref, bf16[256,128]{1,0:T(8,128)(2,1)S(1)} %get-tuple-element.21.half_ref, f32[256,1]{1,0:T(8,128)S(1)} %copy.31.factor_ref), custom_call_target="tpu_custom_call" | custom-call | flops 335544320 | bytes 5242880 | tf_op jit(solution)/shard_map/term/pallas_call | solution.py:199
  104.9 4.3 %collective-permute-start.2 = (bf16[5120,128]{1,0:T(8,128)(2,1)}, bf16[5120,128]{1,0:T(8,128)(2,1)}, u32[]{:S(2)}, u32[]{:S(2)}) collective-permute-start(bf16[5120,128]{1,0:T(8,128)(2,1)} %term.3), channel_id=1, source_target_pairs={{0,1},{1,0},{2,3},{3,2},{4,5},{5,4},{6,7},{7,6},{8,9},{9,8},{10,11... | collective-permute-start | bytes 3932168 | tf_op jit(solution)/shard_map/reduce/ppermute | solution.py:297
  109.2 0.6 fusion.5
  111.1 0.1 maximum_bitcast_fusion
  111.2 3.8 %term.2 = f32[5120,128]{1,0:T(8,128)S(1)} custom-call(s32[1]{0:T(128)} %bitcast.core_ref.pick_ref, bf16[256,5120]{1,0:T(8,128)(2,1)S(1)} %copy-done, bf16[256,5120]{1,0:T(8,128)(2,1)} %copy-done.1, f32[256,128]{1,0:T(8,128)S(1)} %get-tuple-element.20.values_ref, bf16[256,128]{1,0:T(8,128)(2,1)S(1)} %get-tuple-element.21.half_ref, f32[256,1]{1,0:T(8,128)S(1)} %copy.31.factor_ref), custom_call_target="tpu_custom_call" | custom-call | flops 335544320 | bytes 5242880 | tf_op jit(solution)/shard_map/reduce/term/pallas_call | solution.py:199
  115.0 0.0 collective-permute-done.2
  115.0 1.6 add_convert_fusion
  116.6 0.1 pad_maximum_fusion
  116.7 39.9 %all_to_all.20 = bf16[32,168,128]{2,1,0:T(8,128)(2,1)S(1)} all-to-all(bf16[32,168,128]{2,1,0:T(8,128)(2,1)S(1)} %pad_maximum_fusion), channel_id=1, replica_groups=mesh['yh'=4,'yl'=2,'x'=4,'zh'=2,'zl'=6,'c'=2] {'yh','yl','x'}, dimensions={0} | all-to-all | bytes 2752512 | tf_op jit(solution)/shard_map/reduce/all_to_all | solution.py:307
  156.6 0.2 slice_reduce_fusion
  156.8 0.7 broadcast_in_dim.38
  157.5 6.5 %all-to-all-start.3 = ((bf16[12,80,128]{2,1,0:T(8,128)(2,1)}), bf16[12,80,128]{2,1,0:T(8,128)(2,1)S(1)}, u32[]{:S(2)}, u32[]{:S(2)}) async-start(bf16[12,80,128]{2,1,0:T(8,128)(2,1)} %bitcast.22), calls=%async_computation.3 | async-start | bytes 491520 | tf_op jit(solution)/shard_map/reduce/all_to_all | solution.py:313
  164.1 0.6 fusion.3
  164.7 13.9 %all-to-all-done.3 = bf16[12,80,128]{2,1,0:T(8,128)(2,1)S(1)} async-done(((bf16[12,80,128]{2,1,0:T(8,128)(2,1)}), bf16[12,80,128]{2,1,0:T(8,128)(2,1)S(1)}, u32[]{:S(2)}, u32[]{:S(2)}) %all-to-all-start.3) | async-done | bytes 245792 | tf_op jit(solution)/shard_map/reduce/all_to_all | solution.py:313
  178.6 3.3 %all-gather = f32[160,128]{1,0:T(8,128)S(1)} all-gather(f32[80,128]{1,0:T(8,128)S(1)} %convert_reduce_fusion), channel_id=2, replica_groups=mesh['yh'=4,'yl'=2,'x'=4,'zh'=2,'zl'=6,'c'=2] {'c'}, dimensions={0}, use_global_device_ids=true | all-gather | bytes 122880 | tf_op jit(solution)/shard_map/reduce/all_gather | solution.py:314
  182.0 0.6 fusion.8
  (16 shorter events, 0.2 us)
Async XLA Ops:
  2.1 16.3 %collective-permute-start = (bf16[88,128]{1,0:T(8,128)(2,1)S(1)}, bf16[88,128]{1,0:T(8,128)(2,1)S(1)}, u32[]{:S(2)}, u32[]{:S(2)}) collective-permute-start(bf16[88,128]{1,0:T(8,128)(2,1)S(1)} %fusion.2), channel_id=1, source_target_pairs={{0,18},{2,20},{4,22},{6,12},{8,14},{10,16},{12,6},{14,8},{16,10},{... | collective-permute-start | bytes 67592 | tf_op jit(solution)/shard_map/gather/ppermute | solution.py:251
  19.8 41.5 %all-to-all-start = ((bf16[32,168,128]{2,1,0:T(8,128)(2,1)}), bf16[32,168,128]{2,1,0:T(8,128)(2,1)S(1)}, u32[]{:S(2)}, u32[]{:S(2)}) async-start(bf16[32,168,128]{2,1,0:T(8,128)(2,1)} %broadcast_in_dim.32), calls=%async_computation | async-start | bytes 2752512 | tf_op jit(solution)/shard_map/gather/all_to_all | solution.py:256
  29.5 37.8 %copy-start.5 = (s32[1,256]{1,0:T(1,128)S(1)}, s32[1,256]{1,0:T(1,128)}, u32[]{:S(2)}) copy-start(s32[1,256]{1,0:T(1,128)} %param.11) | copy-start | bytes 3076
  29.5 41.1 %copy-start.4 = (f32[128]{0:T(128)S(1)}, f32[128]{0:T(128)}, u32[]{:S(2)}) copy-start(f32[128]{0:T(128)} %param.14) | copy-start | bytes 1540
  61.3 8.7 %collective-permute-start.1 = (bf16[32,168,128]{2,1,0:T(8,128)(2,1)S(1)}, bf16[32,168,128]{2,1,0:T(8,128)(2,1)S(1)}, u32[]{:S(2)}, u32[]{:S(2)}) collective-permute-start(bf16[32,168,128]{2,1,0:T(8,128)(2,1)S(1)} %all-to-all-done.own_ref), channel_id=1, source_target_pairs={{0,1},{1,0},{2,3},{3,2},{4,5},{5,4},{6,7},{7,6},{8,9},{9,8},{10,11... | collective-permute-start | bytes 4128776 | tf_op jit(solution)/shard_map/gather/ppermute | solution.py:260
  70.6 16.5 %copy-start.6 = (s32[1,4,20]{2,1,0:T(4,128)S(1)}, s32[1,4,20]{2,1,0:T(4,128)}, u32[]{:S(2)}) copy-start(s32[1,4,20]{2,1,0:T(4,128)} %param.12) | copy-start | bytes 964
  76.7 1.1 copy-start.2
  77.8 21.6 %all-to-all-start.1 = ((f32[16,8,128]{2,1,0:T(8,128)}), f32[16,8,128]{2,1,0:T(8,128)S(1)}, u32[]{:S(2)}, u32[]{:S(2)}) async-start(f32[16,8,128]{2,1,0:T(8,128)} %get-tuple-element.22), calls=%async_computation.1 | async-start | bytes 131072 | tf_op jit(solution)/shard_map/stats/all_to_all | solution.py:278
  88.4 1.3 copy-start.3
  89.7 11.3 %copy-start = (bf16[256,5120]{1,0:T(8,128)(2,1)S(1)}, bf16[256,5120]{1,0:T(8,128)(2,1)}, u32[]{:S(2)}) copy-start(bf16[256,5120]{1,0:T(8,128)(2,1)} %get-tuple-element.15.normed_ref) | copy-start | bytes 7864324
  93.0 1.5 copy-start.1
  104.9 10.1 %collective-permute-start.2 = (bf16[5120,128]{1,0:T(8,128)(2,1)}, bf16[5120,128]{1,0:T(8,128)(2,1)}, u32[]{:S(2)}, u32[]{:S(2)}) collective-permute-start(bf16[5120,128]{1,0:T(8,128)(2,1)} %term.3), channel_id=1, source_target_pairs={{0,1},{1,0},{2,3},{3,2},{4,5},{5,4},{6,7},{7,6},{8,9},{9,8},{10,11... | collective-permute-start | bytes 3932168 | tf_op jit(solution)/shard_map/reduce/ppermute | solution.py:297
  157.5 21.0 %all-to-all-start.3 = ((bf16[12,80,128]{2,1,0:T(8,128)(2,1)}), bf16[12,80,128]{2,1,0:T(8,128)(2,1)S(1)}, u32[]{:S(2)}, u32[]{:S(2)}) async-start(bf16[12,80,128]{2,1,0:T(8,128)(2,1)} %bitcast.22), calls=%async_computation.3 | async-start | bytes 491520 | tf_op jit(solution)/shard_map/reduce/all_to_all | solution.py:313

commit v4 on v3

--- a/solution.py
+++ b/solution.py
@@ -7,10 +7,11 @@
 
 EPSILON = 1e-06
 SOFT_CAP = 30.0
-YX = ("yh", "yl", "x")
+Y = ("yh", "yl")
 WIDE = ("yh", "yl", "x", "zh")
-NARROW = ("zl", "c")
-Z = ("zh", "zl")
+NARROW = ("za", "zb", "c")
+Z = ("zh", "za", "zb")
+XB = ("x", "zb")
 SWAP = [(0, 1), (1, 0)]
 LIST_DEVICES = 16
 VMEM_LIMIT = 48 * 1024 * 1024
@@ -21,9 +22,17 @@
 def half_partner():
     pairs = []
     for z in range(12):
-        to = (z + 3) % 12 if z % 6 >= 3 else (z - 3) % 12
-        pairs.append((z, to))
+        if z // 6 != z % 2:
+            pairs.append((z, (z + 3) % 12 if z % 6 >= 3 else (z - 3) % 12))
     return pairs
+
+
+def place(source_ref, rows, target_ref):
+    pairs, ys = source_ref.shape[0], source_ref.shape[1]
+    for y in range(ys):
+        for k in range(pairs):
+            at = rows * (y * pairs + k)
+            target_ref[at : at + rows, :] = source_ref[k, y, :rows, :]
 
 
 def lane_fold(x):
@@ -46,29 +55,25 @@
     segment_ref,
     normed_ref,
     resid_ref,
-    out_ref,
     half_ref,
     columns_ref,
     stats_ref,
     value_ref,
+    out_ref,
 ):
-    blocks, _, _ = own_ref.shape
     tokens, width = hidden_ref.shape
-    per = width // blocks
-    tile = 4 * per
-
-    def place(value_from, out_from):
-        for k in range(blocks):
-            value_ref[per * k : per * (k + 1), :] = value_from[k, :per, :]
-            out_ref[per * k : per * (k + 1), :] = out_from[k, :per, :]
+    rows = width // (own_ref.shape[0] * own_ref.shape[1])
+    tile = 640
 
     @pl.when(core_ref[0] == 0)
     def _():
-        place(own_ref, beside_ref)
+        place(own_ref, rows, value_ref)
+        place(beside_ref, rows, out_ref)
 
     @pl.when(core_ref[0] != 0)
     def _():
-        place(beside_ref, own_ref)
+        place(beside_ref, rows, value_ref)
+        place(own_ref, rows, out_ref)
 
     inverse = 1.0 / root_ref[...]
     mixed = jnp.zeros((tokens, value_ref.shape[1]), F32)
@@ -110,10 +115,30 @@
 
 
 def backward_kernel(
-    resid_ref, out_ref, columns_ref, scale_ref, weighted_ref, value_scale_ref, unit_ref, values_ref
+    core_ref,
+    resid_ref,
+    own_ref,
+    beside_ref,
+    columns_ref,
+    scale_ref,
+    weighted_ref,
+    value_scale_ref,
+    unit_ref,
+    values_ref,
+    out_ref,
 ):
     tokens, width = resid_ref.shape
+    rows = width // (own_ref.shape[0] * own_ref.shape[1])
     tile = 640
+
+    @pl.when(core_ref[0] == 0)
+    def _():
+        place(beside_ref, rows, out_ref)
+
+    @pl.when(core_ref[0] != 0)
+    def _():
+        place(own_ref, rows, out_ref)
+
     lead = columns_ref[:, 0:1]
     pull = columns_ref[:, 1:2]
     total = jnp.zeros(values_ref.shape, F32)
@@ -155,14 +180,13 @@
         out_shape=(
             shape((tokens, width), BF16),
             shape((tokens, width), BF16),
-            shape((width, head), BF16),
             shape((tokens, head), BF16),
             shape((tokens, 128), F32),
             shape((LIST_DEVICES, 8, 128), F32),
         ),
         in_specs=[pl.BlockSpec(memory_space=pltpu.SMEM)] + [vmem] * 9,
-        out_specs=(vmem,) * 6,
-        scratch_shapes=[pltpu.VMEM((width, head), BF16)],
+        out_specs=(vmem,) * 5,
+        scratch_shapes=[pltpu.VMEM((width, head), BF16), pltpu.VMEM((width, head), BF16)],
         compiler_params=pltpu.CompilerParams(vmem_limit_bytes=VMEM_LIMIT),
         cost_estimate=pl.CostEstimate(
             flops=4 * tokens * width * head, bytes_accessed=12 * width * tokens, transcendentals=tokens
@@ -171,7 +195,7 @@
     )(core, hidden, root, own, beside, gain, scale, weighted, value_scale, segment)
 
 
-def run_backward(resid, out_full, columns, scale, weighted, value_scale):
+def run_backward(core, resid, own, beside, columns, scale, weighted, value_scale):
     tokens, width = resid.shape
     head = value_scale.shape[1]
     vmem = pl.BlockSpec(memory_space=pltpu.VMEM)
@@ -181,14 +205,15 @@
             jax.ShapeDtypeStruct((tokens, width), BF16),
             jax.ShapeDtypeStruct((tokens, head), F32),
         ),
-        in_specs=[vmem] * 6,
+        in_specs=[pl.BlockSpec(memory_space=pltpu.SMEM)] + [vmem] * 7,
         out_specs=(vmem,) * 2,
+        scratch_shapes=[pltpu.VMEM((width, head), BF16)],
         compiler_params=pltpu.CompilerParams(vmem_limit_bytes=VMEM_LIMIT),
         cost_estimate=pl.CostEstimate(
             flops=2 * tokens * width * head, bytes_accessed=8 * width * tokens, transcendentals=0
         ),
         name="backward",
-    )(resid, out_full, columns, scale, weighted, value_scale)
+    )(core, resid, own, beside, columns, scale, weighted, value_scale)
 
 
 def run_term(pick, normed, unit, values, half, factor, dtype):
@@ -234,7 +259,6 @@
 ):
     rows, head_size = value_codes.shape
     core = lax.axis_index("c")
-    z_half = lax.axis_index("zh")
     first = core == 0
     tokens = hidden[0]
     width = tokens.shape[1]
@@ -249,19 +273,18 @@
         vectors = jnp.pad(vectors, ((0, 6), (0, head_size - rows)))
         mine = jnp.concatenate([jnp.where(first, value_codes, output_codes), vectors], axis=0)
         other = lax.ppermute(mine, Z, half_partner())
-        low = jnp.where(z_half == 0, mine, other)
-        high = jnp.where(z_half == 0, other, mine)
-        block = jnp.concatenate([low[:rows], high[:rows], low[rows : rows + 2], high[rows : rows + 6]], axis=0)
-        spread = jnp.broadcast_to(block, (32,) + block.shape)
-        own = lax.all_to_all(spread, YX, 0, 0)
+        block = jnp.where(lax.axis_index("zh") == lax.axis_index("zb"), mine, other)
+        column = lax.all_to_all(jnp.broadcast_to(block, (8,) + block.shape), Y, 0, 0)
+        spread = jnp.broadcast_to(column, (8,) + column.shape)
+        own = lax.all_to_all(spread, XB, 0, 0)
         tokens32 = tokens.astype(F32)
         root = jnp.sqrt(jnp.mean(tokens32 * tokens32, axis=-1, keepdims=True) + EPSILON)
         own, root = lax.optimization_barrier((own, root))
         beside = lax.ppermute(own, "c", SWAP)
 
         def vector(block, which):
-            parts = block[:, 2 * rows : 2 * rows + 4, :rows].reshape(32, 2, 2, rows)
-            return parts[:, :, which].reshape(1, width).astype(F32)
+            parts = block[:, :, rows + which, :rows]
+            return jnp.swapaxes(parts, 0, 1).reshape(1, width).astype(F32)
 
         gain32 = jnp.where(first, vector(own, 0), vector(beside, 0))
         scale32 = jnp.where(first, vector(own, 1), vector(beside, 1))
@@ -271,13 +294,13 @@
 
     value_row = value_scale[None, :]
     pick = core.astype(jnp.int32)[None]
-    normed, resid, out_full, value_half, columns, stats = run_forward(
+    normed, resid, value_half, columns, stats = run_forward(
         pick, tokens, root, own, beside, gain32, scale32, weighted, value_row, seg_local
     )
     with jax.named_scope("stats"):
         arrived = lax.all_to_all(stats, ("yl", "x", "zh"), 0, 0)
 
-    unit, values = run_backward(resid, out_full, columns, scale32, weighted, value_row)
+    unit, values = run_backward(pick, resid, own, beside, columns, scale32, weighted, value_row)
 
     with jax.named_scope("factor"):
         stats = jnp.sum(arrived, axis=0)
@@ -300,23 +323,25 @@
         loss_hi = own_loss.astype(BF16)
         loss_lo = (own_loss - loss_hi.astype(F32)).astype(BF16)
         loss_row = jnp.pad(jnp.stack([loss_hi, loss_lo])[None, :], ((0, 7), (0, head_size - 2)))
-        sent = jnp.concatenate(
-            [both.reshape(32, 2 * rows, head_size), jnp.broadcast_to(loss_row, (32, 8, head_size))],
-            axis=1,
-        )
-        came = lax.all_to_all(sent, YX, 0, 0)
-        part = jnp.sum(came[:, : 2 * rows].astype(F32), axis=0)
-        losses = came.reshape(4, 8, 2 * rows + 8, head_size)[:, 0, 2 * rows, :2]
+        half = rows // 2
+        sent = both.reshape(8, 4, 2, 2, half, head_size).transpose(1, 3, 0, 2, 4, 5)
+        came = lax.all_to_all(sent.reshape(8, 8 * rows, head_size), XB, 0, 0)
+        part = jnp.sum(came.astype(F32), axis=0).astype(BF16).reshape(8, rows, head_size)
+        part = jnp.concatenate([part, jnp.broadcast_to(loss_row, (8, 8, head_size))], axis=1)
+        came = lax.all_to_all(part, Y, 0, 0)
+        losses = came.reshape(4, 2, rows + 8, head_size)[:, 0, rows, :2]
         list_loss = jnp.sum(losses.astype(F32), axis=-1)
-        part = part.astype(BF16).reshape(2, 1, rows, head_size)
-        part = jnp.broadcast_to(part, (2, 6, rows, head_size)).reshape(12, rows, head_size)
-        total = jnp.sum(lax.all_to_all(part, Z, 0, 0).astype(F32), axis=0)
+        part = jnp.sum(came[:, :rows].astype(F32), axis=0).astype(BF16)
+        part = part.reshape(2, 1, half, head_size)
+        part = jnp.broadcast_to(part, (2, 6, half, head_size)).reshape(12, half, head_size)
+        came = lax.all_to_all(part, Z, 0, 0).astype(F32)
+        total = jnp.sum(came.reshape(6, 2, half, head_size), axis=0).reshape(rows, head_size)
         pair = lax.all_gather(total, "c")
     return (pair[0], pair[1], list_loss[None, :])
 
 
 def solution(mesh):
-    grid = Mesh(mesh.devices.reshape(4, 2, 4, 2, 6, 2), WIDE + NARROW)
+    grid = Mesh(mesh.devices.reshape(4, 2, 4, 2, 3, 2, 2), WIDE + NARROW)
     in_specs = (
         P(NARROW, WIDE, None),
         P(NARROW, WIDE),

time: 183 us -> 166 us (0.907)
  blocking collectives: 43.3 us -> 32.2 us
  starting transfers between devices: 50.9 us -> 47.1 us
  waiting for transfers between devices: 51.8 us -> 49.8 us
  local copies, waits for them, and re-layouts: 7.46 us -> 9.45 us
    ppermute x1, starting transfers between devices: 15.1 us -> 0.66 us  [shards(): other = lax.ppermute(mine, Z, half_partner())]
    all_to_all x2 -> x3, starting transfers between devices: 16.2 us -> 29.8 us  [the longest x1 19.8 us: shards(): own = lax.all_to_all(spread, XB, 0, 0)]
    all_to_all x1 -> x2, blocking collectives: 39.9 us -> 27.8 us  [the longest x1 15.9 us: shards(): lax.all_to_all(jnp.broadcast_to(block, (8,) + block.shape), Y, 0, 0)]
    all_to_all x1, starting transfers between devices: 9.26 us -> 6.32 us  [shards(): arrived = lax.all_to_all(stats, ('yl', 'x', 'zh'), 0, 0)]
    all_to_all x2 -> x3, waiting for transfers between devices: 43.3 us -> 41.1 us  [the longest x1 16.8 us: shards(): came = lax.all_to_all(sent.reshape(8, 8 * rows, head_size), XB, 0, 0)]
    unnamed x14 -> x15, local copies, waits for them, and re-layouts: 3.93 us -> 4.89 us
  transfers between devices with their start and end apart: 6 -> 7, of which waited for: 5 -> 5; matrix products, arithmetic and copies ran while one was open for 3% -> 3% of each run, Pallas kernels for 4% -> 4%
where the time goes in v4:
time: 166 us; the launch traced here: 165 us
  waiting for transfers between devices  49.8 us (30%)
  starting transfers between devices  47.1 us (28%)
  blocking collectives  32.2 us (19%)
  Pallas kernels  16.2 us (10%)
  local copies, waits for them, and re-layouts  9.45 us (6%)
  other arithmetic  7.05 us (4%)
  between operations  3.63 us (2%)
    all_to_all x1, starting transfers between devices, shards(): own = lax.all_to_all(spread, XB, 0, 0)  19.8 us
    all_to_all x1, waiting for transfers between devices, shards(): came = lax.all_to_all(sent.reshape(8, 8 * rows, head_size), XB, 0, 0)  16.8 us
    all_to_all x1, blocking collectives, shards(): lax.all_to_all(jnp.broadcast_to(block, (8,) + block.shape), Y, 0, 0)  15.9 us
    all_to_all x1, waiting for transfers between devices, shards(): own = lax.all_to_all(spread, XB, 0, 0)  14.5 us
    all_to_all x1, blocking collectives, shards(): came = lax.all_to_all(part, Y, 0, 0)  11.9 us
    all_to_all x1, waiting for transfers between devices, shards(): came = lax.all_to_all(part, Z, 0, 0).astype(F32)  9.78 us
    pallas_call x2, Pallas kernels, run_term(): pl.pallas_call(term_kernel, out_shape=jax.ShapeDtypeStruct((width, head),...  6.84 us
    all_to_all x1, starting transfers between devices, shards(): came = lax.all_to_all(part, Z, 0, 0).astype(F32)  6.41 us
  transfers between devices with their start and end apart: 7, of which 5 were waited for; matrix products, arithmetic and copies ran while one was open for 3% of the time, Pallas kernels for 4%

profile of v4, /device:TPU:1, one launch (start us, length us, event | category | flops | bytes accessed | tf_op | source)
XLA Modules:
  0.0 165.3 jit_solution(5063976123527010251)
XLA Ops:
  0.6 0.7 broadcast_select_fusion.5
  1.4 0.7 broadcast_select_fusion.6
  2.1 0.7 collective-permute-start
  2.8 0.0 collective-permute-done
  2.9 15.9 %all_to_all.30 = bf16[8,88,128]{2,1,0:T(8,128)(2,1)S(1)} all-to-all(bf16[8,88,128]{2,1,0:T(8,128)(2,1)S(1)} %broadcast_in_dim.35), channel_id=1, replica_groups=mesh['yh'=4,'yl'=2,'x'=4,'zh'=2,'za'=3,'zb'=2,'c'=2] {'yh','yl'}, dimensions={0} | all-to-all | bytes 360448 | tf_op jit(solution)/shard_map/gather/all_to_all | solution.py:277
  18.8 1.3 broadcast_in_dim.36
  20.1 19.8 %all-to-all-start.1 = ((bf16[8,8,88,128]{3,2,1,0:T(8,128)(2,1)}), bf16[8,8,88,128]{3,2,1,0:T(8,128)(2,1)S(1)}, u32[]{:S(2)}, u32[]{:S(2)}) async-start(bf16[8,8,88,128]{3,2,1,0:T(8,128)(2,1)} %broadcast_in_dim.36), calls=%async_computation.1 | async-start | bytes 2883584 | tf_op jit(solution)/shard_map/gather/all_to_all | solution.py:279
  39.9 0.0 copy-start.5
  39.9 0.0 copy-start.4
  39.9 2.4 %multiply_reduce_fusion = f32[256]{0:T(256)S(1)} fusion(bf16[1,256,5120]{2,1,0:T(8,128)(2,1)} %param.10), kind=kLoop, calls=%fused_computation | loop fusion | flops 3931904 | bytes 2622464 | tf_op jit(solution)/shard_map/gather/reduce_sum | solution.py:281
  42.3 14.5 %all-to-all-done.1.own_ref = bf16[8,8,88,128]{3,2,1,0:T(8,128)(2,1)S(1)} async-done(((bf16[8,8,88,128]{3,2,1,0:T(8,128)(2,1)}), bf16[8,8,88,128]{3,2,1,0:T(8,128)(2,1)S(1)}, u32[]{:S(2)}, u32[]{:S(2)}) %all-to-all-start.1) | async-done | bytes 1441824 | tf_op jit(solution)/shard_map/gather/all_to_all | solution.py:279
  56.8 5.9 %collective-permute-start.1 = (bf16[8,8,88,128]{3,2,1,0:T(8,128)(2,1)S(1)}, bf16[8,8,88,128]{3,2,1,0:T(8,128)(2,1)S(1)}, u32[]{:S(2)}, u32[]{:S(2)}) collective-permute-start(bf16[8,8,88,128]{3,2,1,0:T(8,128)(2,1)S(1)} %all-to-all-done.1.own_ref), channel_id=1, source_target_pairs={{0,1},{1,0},{2,3},{3,2},{4,5},{5,4},{6,7},{7,6},{8,9},{9,8},{10,11... | collective-permute-start | bytes 4325384 | tf_op jit(solution)/shard_map/gather/ppermute | solution.py:283
  62.7 0.0 copy-done.5
  62.7 0.1 copy.52.segment_ref
  62.8 0.1 copy.51.root_ref
  63.0 2.5 %collective-permute-done.1.beside_ref = bf16[8,8,88,128]{3,2,1,0:T(8,128)(2,1)S(1)} collective-permute-done((bf16[8,8,88,128]{3,2,1,0:T(8,128)(2,1)S(1)}, bf16[8,8,88,128]{3,2,1,0:T(8,128)(2,1)S(1)}, u32[]{:S(2)}, u32[]{:S(2)}) %collective-permute-start.1) | collective-permute-done | bytes 1441824 | tf_op jit(solution)/shard_map/gather/ppermute | solution.py:283
  65.5 0.1 fusion.1
  65.6 0.1 select_n.96.gain_ref
  65.8 0.1 select_n.100.scale_ref
  65.9 0.1 mul.26.weighted_ref
  66.0 0.0 copy-done.4
  66.0 0.0 copy-start.6
  66.0 6.1 %forward.1 = (bf16[256,5120]{1,0:T(8,128)(2,1)S(1)}, bf16[256,5120]{1,0:T(8,128)(2,1)}, bf16[256,128]{1,0:T(8,128)(2,1)S(1)}, f32[256,128]{1,0:T(8,128)S(1)}, f32[16,8,128]{2,1,0:T(8,128)}) custom-call(s32[1]{0:T(128)} %bitcast.core_ref.pick_ref, bf16[256,5120]{1,0:T(8,128)(2,1)} %bitcast.62, f32[256,1]{1,0:T(8,128)S(1)} %copy.51.root_ref, ...), custom_call_target="tpu_custom_call" | custom-call | flops 671088640 | bytes 15728640 | tf_op jit(solution)/shard_map/forward/pallas_call | solution.py:178
  72.1 0.0 copy-start
  72.1 1.5 copy-done
  73.6 6.3 %all-to-all-start.2 = ((f32[16,8,128]{2,1,0:T(8,128)}), f32[16,8,128]{2,1,0:T(8,128)S(1)}, u32[]{:S(2)}, u32[]{:S(2)}) async-start(f32[16,8,128]{2,1,0:T(8,128)} %get-tuple-element.20), calls=%async_computation.2 | async-start | bytes 131072 | tf_op jit(solution)/shard_map/stats/all_to_all | solution.py:301
  79.9 0.0 copy-done.6
  79.9 0.6 exponential_reduce_fusion
  81.2 3.2 %backward.1 = (bf16[256,5120]{1,0:T(8,128)(2,1)S(1)}, f32[256,128]{1,0:T(8,128)S(1)}) custom-call(s32[1]{0:T(128)} %bitcast.core_ref.pick_ref, bf16[256,5120]{1,0:T(8,128)(2,1)} %get-tuple-element.15.resid_ref, bf16[8,8,88,128]{3,2,1,0:T(8,128)(2,1)S(1)} %all-to-all-done.1.own_ref, bf16[8,8,88,128]{3,2,1,0:T(8,128)(2,1)S(1)} %collective-permute-done.1.beside_ref, ...), custom_call_target="tpu_custom_call" | custom-call | flops 335544320 | bytes 10485760 | tf_op jit(solution)/shard_map/backward/pallas_call | solution.py:202
  84.5 0.0 copy-start.3
  84.5 1.5 copy-done.3
  86.0 6.1 %all-to-all-done.2 = f32[16,8,128]{2,1,0:T(8,128)S(1)} async-done(((f32[16,8,128]{2,1,0:T(8,128)}), f32[16,8,128]{2,1,0:T(8,128)S(1)}, u32[]{:S(2)}, u32[]{:S(2)}) %all-to-all-start.2) | async-done | bytes 65568 | tf_op jit(solution)/shard_map/stats/all_to_all | solution.py:301
  92.2 0.6 exponential_reduce_fusion.1
  93.5 0.1 select_reduce_fusion
  93.6 0.1 copy.53.factor_ref
  93.7 0.0 copy-start.1
  93.8 1.7 %copy-done.1 = bf16[256,5120]{1,0:T(8,128)(2,1)S(1)} copy-done((bf16[256,5120]{1,0:T(8,128)(2,1)S(1)}, bf16[256,5120]{1,0:T(8,128)(2,1)}, u32[]{:S(2)}) %copy-start.1) | copy-done | bytes 2621464
  95.5 0.0 copy-start.2
  95.5 3.0 %term.3 = bf16[5120,128]{1,0:T(8,128)(2,1)S(1)} custom-call(s32[1]{0:T(128)S(6)} %sub.45.pick_ref, bf16[256,5120]{1,0:T(8,128)(2,1)S(1)} %copy-done.1, bf16[256,5120]{1,0:T(8,128)(2,1)} %copy-done.3, f32[256,128]{1,0:T(8,128)S(1)} %get-tuple-element.18.values_ref, bf16[256,128]{1,0:T(8,128)(2,1)S(1)} %get-tuple-element.19.half_ref, f32[256,1]{1,0:T(8,128)S(1)} %copy.53.factor_ref), custom_call_target="tpu_custom_call" | custom-call | flops 335544320 | bytes 5242880 | tf_op jit(solution)/shard_map/term/pallas_call | solution.py:224
  98.5 4.4 %collective-permute-start.2 = (bf16[5120,128]{1,0:T(8,128)(2,1)S(1)}, bf16[5120,128]{1,0:T(8,128)(2,1)S(1)}, u32[]{:S(2)}, u32[]{:S(2)}) collective-permute-start(bf16[5120,128]{1,0:T(8,128)(2,1)S(1)} %term.3), channel_id=1, source_target_pairs={{0,1},{1,0},{2,3},{3,2},{4,5},{5,4},{6,7},{7,6},{8,9},{9,8},{10,11... | collective-permute-start | bytes 3932168 | tf_op jit(solution)/shard_map/reduce/ppermute | solution.py:320
  102.9 0.0 copy-done.2
  102.9 3.8 %term.2 = f32[5120,128]{1,0:T(8,128)S(1)} custom-call(s32[1]{0:T(128)} %bitcast.core_ref.pick_ref, bf16[256,5120]{1,0:T(8,128)(2,1)S(1)} %copy-done.2, bf16[256,5120]{1,0:T(8,128)(2,1)} %copy-done.3, f32[256,128]{1,0:T(8,128)S(1)} %get-tuple-element.18.values_ref, bf16[256,128]{1,0:T(8,128)(2,1)S(1)} %get-tuple-element.19.half_ref, f32[256,1]{1,0:T(8,128)S(1)} %copy.53.factor_ref), custom_call_target="tpu_custom_call" | custom-call | flops 335544320 | bytes 5242880 | tf_op jit(solution)/shard_map/reduce/term/pallas_call | solution.py:224
  106.7 0.0 collective-permute-done.2
  106.7 0.3 add_convert_fusion
  107.0 1.2 copy.55
  108.2 3.6 %all-to-all-start.3 = ((bf16[8,640,128]{2,1,0:T(8,128)(2,1)}), bf16[8,640,128]{2,1,0:T(8,128)(2,1)S(1)}, u32[]{:S(2)}, u32[]{:S(2)}) async-start(bf16[8,640,128]{2,1,0:T(8,128)(2,1)} %bitcast.21), calls=%async_computation.3 | async-start | bytes 2621440 | tf_op jit(solution)/shard_map/reduce/all_to_all | solution.py:328
  111.8 0.6 fusion.4
  113.7 0.1 maximum_bitcast_fusion
  113.8 16.8 %all-to-all-done.3 = bf16[8,640,128]{2,1,0:T(8,128)(2,1)S(1)} async-done(((bf16[8,640,128]{2,1,0:T(8,128)(2,1)}), bf16[8,640,128]{2,1,0:T(8,128)(2,1)S(1)}, u32[]{:S(2)}, u32[]{:S(2)}) %all-to-all-start.3) | async-done | bytes 1310752 | tf_op jit(solution)/shard_map/reduce/all_to_all | solution.py:328
  130.6 0.2 reduce_sum.101
  130.8 11.9 %all_to_all.31 = bf16[8,88,128]{2,1,0:T(8,128)(2,1)S(1)} all-to-all(bf16[8,88,128]{2,1,0:T(8,128)(2,1)S(1)} %pad_maximum_fusion), channel_id=1, replica_groups=mesh['yh'=4,'yl'=2,'x'=4,'zh'=2,'za'=3,'zb'=2,'c'=2] {'yh','yl'}, dimensions={0} | all-to-all | bytes 360448 | tf_op jit(solution)/shard_map/reduce/all_to_all | solution.py:331
  142.8 0.7 broadcast_in_dim.42
  143.4 6.4 %all-to-all-start.5 = ((bf16[12,40,128]{2,1,0:T(8,128)(2,1)}), bf16[12,40,128]{2,1,0:T(8,128)(2,1)S(1)}, u32[]{:S(2)}, u32[]{:S(2)}) async-start(bf16[12,40,128]{2,1,0:T(8,128)(2,1)} %bitcast.29), calls=%async_computation.5 | async-start | bytes 245760 | tf_op jit(solution)/shard_map/reduce/all_to_all | solution.py:337
  149.9 0.1 copy.57
  150.0 0.5 convert_reduce_fusion.1
  150.5 9.8 %all-to-all-done.5 = bf16[12,40,128]{2,1,0:T(8,128)(2,1)S(1)} async-done(((bf16[12,40,128]{2,1,0:T(8,128)(2,1)}), bf16[12,40,128]{2,1,0:T(8,128)(2,1)S(1)}, u32[]{:S(2)}, u32[]{:S(2)}) %all-to-all-start.5) | async-done | bytes 122912 | tf_op jit(solution)/shard_map/reduce/all_to_all | solution.py:337
  160.3 4.4 %all_gather.3 = f32[2,80,128]{2,1,0:T(8,128)S(1)} all-gather(f32[1,80,128]{2,1,0:T(8,128)S(1)} %bitcast.67), channel_id=1, replica_groups=mesh['yh'=4,'yl'=2,'x'=4,'zh'=2,'za'=3,'zb'=2,'c'=2] {'c'}, dimensions={0}, use_global_device_ids=true | all-gather | bytes 122880 | tf_op jit(solution)/shard_map/reduce/all_gather | solution.py:339
  164.7 0.6 slice_bitcast_fusion
  (15 shorter events, 0.2 us)
Async XLA Ops:
  2.1 0.7 collective-permute-start
  20.1 36.7 %all-to-all-start.1 = ((bf16[8,8,88,128]{3,2,1,0:T(8,128)(2,1)}), bf16[8,8,88,128]{3,2,1,0:T(8,128)(2,1)S(1)}, u32[]{:S(2)}, u32[]{:S(2)}) async-start(bf16[8,8,88,128]{3,2,1,0:T(8,128)(2,1)} %broadcast_in_dim.36), calls=%async_computation.1 | async-start | bytes 2883584 | tf_op jit(solution)/shard_map/gather/all_to_all | solution.py:279
  39.9 22.8 %copy-start.5 = (s32[1,256]{1,0:T(1,128)S(1)}, s32[1,256]{1,0:T(1,128)}, u32[]{:S(2)}) copy-start(s32[1,256]{1,0:T(1,128)} %param.11) | copy-start | bytes 3076
  39.9 26.1 %copy-start.4 = (f32[128]{0:T(128)S(1)}, f32[128]{0:T(128)}, u32[]{:S(2)}) copy-start(f32[128]{0:T(128)} %param.14) | copy-start | bytes 1540
  56.8 8.8 %collective-permute-start.1 = (bf16[8,8,88,128]{3,2,1,0:T(8,128)(2,1)S(1)}, bf16[8,8,88,128]{3,2,1,0:T(8,128)(2,1)S(1)}, u32[]{:S(2)}, u32[]{:S(2)}) collective-permute-start(bf16[8,8,88,128]{3,2,1,0:T(8,128)(2,1)S(1)} %all-to-all-done.1.own_ref), channel_id=1, source_target_pairs={{0,1},{1,0},{2,3},{3,2},{4,5},{5,4},{6,7},{7,6},{8,9},{9,8},{10,11... | collective-permute-start | bytes 4325384 | tf_op jit(solution)/shard_map/gather/ppermute | solution.py:283
  66.0 13.9 %copy-start.6 = (s32[1,4,20]{2,1,0:T(4,128)S(1)}, s32[1,4,20]{2,1,0:T(4,128)}, u32[]{:S(2)}) copy-start(s32[1,4,20]{2,1,0:T(4,128)} %param.12) | copy-start | bytes 964
  72.1 1.5 copy-start
  73.6 18.6 %all-to-all-start.2 = ((f32[16,8,128]{2,1,0:T(8,128)}), f32[16,8,128]{2,1,0:T(8,128)S(1)}, u32[]{:S(2)}, u32[]{:S(2)}) async-start(f32[16,8,128]{2,1,0:T(8,128)} %get-tuple-element.20), calls=%async_computation.2 | async-start | bytes 131072 | tf_op jit(solution)/shard_map/stats/all_to_all | solution.py:301
  84.5 1.5 copy-start.3
  93.7 1.7 %copy-start.1 = (bf16[256,5120]{1,0:T(8,128)(2,1)S(1)}, bf16[256,5120]{1,0:T(8,128)(2,1)}, u32[]{:S(2)}) copy-start(bf16[256,5120]{1,0:T(8,128)(2,1)} %copy-done) | copy-start | bytes 7864324
  95.5 7.4 %copy-start.2 = (bf16[256,5120]{1,0:T(8,128)(2,1)S(1)}, bf16[256,5120]{1,0:T(8,128)(2,1)}, u32[]{:S(2)}) copy-start(bf16[256,5120]{1,0:T(8,128)(2,1)} %copy-done) | copy-start | bytes 7864324
  98.5 8.2 %collective-permute-start.2 = (bf16[5120,128]{1,0:T(8,128)(2,1)S(1)}, bf16[5120,128]{1,0:T(8,128)(2,1)S(1)}, u32[]{:S(2)}, u32[]{:S(2)}) collective-permute-start(bf16[5120,128]{1,0:T(8,128)(2,1)S(1)} %term.3), channel_id=1, source_target_pairs={{0,1},{1,0},{2,3},{3,2},{4,5},{5,4},{6,7},{7,6},{8,9},{9,8},{10,11... | collective-permute-start | bytes 3932168 | tf_op jit(solution)/shard_map/reduce/ppermute | solution.py:320
  108.2 22.4 %all-to-all-start.3 = ((bf16[8,640,128]{2,1,0:T(8,128)(2,1)}), bf16[8,640,128]{2,1,0:T(8,128)(2,1)S(1)}, u32[]{:S(2)}, u32[]{:S(2)}) async-start(bf16[8,640,128]{2,1,0:T(8,128)(2,1)} %bitcast.21), calls=%async_computation.3 | async-start | bytes 2621440 | tf_op jit(solution)/shard_map/reduce/all_to_all | solution.py:328
  143.4 16.8 %all-to-all-start.5 = ((bf16[12,40,128]{2,1,0:T(8,128)(2,1)}), bf16[12,40,128]{2,1,0:T(8,128)(2,1)S(1)}, u32[]{:S(2)}, u32[]{:S(2)}) async-start(bf16[12,40,128]{2,1,0:T(8,128)(2,1)} %bitcast.29), calls=%async_computation.5 | async-start | bytes 245760 | tf_op jit(solution)/shard_map/reduce/all_to_all | solution.py:337

commit v5 on v4

--- a/solution.py
+++ b/solution.py
@@ -15,6 +15,7 @@
 SWAP = [(0, 1), (1, 0)]
 LIST_DEVICES = 16
 VMEM_LIMIT = 48 * 1024 * 1024
+TERM_LIMIT = 16 * 1024 * 1024
 F32 = jnp.float32
 BF16 = jnp.bfloat16
 
@@ -53,13 +54,16 @@
     weighted_ref,
     value_scale_ref,
     segment_ref,
-    normed_ref,
-    resid_ref,
+    normed_out,
+    resid_out,
     half_ref,
     columns_ref,
     stats_ref,
     value_ref,
     out_ref,
+    normed_ref,
+    resid_ref,
+    sems,
 ):
     tokens, width = hidden_ref.shape
     rows = width // (own_ref.shape[0] * own_ref.shape[1])
@@ -75,6 +79,7 @@
         place(beside_ref, rows, value_ref)
         place(own_ref, rows, out_ref)
 
+    copies = []
     inverse = 1.0 / root_ref[...]
     mixed = jnp.zeros((tokens, value_ref.shape[1]), F32)
     for j in range(width // tile):
@@ -82,6 +87,8 @@
         scaled = hidden_ref[:, span].astype(F32) * inverse
         normed = (scaled * gain_ref[:, span]).astype(BF16)
         normed_ref[:, span] = normed
+        copies.append(pltpu.make_async_copy(normed_ref.at[:, span], normed_out.at[:, span], sems.at[0, j]))
+        copies[-1].start()
         mixed = mixed + jnp.dot(normed, value_ref[span, :], preferred_element_type=F32)
     value_half = (mixed * value_scale_ref[...]).astype(BF16)
     half_ref[...] = value_half
@@ -94,6 +101,8 @@
         )
         residual = (hidden_ref[:, span].astype(F32) + branch * scale_ref[:, span]).astype(BF16)
         resid_ref[:, span] = residual
+        copies.append(pltpu.make_async_copy(resid_ref.at[:, span], resid_out.at[:, span], sems.at[1, j]))
+        copies[-1].start()
         resid32 = residual.astype(F32)
         squares = squares + lane_fold(resid32 * resid32)
         scores = scores + lane_fold(resid32 * weighted_ref[:, span])
@@ -112,6 +121,8 @@
     packed = jnp.where(row == 0, sums, counts)
     for k in range(stats_ref.shape[0]):
         stats_ref[k] = packed
+    for copy in copies:
+        copy.wait()
 
 
 def backward_kernel(
@@ -123,9 +134,11 @@
     scale_ref,
     weighted_ref,
     value_scale_ref,
-    unit_ref,
+    unit_out,
     values_ref,
     out_ref,
+    unit_ref,
+    sems,
 ):
     tokens, width = resid_ref.shape
     rows = width // (own_ref.shape[0] * own_ref.shape[1])
@@ -139,6 +152,7 @@
     def _():
         place(own_ref, rows, out_ref)
 
+    copies = []
     lead = columns_ref[:, 0:1]
     pull = columns_ref[:, 1:2]
     total = jnp.zeros(values_ref.shape, F32)
@@ -147,8 +161,12 @@
         slope = lead * weighted_ref[:, span] - pull * resid_ref[:, span].astype(F32)
         unit = (slope * scale_ref[:, span]).astype(BF16)
         unit_ref[:, span] = unit
+        copies.append(pltpu.make_async_copy(unit_ref.at[:, span], unit_out.at[:, span], sems.at[j]))
+        copies[-1].start()
         total = total + jnp.dot(unit, out_ref[span, :], preferred_element_type=F32)
     values_ref[...] = total * value_scale_ref[...]
+    for copy in copies:
+        copy.wait()
 
 
 def term_kernel(pick_ref, normed_ref, unit_ref, values_ref, half_ref, factor_ref, term_ref, small_ref):
@@ -175,6 +193,7 @@
     head = value_scale.shape[1]
     shape = jax.ShapeDtypeStruct
     vmem = pl.BlockSpec(memory_space=pltpu.VMEM)
+    far = pl.BlockSpec(memory_space=pltpu.HBM)
     return pl.pallas_call(
         forward_kernel,
         out_shape=(
@@ -185,8 +204,14 @@
             shape((LIST_DEVICES, 8, 128), F32),
         ),
         in_specs=[pl.BlockSpec(memory_space=pltpu.SMEM)] + [vmem] * 9,
-        out_specs=(vmem,) * 5,
-        scratch_shapes=[pltpu.VMEM((width, head), BF16), pltpu.VMEM((width, head), BF16)],
+        out_specs=(far, far, vmem, vmem, vmem),
+        scratch_shapes=[
+            pltpu.VMEM((width, head), BF16),
+            pltpu.VMEM((width, head), BF16),
+            pltpu.VMEM((tokens, width), BF16),
+            pltpu.VMEM((tokens, width), BF16),
+            pltpu.SemaphoreType.DMA((2, width // 640)),
+        ],
         compiler_params=pltpu.CompilerParams(vmem_limit_bytes=VMEM_LIMIT),
         cost_estimate=pl.CostEstimate(
             flops=4 * tokens * width * head, bytes_accessed=12 * width * tokens, transcendentals=tokens
@@ -199,6 +224,7 @@
     tokens, width = resid.shape
     head = value_scale.shape[1]
     vmem = pl.BlockSpec(memory_space=pltpu.VMEM)
+    far = pl.BlockSpec(memory_space=pltpu.HBM)
     return pl.pallas_call(
         backward_kernel,
         out_shape=(
@@ -206,8 +232,12 @@
             jax.ShapeDtypeStruct((tokens, head), F32),
         ),
         in_specs=[pl.BlockSpec(memory_space=pltpu.SMEM)] + [vmem] * 7,
-        out_specs=(vmem,) * 2,
-        scratch_shapes=[pltpu.VMEM((width, head), BF16)],
+        out_specs=(far, vmem),
+        scratch_shapes=[
+            pltpu.VMEM((width, head), BF16),
+            pltpu.VMEM((tokens, width), BF16),
+            pltpu.SemaphoreType.DMA((width // 640,)),
+        ],
         compiler_params=pltpu.CompilerParams(vmem_limit_bytes=VMEM_LIMIT),
         cost_estimate=pl.CostEstimate(
             flops=2 * tokens * width * head, bytes_accessed=8 * width * tokens, transcendentals=0
@@ -219,7 +249,7 @@
 def run_term(pick, normed, unit, values, half, factor, dtype):
     tokens, width = normed.shape
     head = values.shape[1]
-    tile = 1280
+    tile = width // 2
     whole = lambda j, pick: (0, 0)
     return pl.pallas_call(
         term_kernel,
@@ -237,7 +267,7 @@
             out_specs=pl.BlockSpec((tile, head), lambda j, pick: (j, 0)),
             scratch_shapes=[pltpu.VMEM((head, tokens), BF16)],
         ),
-        compiler_params=pltpu.CompilerParams(vmem_limit_bytes=VMEM_LIMIT),
+        compiler_params=pltpu.CompilerParams(vmem_limit_bytes=TERM_LIMIT),
         cost_estimate=pl.CostEstimate(
             flops=2 * tokens * width * head, bytes_accessed=4 * width * tokens, transcendentals=0
         ),
@@ -279,7 +309,6 @@
         own = lax.all_to_all(spread, XB, 0, 0)
         tokens32 = tokens.astype(F32)
         root = jnp.sqrt(jnp.mean(tokens32 * tokens32, axis=-1, keepdims=True) + EPSILON)
-        own, root = lax.optimization_barrier((own, root))
         beside = lax.ppermute(own, "c", SWAP)
 
         def vector(block, which):
@@ -322,6 +351,7 @@
         both = (keep + got.astype(F32)).astype(BF16)
         loss_hi = own_loss.astype(BF16)
         loss_lo = (own_loss - loss_hi.astype(F32)).astype(BF16)
+        both, loss_hi, loss_lo = lax.optimization_barrier((both, loss_hi, loss_lo))
         loss_row = jnp.pad(jnp.stack([loss_hi, loss_lo])[None, :], ((0, 7), (0, head_size - 2)))
         half = rows // 2
         sent = both.reshape(8, 4, 2, 2, half, head_size).transpose(1, 3, 0, 2, 4, 5)
@@ -332,6 +362,7 @@
         losses = came.reshape(4, 2, rows + 8, head_size)[:, 0, rows, :2]
         list_loss = jnp.sum(losses.astype(F32), axis=-1)
         part = jnp.sum(came[:, :rows].astype(F32), axis=0).astype(BF16)
+        part, list_loss = lax.optimization_barrier((part, list_loss))
         part = part.reshape(2, 1, half, head_size)
         part = jnp.broadcast_to(part, (2, 6, half, head_size)).reshape(12, half, head_size)
         came = lax.all_to_all(part, Z, 0, 0).astype(F32)

time: 166 us -> 170 us (1.024)
  blocking collectives: 32.2 us -> 85.3 us
  starting transfers between devices: 47.1 us -> 20.5 us
  waiting for transfers between devices: 49.8 us -> 24.6 us
  local copies, waits for them, and re-layouts: 9.45 us -> 11.2 us
    all_to_all x0 -> x2, blocking collectives: none -> 53.3 us  [the longest x1 36.7 us: shards(): own = lax.all_to_all(spread, XB, 0, 0)]
    all_to_all x2 -> x0, starting transfers between devices: 26.2 us -> none  [the longest x1 19.8 us: shards(): own = lax.all_to_all(spread, XB, 0, 0)]
    all_to_all x2 -> x0, waiting for transfers between devices: 24.3 us -> none  [the longest x1 14.5 us: shards(): own = lax.all_to_all(spread, XB, 0, 0)]
    unnamed x15 -> x21, local copies, waits for them, and re-layouts: 4.89 us -> 8.36 us
    pallas_call x2, Pallas kernels: 6.84 us -> 3.88 us  [run_term(): pl.pallas_call(term_kernel, out_shape=jax.ShapeDtypeStruct((width, head),...]
    all_to_all x1, waiting for transfers between devices: 6.13 us -> 4.14 us  [shards(): arrived = lax.all_to_all(stats, ('yl', 'x', 'zh'), 0, 0)]
    pallas_call x1, Pallas kernels: 3.24 us -> 5.23 us  [run_backward(): pl.pallas_call(backward_kernel, out_shape=(jax.ShapeDtypeStruct((tokens,...]
    reduce_sum x1, other arithmetic: 2.35 us -> 0.6 us  [shards(): jnp.mean(tokens32 * tokens32, axis=-1, keepdims=True) + EPSILON]
  transfers between devices with their start and end apart: 7 -> 5, of which waited for: 5 -> 3; matrix products, arithmetic and copies ran while one was open for 3% -> 1% of each run, Pallas kernels for 4% -> 4%
where the time goes in v5:
time: 170 us; the launch traced here: 169 us
  blocking collectives  85.3 us (50%)
  waiting for transfers between devices  24.6 us (14%)
  starting transfers between devices  20.5 us (12%)
  Pallas kernels  16.9 us (10%)
  local copies, waits for them, and re-layouts  11.2 us (7%)
  other arithmetic  6.69 us (4%)
  between operations  3.65 us (2%)
    all_to_all x1, blocking collectives, shards(): own = lax.all_to_all(spread, XB, 0, 0)  36.7 us
    all_to_all x1, waiting for transfers between devices, shards(): came = lax.all_to_all(sent.reshape(8, 8 * rows, head_size), XB, 0, 0)  18.6 us
    all_to_all x1, blocking collectives, shards(): came = lax.all_to_all(part, Z, 0, 0).astype(F32)  16.6 us
    all_to_all x1, blocking collectives, shards(): lax.all_to_all(jnp.broadcast_to(block, (8,) + block.shape), Y, 0, 0)  15.9 us
    all_to_all x1, blocking collectives, shards(): came = lax.all_to_all(part, Y, 0, 0)  10.8 us
    unnamed x21, local copies, waits for them, and re-layouts  8.36 us
    pallas_call x1, Pallas kernels, run_forward(): pl.pallas_call(forward_kernel, out_shape=(shape((tokens, width), BF16), s...  7.75 us
    ppermute x1, starting transfers between devices, shards(): beside = lax.ppermute(own, 'c', SWAP)  6.22 us
  transfers between devices with their start and end apart: 5, of which 3 were waited for; matrix products, arithmetic and copies ran while one was open for 1% of the time, Pallas kernels for 4%

profile of v5, /device:TPU:1, one launch (start us, length us, event | category | flops | bytes accessed | tf_op | source)
XLA Modules:
  0.0 168.8 jit_solution(11583911643443234717)
XLA Ops:
  0.6 0.7 broadcast_select_fusion.5
  1.4 0.7 broadcast_select_fusion.6
  2.1 0.7 collective-permute-start
  2.8 0.0 collective-permute-done
  2.9 15.9 %all_to_all.30 = bf16[8,88,128]{2,1,0:T(8,128)(2,1)S(1)} all-to-all(bf16[8,88,128]{2,1,0:T(8,128)(2,1)S(1)} %broadcast_in_dim.35), channel_id=1, replica_groups=mesh['yh'=4,'yl'=2,'x'=4,'zh'=2,'za'=3,'zb'=2,'c'=2] {'yh','yl'}, dimensions={0} | all-to-all | bytes 360448 | tf_op jit(solution)/shard_map/gather/all_to_all | solution.py:307
  18.8 0.2 broadcast_in_dim.36
  19.0 0.0 copy-start.7
  19.0 36.7 %all_to_all.31.own_ref = bf16[8,8,88,128]{3,2,1,0:T(8,128)(2,1)S(1)} all-to-all(bf16[8,8,88,128]{3,2,1,0:T(8,128)(2,1)S(1)} %broadcast_in_dim.36), channel_id=1, replica_groups=mesh['yh'=4,'yl'=2,'x'=4,'zh'=2,'za'=3,'zb'=2,'c'=2] {'x','zb'}, dimensions={0} | all-to-all | bytes 2883584 | tf_op jit(solution)/shard_map/gather/all_to_all | solution.py:309
  55.6 0.0 copy-start.8
  55.6 0.0 copy-start.6
  55.6 6.2 %collective-permute-start.1 = (bf16[8,8,88,128]{3,2,1,0:T(8,128)(2,1)S(1)}, bf16[8,8,88,128]{3,2,1,0:T(8,128)(2,1)S(1)}, u32[]{:S(2)}, u32[]{:S(2)}) collective-permute-start(bf16[8,8,88,128]{3,2,1,0:T(8,128)(2,1)S(1)} %all_to_all.31.own_ref), channel_id=1, source_target_pairs={{0,1},{1,0},{2,3},{3,2},{4,5},{5,4},{6,7},{7,6},{8,9},{9,8},{10,11... | collective-permute-start | bytes 4325384 | tf_op jit(solution)/shard_map/gather/ppermute | solution.py:312
  61.9 0.0 copy-done.7
  61.9 0.6 multiply_reduce_fusion
  62.5 0.1 copy.51.root_ref
  62.6 0.0 copy-done.8
  62.6 0.1 copy.52.segment_ref
  62.8 1.9 %collective-permute-done.1.beside_ref = bf16[8,8,88,128]{3,2,1,0:T(8,128)(2,1)S(1)} collective-permute-done((bf16[8,8,88,128]{3,2,1,0:T(8,128)(2,1)S(1)}, bf16[8,8,88,128]{3,2,1,0:T(8,128)(2,1)S(1)}, u32[]{:S(2)}, u32[]{:S(2)}) %collective-permute-start.1) | collective-permute-done | bytes 1441824 | tf_op jit(solution)/shard_map/gather/ppermute | solution.py:312
  64.7 0.1 fusion.1
  64.8 0.1 select_n.96.gain_ref
  64.9 0.1 select_n.100.scale_ref
  65.0 0.1 mul.26.weighted_ref
  65.1 0.0 copy-done.6
  65.2 0.0 copy-start.9
  65.2 7.7 %forward.1 = (bf16[256,5120]{1,0:T(8,128)(2,1)S(1)}, bf16[256,5120]{1,0:T(8,128)(2,1)}, bf16[256,128]{1,0:T(8,128)(2,1)S(1)}, f32[256,128]{1,0:T(8,128)S(1)}, f32[16,8,128]{2,1,0:T(8,128)}) custom-call(s32[1]{0:T(128)} %bitcast.core_ref.pick_ref, bf16[256,5120]{1,0:T(8,128)(2,1)} %bitcast.62, f32[256,1]{1,0:T(8,128)S(1)} %copy.51.root_ref, ...), custom_call_target="tpu_custom_call" | custom-call | flops 671088640 | bytes 15728640 | tf_op jit(solution)/shard_map/forward/pallas_call | solution.py:197
  72.9 0.0 copy-start
  72.9 1.5 copy-done
  74.4 6.2 %all-to-all-start.2 = ((f32[16,8,128]{2,1,0:T(8,128)}), f32[16,8,128]{2,1,0:T(8,128)S(1)}, u32[]{:S(2)}, u32[]{:S(2)}) async-start(f32[16,8,128]{2,1,0:T(8,128)} %get-tuple-element.21), calls=%async_computation.2 | async-start | bytes 131072 | tf_op jit(solution)/shard_map/stats/all_to_all | solution.py:330
  80.6 0.0 copy-done.9
  80.6 0.6 exponential_reduce_fusion
  81.9 5.2 %backward.1 = (bf16[256,5120]{1,0:T(8,128)(2,1)S(1)}, f32[256,128]{1,0:T(8,128)S(1)}) custom-call(s32[1]{0:T(128)} %bitcast.core_ref.pick_ref, bf16[256,5120]{1,0:T(8,128)(2,1)} %get-tuple-element.16.resid_ref, bf16[8,8,88,128]{3,2,1,0:T(8,128)(2,1)S(1)} %all_to_all.31.own_ref, bf16[8,8,88,128]{3,2,1,0:T(8,128)(2,1)S(1)} %collective-permute-done.1.beside_ref, ...), custom_call_target="tpu_custom_call" | custom-call | flops 335544320 | bytes 10485760 | tf_op jit(solution)/shard_map/backward/pallas_call | solution.py:228
  87.1 0.0 copy-start.3
  87.2 1.5 copy-done.3
  88.7 4.1 %all-to-all-done.2 = f32[16,8,128]{2,1,0:T(8,128)S(1)} async-done(((f32[16,8,128]{2,1,0:T(8,128)}), f32[16,8,128]{2,1,0:T(8,128)S(1)}, u32[]{:S(2)}, u32[]{:S(2)}) %all-to-all-start.2) | async-done | bytes 65568 | tf_op jit(solution)/shard_map/stats/all_to_all | solution.py:330
  92.8 0.6 exponential_reduce_fusion.1
  94.2 0.1 select_reduce_fusion
  94.3 0.1 copy.53.factor_ref
  94.4 0.0 copy-start.1
  94.4 1.7 %copy-done.1 = bf16[256,5120]{1,0:T(8,128)(2,1)S(1)} copy-done((bf16[256,5120]{1,0:T(8,128)(2,1)S(1)}, bf16[256,5120]{1,0:T(8,128)(2,1)}, u32[]{:S(2)}) %copy-start.1) | copy-done | bytes 2621464
  96.2 0.0 copy-start.4
  96.2 1.7 %copy-done.4 = bf16[256,5120]{1,0:T(8,128)(2,1)S(1)} copy-done((bf16[256,5120]{1,0:T(8,128)(2,1)S(1)}, bf16[256,5120]{1,0:T(8,128)(2,1)}, u32[]{:S(2)}) %copy-start.4) | copy-done | bytes 2621464
  97.9 0.0 copy-start.2
  97.9 2.2 %term.3 = bf16[5120,128]{1,0:T(8,128)(2,1)} custom-call(s32[1]{0:T(128)S(6)} %sub.45.pick_ref, bf16[256,5120]{1,0:T(8,128)(2,1)S(1)} %copy-done.1, bf16[256,5120]{1,0:T(8,128)(2,1)S(1)} %copy-done.4, f32[256,128]{1,0:T(8,128)S(1)} %get-tuple-element.19.values_ref, bf16[256,128]{1,0:T(8,128)(2,1)S(1)} %get-tuple-element.20.half_ref, f32[256,1]{1,0:T(8,128)S(1)} %copy.53.factor_ref), custom_call_target="tpu_custom_call" | custom-call | flops 335544320 | bytes 5242880 | tf_op jit(solution)/shard_map/term/pallas_call | solution.py:254
  100.1 3.9 %collective-permute-start.2 = (bf16[5120,128]{1,0:T(8,128)(2,1)}, bf16[5120,128]{1,0:T(8,128)(2,1)}, u32[]{:S(2)}, u32[]{:S(2)}) collective-permute-start(bf16[5120,128]{1,0:T(8,128)(2,1)} %term.3), channel_id=1, source_target_pairs={{0,1},{1,0},{2,3},{3,2},{4,5},{5,4},{6,7},{7,6},{8,9},{9,8},{10,11... | collective-permute-start | bytes 3932168 | tf_op jit(solution)/shard_map/reduce/ppermute | solution.py:349
  104.0 0.6 fusion.4
  105.9 0.0 copy-done.2
  105.9 0.0 copy-start.5
  105.9 1.7 %copy-done.5 = bf16[256,5120]{1,0:T(8,128)(2,1)S(1)} copy-done((bf16[256,5120]{1,0:T(8,128)(2,1)S(1)}, bf16[256,5120]{1,0:T(8,128)(2,1)}, u32[]{:S(2)}) %copy-start.5) | copy-done | bytes 2621464
  107.7 1.7 term.2
  109.4 0.0 collective-permute-done.2
  109.4 1.7 add_convert_fusion
  111.0 1.2 copy.55
  112.2 3.6 %all-to-all-start.3 = ((bf16[8,640,128]{2,1,0:T(8,128)(2,1)}), bf16[8,640,128]{2,1,0:T(8,128)(2,1)S(1)}, u32[]{:S(2)}, u32[]{:S(2)}) async-start(bf16[8,640,128]{2,1,0:T(8,128)(2,1)} %bitcast.23), calls=%async_computation.3 | async-start | bytes 2621440 | tf_op jit(solution)/shard_map/reduce/all_to_all | solution.py:358
  115.8 0.1 maximum_bitcast_fusion
  115.9 18.6 %all-to-all-done.3 = bf16[8,640,128]{2,1,0:T(8,128)(2,1)S(1)} async-done(((bf16[8,640,128]{2,1,0:T(8,128)(2,1)}), bf16[8,640,128]{2,1,0:T(8,128)(2,1)S(1)}, u32[]{:S(2)}, u32[]{:S(2)}) %all-to-all-start.3) | async-done | bytes 1310752 | tf_op jit(solution)/shard_map/reduce/all_to_all | solution.py:358
  134.4 0.2 reduce_sum.102
  134.7 10.8 %all_to_all.32 = bf16[8,88,128]{2,1,0:T(8,128)(2,1)S(1)} all-to-all(bf16[8,88,128]{2,1,0:T(8,128)(2,1)S(1)} %pad_maximum_fusion), channel_id=1, replica_groups=mesh['yh'=4,'yl'=2,'x'=4,'zh'=2,'za'=3,'zb'=2,'c'=2] {'yh','yl'}, dimensions={0} | all-to-all | bytes 360448 | tf_op jit(solution)/shard_map/reduce/all_to_all | solution.py:361
  145.5 0.1 copy.57
  145.6 0.5 convert_reduce_fusion.1
  146.2 16.6 %all_to_all.33 = bf16[12,40,128]{2,1,0:T(8,128)(2,1)S(1)} all-to-all(bf16[12,40,128]{2,1,0:T(8,128)(2,1)S(1)} %bitcast.66), channel_id=1, replica_groups=mesh['yh'=4,'yl'=2,'x'=4,'zh'=2,'za'=3,'zb'=2,'c'=2] {'zh','za','zb'}, dimensions={0} | all-to-all | bytes 245760 | tf_op jit(solution)/shard_map/reduce/all_to_all | solution.py:368
  162.9 5.3 %all_gather.3 = f32[2,80,128]{2,1,0:T(8,128)S(1)} all-gather(f32[1,80,128]{2,1,0:T(8,128)S(1)} %bitcast.68), channel_id=1, replica_groups=mesh['yh'=4,'yl'=2,'x'=4,'zh'=2,'za'=3,'zb'=2,'c'=2] {'c'}, dimensions={0}, use_global_device_ids=true | all-gather | bytes 122880 | tf_op jit(solution)/shard_map/reduce/all_gather | solution.py:370
  168.2 0.6 slice_bitcast_fusion
  (16 shorter events, 0.2 us)
Async XLA Ops:
  2.1 0.7 collective-permute-start
  19.0 42.9 %copy-start.7 = (bf16[1,256,5120]{2,1,0:T(8,128)(2,1)S(1)}, bf16[1,256,5120]{2,1,0:T(8,128)(2,1)}, u32[]{:S(2)}) copy-start(bf16[1,256,5120]{2,1,0:T(8,128)(2,1)} %param.10) | copy-start | bytes 7864324
  55.6 7.0 %copy-start.8 = (s32[1,256]{1,0:T(1,128)S(1)}, s32[1,256]{1,0:T(1,128)}, u32[]{:S(2)}) copy-start(s32[1,256]{1,0:T(1,128)} %param.11) | copy-start | bytes 3076
  55.6 9.5 %copy-start.6 = (f32[128]{0:T(128)S(1)}, f32[128]{0:T(128)}, u32[]{:S(2)}) copy-start(f32[128]{0:T(128)} %param.14) | copy-start | bytes 1540
  55.6 9.1 %collective-permute-start.1 = (bf16[8,8,88,128]{3,2,1,0:T(8,128)(2,1)S(1)}, bf16[8,8,88,128]{3,2,1,0:T(8,128)(2,1)S(1)}, u32[]{:S(2)}, u32[]{:S(2)}) collective-permute-start(bf16[8,8,88,128]{3,2,1,0:T(8,128)(2,1)S(1)} %all_to_all.31.own_ref), channel_id=1, source_target_pairs={{0,1},{1,0},{2,3},{3,2},{4,5},{5,4},{6,7},{7,6},{8,9},{9,8},{10,11... | collective-permute-start | bytes 4325384 | tf_op jit(solution)/shard_map/gather/ppermute | solution.py:312
  65.2 15.4 %copy-start.9 = (s32[1,4,20]{2,1,0:T(4,128)S(1)}, s32[1,4,20]{2,1,0:T(4,128)}, u32[]{:S(2)}) copy-start(s32[1,4,20]{2,1,0:T(4,128)} %param.12) | copy-start | bytes 964
  72.9 1.5 copy-start
  74.4 18.4 %all-to-all-start.2 = ((f32[16,8,128]{2,1,0:T(8,128)}), f32[16,8,128]{2,1,0:T(8,128)S(1)}, u32[]{:S(2)}, u32[]{:S(2)}) async-start(f32[16,8,128]{2,1,0:T(8,128)} %get-tuple-element.21), calls=%async_computation.2 | async-start | bytes 131072 | tf_op jit(solution)/shard_map/stats/all_to_all | solution.py:330
  87.1 1.5 copy-start.3
  94.4 1.7 %copy-start.1 = (bf16[256,5120]{1,0:T(8,128)(2,1)S(1)}, bf16[256,5120]{1,0:T(8,128)(2,1)}, u32[]{:S(2)}) copy-start(bf16[256,5120]{1,0:T(8,128)(2,1)} %copy-done) | copy-start | bytes 7864324
  96.2 1.7 %copy-start.4 = (bf16[256,5120]{1,0:T(8,128)(2,1)S(1)}, bf16[256,5120]{1,0:T(8,128)(2,1)}, u32[]{:S(2)}) copy-start(bf16[256,5120]{1,0:T(8,128)(2,1)} %copy-done.3) | copy-start | bytes 7864324
  97.9 8.0 %copy-start.2 = (bf16[256,5120]{1,0:T(8,128)(2,1)S(1)}, bf16[256,5120]{1,0:T(8,128)(2,1)}, u32[]{:S(2)}) copy-start(bf16[256,5120]{1,0:T(8,128)(2,1)} %copy-done) | copy-start | bytes 7864324
  100.1 9.3 %collective-permute-start.2 = (bf16[5120,128]{1,0:T(8,128)(2,1)}, bf16[5120,128]{1,0:T(8,128)(2,1)}, u32[]{:S(2)}, u32[]{:S(2)}) collective-permute-start(bf16[5120,128]{1,0:T(8,128)(2,1)} %term.3), channel_id=1, source_target_pairs={{0,1},{1,0},{2,3},{3,2},{4,5},{5,4},{6,7},{7,6},{8,9},{9,8},{10,11... | collective-permute-start | bytes 3932168 | tf_op jit(solution)/shard_map/reduce/ppermute | solution.py:349
  105.9 1.7 %copy-start.5 = (bf16[256,5120]{1,0:T(8,128)(2,1)S(1)}, bf16[256,5120]{1,0:T(8,128)(2,1)}, u32[]{:S(2)}) copy-start(bf16[256,5120]{1,0:T(8,128)(2,1)} %copy-done.3) | copy-start | bytes 7864324
  112.2 22.2 %all-to-all-start.3 = ((bf16[8,640,128]{2,1,0:T(8,128)(2,1)}), bf16[8,640,128]{2,1,0:T(8,128)(2,1)S(1)}, u32[]{:S(2)}, u32[]{:S(2)}) async-start(bf16[8,640,128]{2,1,0:T(8,128)(2,1)} %bitcast.23), calls=%async_computation.3 | async-start | bytes 2621440 | tf_op jit(solution)/shard_map/reduce/all_to_all | solution.py:358

commit v6 on v5

--- a/solution.py
+++ b/solution.py
@@ -14,8 +14,8 @@
 XB = ("x", "zb")
 SWAP = [(0, 1), (1, 0)]
 LIST_DEVICES = 16
-VMEM_LIMIT = 48 * 1024 * 1024
-TERM_LIMIT = 16 * 1024 * 1024
+VMEM_LIMIT = 50 * 1024 * 1024
+TERM_LIMIT = 52 * 1024 * 1024
 F32 = jnp.float32
 BF16 = jnp.bfloat16
 
@@ -134,11 +134,9 @@
     scale_ref,
     weighted_ref,
     value_scale_ref,
-    unit_out,
+    unit_ref,
     values_ref,
     out_ref,
-    unit_ref,
-    sems,
 ):
     tokens, width = resid_ref.shape
     rows = width // (own_ref.shape[0] * own_ref.shape[1])
@@ -152,7 +150,6 @@
     def _():
         place(own_ref, rows, out_ref)
 
-    copies = []
     lead = columns_ref[:, 0:1]
     pull = columns_ref[:, 1:2]
     total = jnp.zeros(values_ref.shape, F32)
@@ -161,12 +158,8 @@
         slope = lead * weighted_ref[:, span] - pull * resid_ref[:, span].astype(F32)
         unit = (slope * scale_ref[:, span]).astype(BF16)
         unit_ref[:, span] = unit
-        copies.append(pltpu.make_async_copy(unit_ref.at[:, span], unit_out.at[:, span], sems.at[j]))
-        copies[-1].start()
         total = total + jnp.dot(unit, out_ref[span, :], preferred_element_type=F32)
     values_ref[...] = total * value_scale_ref[...]
-    for copy in copies:
-        copy.wait()
 
 
 def term_kernel(pick_ref, normed_ref, unit_ref, values_ref, half_ref, factor_ref, term_ref, small_ref):
@@ -224,7 +217,6 @@
     tokens, width = resid.shape
     head = value_scale.shape[1]
     vmem = pl.BlockSpec(memory_space=pltpu.VMEM)
-    far = pl.BlockSpec(memory_space=pltpu.HBM)
     return pl.pallas_call(
         backward_kernel,
         out_shape=(
@@ -232,12 +224,8 @@
             jax.ShapeDtypeStruct((tokens, head), F32),
         ),
         in_specs=[pl.BlockSpec(memory_space=pltpu.SMEM)] + [vmem] * 7,
-        out_specs=(far, vmem),
-        scratch_shapes=[
-            pltpu.VMEM((width, head), BF16),
-            pltpu.VMEM((tokens, width), BF16),
-            pltpu.SemaphoreType.DMA((width // 640,)),
-        ],
+        out_specs=(vmem,) * 2,
+        scratch_shapes=[pltpu.VMEM((width, head), BF16)],
         compiler_params=pltpu.CompilerParams(vmem_limit_bytes=VMEM_LIMIT),
         cost_estimate=pl.CostEstimate(
             flops=2 * tokens * width * head, bytes_accessed=8 * width * tokens, transcendentals=0
@@ -351,13 +339,13 @@
         both = (keep + got.astype(F32)).astype(BF16)
         loss_hi = own_loss.astype(BF16)
         loss_lo = (own_loss - loss_hi.astype(F32)).astype(BF16)
-        both, loss_hi, loss_lo = lax.optimization_barrier((both, loss_hi, loss_lo))
         loss_row = jnp.pad(jnp.stack([loss_hi, loss_lo])[None, :], ((0, 7), (0, head_size - 2)))
+        both, loss_row = lax.optimization_barrier((both, jnp.broadcast_to(loss_row, (8, 8, head_size))))
         half = rows // 2
         sent = both.reshape(8, 4, 2, 2, half, head_size).transpose(1, 3, 0, 2, 4, 5)
         came = lax.all_to_all(sent.reshape(8, 8 * rows, head_size), XB, 0, 0)
         part = jnp.sum(came.astype(F32), axis=0).astype(BF16).reshape(8, rows, head_size)
-        part = jnp.concatenate([part, jnp.broadcast_to(loss_row, (8, 8, head_size))], axis=1)
+        part = jnp.concatenate([part, loss_row], axis=1)
         came = lax.all_to_all(part, Y, 0, 0)
         losses = came.reshape(4, 2, rows + 8, head_size)[:, 0, rows, :2]
         list_loss = jnp.sum(losses.astype(F32), axis=-1)

time: 170 us -> 162 us (0.953)
  blocking collectives: 85.3 us -> 106 us
  waiting for transfers between devices: 24.6 us -> 8.17 us
  local copies, waits for them, and re-layouts: 11.2 us -> 1.88 us
  starting transfers between devices: 20.5 us -> 16.8 us
    all_to_all x0 -> x1, blocking collectives: none -> 20.8 us  [shards(): came = lax.all_to_all(sent.reshape(8, 8 * rows, head_size), XB, 0, 0)]
    all_to_all x1 -> x0, waiting for transfers between devices: 18.6 us -> none  [shards(): came = lax.all_to_all(sent.reshape(8, 8 * rows, head_size), XB, 0, 0)]
    unnamed x21 -> x9, local copies, waits for them, and re-layouts: 8.36 us -> 0.13 us
    all_to_all x1 -> x0, starting transfers between devices: 3.57 us -> none  [shards(): came = lax.all_to_all(sent.reshape(8, 8 * rows, head_size), XB, 0, 0)]
    pallas_call x2, Pallas kernels: 3.88 us -> 6.97 us  [run_term(): pl.pallas_call(term_kernel, out_shape=jax.ShapeDtypeStruct((width, head),...]
    all_to_all x1, waiting for transfers between devices: 4.14 us -> 6.26 us  [shards(): arrived = lax.all_to_all(stats, ('yl', 'x', 'zh'), 0, 0)]
  transfers between devices with their start and end apart: 5 -> 4, of which waited for: 3 -> 2; matrix products, arithmetic and copies ran while one was open for 1% -> 1% of each run, Pallas kernels for 4% -> 5%
where the time goes in v6:
time: 162 us
  blocking collectives  106 us (65%)
  Pallas kernels  18.2 us (11%)
  starting transfers between devices  16.8 us (10%)
  waiting for transfers between devices  8.17 us (5%)
  other arithmetic  7.03 us (4%)
  between operations  3.59 us (2%)
  local copies, waits for them, and re-layouts  1.88 us (1%)
    all_to_all x1, blocking collectives, shards(): own = lax.all_to_all(spread, XB, 0, 0)  36.7 us
    all_to_all x1, blocking collectives, shards(): came = lax.all_to_all(sent.reshape(8, 8 * rows, head_size), XB, 0, 0)  20.8 us
    all_to_all x1, blocking collectives, shards(): came = lax.all_to_all(part, Z, 0, 0).astype(F32)  16.4 us
    all_to_all x1, blocking collectives, shards(): lax.all_to_all(jnp.broadcast_to(block, (8,) + block.shape), Y, 0, 0)  15.9 us
    all_to_all x1, blocking collectives, shards(): came = lax.all_to_all(part, Y, 0, 0)  10.7 us
    pallas_call x2, Pallas kernels, run_term(): pl.pallas_call(term_kernel, out_shape=jax.ShapeDtypeStruct((width, head),...  6.97 us
    pallas_call x1, Pallas kernels, run_forward(): pl.pallas_call(forward_kernel, out_shape=(shape((tokens, width), BF16), s...  6.58 us
    all_to_all x1, waiting for transfers between devices, shards(): arrived = lax.all_to_all(stats, ('yl', 'x', 'zh'), 0, 0)  6.26 us
  transfers between devices with their start and end apart: 4, of which 2 were waited for; matrix products, arithmetic and copies ran while one was open for 1% of the time, Pallas kernels for 5%

profile of v6, /device:TPU:1, one launch (start us, length us, event | category | flops | bytes accessed | tf_op | source)
XLA Modules:
  0.0 161.7 jit_solution(11595267937714606435)
XLA Ops:
  0.6 0.7 broadcast_select_fusion.5
  1.4 0.7 broadcast_select_fusion.6
  2.1 0.7 collective-permute-start
  2.8 0.0 collective-permute-done
  2.9 15.9 %all_to_all.30 = bf16[8,88,128]{2,1,0:T(8,128)(2,1)S(1)} all-to-all(bf16[8,88,128]{2,1,0:T(8,128)(2,1)S(1)} %broadcast_in_dim.35), channel_id=1, replica_groups=mesh['yh'=4,'yl'=2,'x'=4,'zh'=2,'za'=3,'zb'=2,'c'=2] {'yh','yl'}, dimensions={0} | all-to-all | bytes 360448 | tf_op jit(solution)/shard_map/gather/all_to_all | solution.py:295
  18.8 0.2 broadcast_in_dim.36
  19.0 0.0 copy-start.1
  19.0 36.7 %all_to_all.31.own_ref = bf16[8,8,88,128]{3,2,1,0:T(8,128)(2,1)S(1)} all-to-all(bf16[8,8,88,128]{3,2,1,0:T(8,128)(2,1)S(1)} %broadcast_in_dim.36), channel_id=1, replica_groups=mesh['yh'=4,'yl'=2,'x'=4,'zh'=2,'za'=3,'zb'=2,'c'=2] {'x','zb'}, dimensions={0} | all-to-all | bytes 2883584 | tf_op jit(solution)/shard_map/gather/all_to_all | solution.py:297
  55.6 0.0 copy-start.2
  55.6 0.0 copy-start
  55.6 6.2 %collective-permute-start.1 = (bf16[8,8,88,128]{3,2,1,0:T(8,128)(2,1)S(1)}, bf16[8,8,88,128]{3,2,1,0:T(8,128)(2,1)S(1)}, u32[]{:S(2)}, u32[]{:S(2)}) collective-permute-start(bf16[8,8,88,128]{3,2,1,0:T(8,128)(2,1)S(1)} %all_to_all.31.own_ref), channel_id=1, source_target_pairs={{0,1},{1,0},{2,3},{3,2},{4,5},{5,4},{6,7},{7,6},{8,9},{9,8},{10,11... | collective-permute-start | bytes 4325384 | tf_op jit(solution)/shard_map/gather/ppermute | solution.py:300
  61.9 0.0 copy-done.1
  61.9 0.6 multiply_reduce_fusion
  62.5 0.1 copy.51.root_ref
  62.6 0.0 copy-done.2
  62.6 0.1 copy.52.segment_ref
  62.8 1.9 %collective-permute-done.1.beside_ref = bf16[8,8,88,128]{3,2,1,0:T(8,128)(2,1)S(1)} collective-permute-done((bf16[8,8,88,128]{3,2,1,0:T(8,128)(2,1)S(1)}, bf16[8,8,88,128]{3,2,1,0:T(8,128)(2,1)S(1)}, u32[]{:S(2)}, u32[]{:S(2)}) %collective-permute-start.1) | collective-permute-done | bytes 1441824 | tf_op jit(solution)/shard_map/gather/ppermute | solution.py:300
  64.7 0.1 fusion.1
  64.8 0.1 select_n.96.gain_ref
  64.9 0.1 select_n.100.scale_ref
  65.0 0.1 mul.26.weighted_ref
  65.1 0.0 copy-done
  65.2 0.0 copy-start.3
  65.2 6.6 %forward.1 = (bf16[256,5120]{1,0:T(8,128)(2,1)}, bf16[256,5120]{1,0:T(8,128)(2,1)}, bf16[256,128]{1,0:T(8,128)(2,1)S(1)}, f32[256,128]{1,0:T(8,128)S(1)}, f32[16,8,128]{2,1,0:T(8,128)}) custom-call(s32[1]{0:T(128)} %bitcast.core_ref.pick_ref, bf16[256,5120]{1,0:T(8,128)(2,1)} %bitcast.62, f32[256,1]{1,0:T(8,128)S(1)} %copy.51.root_ref, ...), custom_call_target="tpu_custom_call" | custom-call | flops 671088640 | bytes 15728640 | tf_op jit(solution)/shard_map/forward/pallas_call | solution.py:190
  71.8 6.2 %all-to-all-start.2 = ((f32[16,8,128]{2,1,0:T(8,128)}), f32[16,8,128]{2,1,0:T(8,128)S(1)}, u32[]{:S(2)}, u32[]{:S(2)}) async-start(f32[16,8,128]{2,1,0:T(8,128)} %get-tuple-element.20), calls=%async_computation.2 | async-start | bytes 131072 | tf_op jit(solution)/shard_map/stats/all_to_all | solution.py:318
  77.9 0.0 copy-done.3
  78.0 0.6 exponential_reduce_fusion
  79.3 4.6 %backward.1 = (bf16[256,5120]{1,0:T(8,128)(2,1)}, f32[256,128]{1,0:T(8,128)S(1)}) custom-call(s32[1]{0:T(128)} %bitcast.core_ref.pick_ref, bf16[256,5120]{1,0:T(8,128)(2,1)} %get-tuple-element.15.resid_ref, bf16[8,8,88,128]{3,2,1,0:T(8,128)(2,1)S(1)} %all_to_all.31.own_ref, bf16[8,8,88,128]{3,2,1,0:T(8,128)(2,1)S(1)} %collective-permute-done.1.beside_ref, ...), custom_call_target="tpu_custom_call" | custom-call | flops 335544320 | bytes 10485760 | tf_op jit(solution)/shard_map/backward/pallas_call | solution.py:220
  83.9 6.3 %all-to-all-done.2 = f32[16,8,128]{2,1,0:T(8,128)S(1)} async-done(((f32[16,8,128]{2,1,0:T(8,128)}), f32[16,8,128]{2,1,0:T(8,128)S(1)}, u32[]{:S(2)}, u32[]{:S(2)}) %all-to-all-start.2) | async-done | bytes 65568 | tf_op jit(solution)/shard_map/stats/all_to_all | solution.py:318
  90.2 0.6 exponential_reduce_fusion.1
  91.5 0.1 select_reduce_fusion
  91.6 0.1 copy.53.factor_ref
  91.8 2.8 %term.3 = bf16[5120,128]{1,0:T(8,128)(2,1)S(1)} custom-call(s32[1]{0:T(128)S(6)} %sub.45.pick_ref, bf16[256,5120]{1,0:T(8,128)(2,1)} %get-tuple-element.14.normed_ref, bf16[256,5120]{1,0:T(8,128)(2,1)} %get-tuple-element.17.unit_ref, f32[256,128]{1,0:T(8,128)S(1)} %get-tuple-element.18.values_ref, bf16[256,128]{1,0:T(8,128)(2,1)S(1)} %get-tuple-element.19.half_ref, ...), custom_call_target="tpu_custom_call" | custom-call | flops 335544320 | bytes 5242880 | tf_op jit(solution)/shard_map/term/pallas_call | solution.py:242
  94.6 3.7 %collective-permute-start.2 = (bf16[5120,128]{1,0:T(8,128)(2,1)S(1)}, bf16[5120,128]{1,0:T(8,128)(2,1)S(1)}, u32[]{:S(2)}, u32[]{:S(2)}) collective-permute-start(bf16[5120,128]{1,0:T(8,128)(2,1)S(1)} %term.3), channel_id=1, source_target_pairs={{0,1},{1,0},{2,3},{3,2},{4,5},{5,4},{6,7},{7,6},{8,9},{9,8},{10,11... | collective-permute-start | bytes 3932168 | tf_op jit(solution)/shard_map/reduce/ppermute | solution.py:337
  98.3 0.6 fusion.4
  100.2 0.1 maximum_bitcast_fusion
  100.3 4.2 %term.2 = f32[5120,128]{1,0:T(8,128)} custom-call(s32[1]{0:T(128)} %bitcast.core_ref.pick_ref, bf16[256,5120]{1,0:T(8,128)(2,1)} %get-tuple-element.14.normed_ref, bf16[256,5120]{1,0:T(8,128)(2,1)} %get-tuple-element.17.unit_ref, f32[256,128]{1,0:T(8,128)S(1)} %get-tuple-element.18.values_ref, bf16[256,128]{1,0:T(8,128)(2,1)S(1)} %get-tuple-element.19.half_ref, ...), custom_call_target="tpu_custom_call" | custom-call | flops 335544320 | bytes 5242880 | tf_op jit(solution)/shard_map/reduce/term/pallas_call | solution.py:242
  104.5 0.0 collective-permute-done.2
  104.5 2.0 %add_convert_fusion = bf16[5120,128]{1,0:T(8,128)(2,1)S(1)} fusion(f32[5120,128]{1,0:T(8,128)} %term.2, bf16[5120,128]{1,0:T(8,128)(2,1)S(1)} %collective-permute-done.2), kind=kLoop, calls=%fused_computation.1 | loop fusion | flops 1966080 | bytes 5242880 | tf_op jit(solution)/shard_map/reduce/convert_element_type | solution.py:339
  106.5 0.1 copy.55
  106.6 20.8 %all_to_all.32 = bf16[8,640,128]{2,1,0:T(8,128)(2,1)S(1)} all-to-all(bf16[8,640,128]{2,1,0:T(8,128)(2,1)S(1)} %bitcast.64), channel_id=1, replica_groups=mesh['yh'=4,'yl'=2,'x'=4,'zh'=2,'za'=3,'zb'=2,'c'=2] {'x','zb'}, dimensions={0} | all-to-all | bytes 2621440 | tf_op jit(solution)/shard_map/reduce/all_to_all | solution.py:346
  127.4 0.2 reduce_sum.102
  127.6 10.7 %all_to_all.33 = bf16[8,88,128]{2,1,0:T(8,128)(2,1)S(1)} all-to-all(bf16[8,88,128]{2,1,0:T(8,128)(2,1)S(1)} %pad_maximum_fusion), channel_id=1, replica_groups=mesh['yh'=4,'yl'=2,'x'=4,'zh'=2,'za'=3,'zb'=2,'c'=2] {'yh','yl'}, dimensions={0} | all-to-all | bytes 360448 | tf_op jit(solution)/shard_map/reduce/all_to_all | solution.py:349
  138.4 0.1 copy.57
  138.5 0.5 convert_reduce_fusion.1
  139.1 16.4 %all_to_all.34 = bf16[12,40,128]{2,1,0:T(8,128)(2,1)S(1)} all-to-all(bf16[12,40,128]{2,1,0:T(8,128)(2,1)S(1)} %bitcast.67), channel_id=1, replica_groups=mesh['yh'=4,'yl'=2,'x'=4,'zh'=2,'za'=3,'zb'=2,'c'=2] {'zh','za','zb'}, dimensions={0} | all-to-all | bytes 245760 | tf_op jit(solution)/shard_map/reduce/all_to_all | solution.py:356
  155.5 5.6 %all_gather.3 = f32[2,80,128]{2,1,0:T(8,128)S(1)} all-gather(f32[1,80,128]{2,1,0:T(8,128)S(1)} %bitcast.69), channel_id=1, replica_groups=mesh['yh'=4,'yl'=2,'x'=4,'zh'=2,'za'=3,'zb'=2,'c'=2] {'c'}, dimensions={0}, use_global_device_ids=true | all-gather | bytes 122880 | tf_op jit(solution)/shard_map/reduce/all_gather | solution.py:358
  161.1 0.6 slice_bitcast_fusion
  (16 shorter events, 0.2 us)
Async XLA Ops:
  2.1 0.7 collective-permute-start
  19.0 42.9 %copy-start.1 = (bf16[1,256,5120]{2,1,0:T(8,128)(2,1)S(1)}, bf16[1,256,5120]{2,1,0:T(8,128)(2,1)}, u32[]{:S(2)}) copy-start(bf16[1,256,5120]{2,1,0:T(8,128)(2,1)} %param.10) | copy-start | bytes 7864324
  55.6 7.0 %copy-start.2 = (s32[1,256]{1,0:T(1,128)S(1)}, s32[1,256]{1,0:T(1,128)}, u32[]{:S(2)}) copy-start(s32[1,256]{1,0:T(1,128)} %param.11) | copy-start | bytes 3076
  55.6 9.5 %copy-start = (f32[128]{0:T(128)S(1)}, f32[128]{0:T(128)}, u32[]{:S(2)}) copy-start(f32[128]{0:T(128)} %param.14) | copy-start | bytes 1540
  55.6 9.1 %collective-permute-start.1 = (bf16[8,8,88,128]{3,2,1,0:T(8,128)(2,1)S(1)}, bf16[8,8,88,128]{3,2,1,0:T(8,128)(2,1)S(1)}, u32[]{:S(2)}, u32[]{:S(2)}) collective-permute-start(bf16[8,8,88,128]{3,2,1,0:T(8,128)(2,1)S(1)} %all_to_all.31.own_ref), channel_id=1, source_target_pairs={{0,1},{1,0},{2,3},{3,2},{4,5},{5,4},{6,7},{7,6},{8,9},{9,8},{10,11... | collective-permute-start | bytes 4325384 | tf_op jit(solution)/shard_map/gather/ppermute | solution.py:300
  65.2 12.8 %copy-start.3 = (s32[1,4,20]{2,1,0:T(4,128)S(1)}, s32[1,4,20]{2,1,0:T(4,128)}, u32[]{:S(2)}) copy-start(s32[1,4,20]{2,1,0:T(4,128)} %param.12) | copy-start | bytes 964
  71.8 18.4 %all-to-all-start.2 = ((f32[16,8,128]{2,1,0:T(8,128)}), f32[16,8,128]{2,1,0:T(8,128)S(1)}, u32[]{:S(2)}, u32[]{:S(2)}) async-start(f32[16,8,128]{2,1,0:T(8,128)} %get-tuple-element.20), calls=%async_computation.2 | async-start | bytes 131072 | tf_op jit(solution)/shard_map/stats/all_to_all | solution.py:318
  94.6 9.9 %collective-permute-start.2 = (bf16[5120,128]{1,0:T(8,128)(2,1)S(1)}, bf16[5120,128]{1,0:T(8,128)(2,1)S(1)}, u32[]{:S(2)}, u32[]{:S(2)}) collective-permute-start(bf16[5120,128]{1,0:T(8,128)(2,1)S(1)} %term.3), channel_id=1, source_target_pairs={{0,1},{1,0},{2,3},{3,2},{4,5},{5,4},{6,7},{7,6},{8,9},{9,8},{10,11... | collective-permute-start | bytes 3932168 | tf_op jit(solution)/shard_map/reduce/ppermute | solution.py:337

commit v7 on v6

--- a/solution.py
+++ b/solution.py
@@ -14,6 +14,7 @@
 XB = ("x", "zb")
 SWAP = [(0, 1), (1, 0)]
 LIST_DEVICES = 16
+CANDS = 20
 VMEM_LIMIT = 50 * 1024 * 1024
 TERM_LIMIT = 52 * 1024 * 1024
 F32 = jnp.float32
@@ -29,11 +30,11 @@
 
 
 def place(source_ref, rows, target_ref):
-    pairs, ys = source_ref.shape[0], source_ref.shape[1]
-    for y in range(ys):
+    pairs = source_ref.shape[0]
+    for y in range(target_ref.shape[0] // (rows * pairs)):
         for k in range(pairs):
             at = rows * (y * pairs + k)
-            target_ref[at : at + rows, :] = source_ref[k, y, :rows, :]
+            target_ref[at : at + rows, :] = source_ref[k, rows * y : rows * (y + 1), :]
 
 
 def lane_fold(x):
@@ -45,7 +46,7 @@
 
 def forward_kernel(
     core_ref,
-    hidden_ref,
+    hidden_in,
     root_ref,
     own_ref,
     beside_ref,
@@ -63,11 +64,17 @@
     out_ref,
     normed_ref,
     resid_ref,
+    hidden_ref,
     sems,
 ):
     tokens, width = hidden_ref.shape
-    rows = width // (own_ref.shape[0] * own_ref.shape[1])
+    rows = width // 64
     tile = 640
+    loads = []
+    for j in range(width // tile):
+        span = slice(tile * j, tile * (j + 1))
+        loads.append(pltpu.make_async_copy(hidden_in.at[:, span], hidden_ref.at[:, span], sems.at[2, j]))
+        loads[-1].start()
 
     @pl.when(core_ref[0] == 0)
     def _():
@@ -84,6 +91,7 @@
     mixed = jnp.zeros((tokens, value_ref.shape[1]), F32)
     for j in range(width // tile):
         span = slice(tile * j, tile * (j + 1))
+        loads[j].wait()
         scaled = hidden_ref[:, span].astype(F32) * inverse
         normed = (scaled * gain_ref[:, span]).astype(BF16)
         normed_ref[:, span] = normed
@@ -139,7 +147,7 @@
     out_ref,
 ):
     tokens, width = resid_ref.shape
-    rows = width // (own_ref.shape[0] * own_ref.shape[1])
+    rows = width // 64
     tile = 640
 
     @pl.when(core_ref[0] == 0)
@@ -162,11 +170,40 @@
     values_ref[...] = total * value_scale_ref[...]
 
 
-def term_kernel(pick_ref, normed_ref, unit_ref, values_ref, half_ref, factor_ref, term_ref, small_ref):
+def list_factor(arrived_ref, teacher_ref, segment_ref):
+    stats = jnp.sum(arrived_ref[...], axis=0)
+    lanes = lax.broadcasted_iota(jnp.int32, (1, 128), 1)
+    real = lanes < CANDS
+    counts = jnp.where(real, stats[1:2, :], 1.0)
+    cand_score = jnp.where(real, stats[0:1, :] / counts, 0.0)
+    teacher = teacher_ref[...]
+    exp_teacher = jnp.where(real, jnp.exp(teacher), 0.0)
+    exp_student = jnp.where(real, jnp.exp(cand_score), 0.0)
+    log_teacher = teacher - jnp.log(jnp.sum(exp_teacher, axis=1, keepdims=True))
+    log_student = cand_score - jnp.log(jnp.sum(exp_student, axis=1, keepdims=True))
+    grad_cand = (jnp.exp(log_student) - jnp.exp(log_teacher)) / counts
+    places = lax.broadcasted_iota(jnp.int32, (segment_ref.shape[0], 128), 1)
+    member = segment_ref[...] == places
+    return jnp.sum(jnp.where(member, grad_cand, 0.0), axis=1, keepdims=True)
+
+
+def term_kernel(
+    pick_ref,
+    normed_ref,
+    unit_ref,
+    values_ref,
+    half_ref,
+    arrived_ref,
+    teacher_ref,
+    segment_ref,
+    term_ref,
+    small_ref,
+):
     @pl.when(pl.program_id(0) == 0)
     def _():
+        factor = list_factor(arrived_ref, teacher_ref, segment_ref)
         side = jnp.where(pick_ref[0] == 0, values_ref[...], half_ref[...].astype(F32))
-        small_ref[...] = (factor_ref[...] * side).T.astype(BF16)
+        small_ref[...] = (factor * side).T.astype(BF16)
 
     def fill(tall_ref):
         term = jnp.dot(small_ref[...], tall_ref[...], preferred_element_type=F32)
@@ -196,14 +233,15 @@
             shape((tokens, 128), F32),
             shape((LIST_DEVICES, 8, 128), F32),
         ),
-        in_specs=[pl.BlockSpec(memory_space=pltpu.SMEM)] + [vmem] * 9,
+        in_specs=[pl.BlockSpec(memory_space=pltpu.SMEM), far] + [vmem] * 8,
         out_specs=(far, far, vmem, vmem, vmem),
         scratch_shapes=[
             pltpu.VMEM((width, head), BF16),
             pltpu.VMEM((width, head), BF16),
             pltpu.VMEM((tokens, width), BF16),
             pltpu.VMEM((tokens, width), BF16),
-            pltpu.SemaphoreType.DMA((2, width // 640)),
+            pltpu.VMEM((tokens, width), BF16),
+            pltpu.SemaphoreType.DMA((3, width // 640)),
         ],
         compiler_params=pltpu.CompilerParams(vmem_limit_bytes=VMEM_LIMIT),
         cost_estimate=pl.CostEstimate(
@@ -234,14 +272,14 @@
     )(core, resid, own, beside, columns, scale, weighted, value_scale)
 
 
-def run_term(pick, normed, unit, values, half, factor, dtype):
+def run_term(pick, normed, unit, values, half, arrived, teacher, segment):
     tokens, width = normed.shape
     head = values.shape[1]
     tile = width // 2
     whole = lambda j, pick: (0, 0)
     return pl.pallas_call(
         term_kernel,
-        out_shape=jax.ShapeDtypeStruct((width, head), dtype),
+        out_shape=jax.ShapeDtypeStruct((width, head), BF16),
         grid_spec=pltpu.PrefetchScalarGridSpec(
             num_scalar_prefetch=1,
             grid=(width // tile,),
@@ -250,6 +288,8 @@
                 pl.BlockSpec((tokens, tile), lambda j, pick: (0, j * pick[0])),
                 pl.BlockSpec((tokens, head), whole),
                 pl.BlockSpec((tokens, head), whole),
+                pl.BlockSpec(arrived.shape, lambda j, pick: (0, 0, 0)),
+                pl.BlockSpec((1, 128), whole),
                 pl.BlockSpec((tokens, 1), whole),
             ],
             out_specs=pl.BlockSpec((tile, head), lambda j, pick: (j, 0)),
@@ -260,7 +300,7 @@
             flops=2 * tokens * width * head, bytes_accessed=4 * width * tokens, transcendentals=0
         ),
         name="term",
-    )(pick, normed, unit, values, half, factor)
+    )(pick, normed, unit, values, half, arrived, teacher, segment)
 
 
 def shards(
@@ -281,8 +321,6 @@
     tokens = hidden[0]
     width = tokens.shape[1]
     seg_local = segment[0][:, None]
-    grade_rows = grades[0]
-    cand_count = grade_rows.shape[1]
 
     with jax.named_scope("gather"):
         vectors = jnp.where(
@@ -293,6 +331,13 @@
         other = lax.ppermute(mine, Z, half_partner())
         block = jnp.where(lax.axis_index("zh") == lax.axis_index("zb"), mine, other)
         column = lax.all_to_all(jnp.broadcast_to(block, (8,) + block.shape), Y, 0, 0)
+        column = jnp.concatenate(
+            [
+                column[:, :rows].reshape(8 * rows, head_size),
+                column[:, rows : rows + 2].reshape(16, head_size),
+            ],
+            axis=0,
+        )
         spread = jnp.broadcast_to(column, (8,) + column.shape)
         own = lax.all_to_all(spread, XB, 0, 0)
         tokens32 = tokens.astype(F32)
@@ -300,7 +345,7 @@
         beside = lax.ppermute(own, "c", SWAP)
 
         def vector(block, which):
-            parts = block[:, :, rows + which, :rows]
+            parts = block[:, 8 * rows :, :rows].reshape(8, 8, 2, rows)[:, :, which]
             return jnp.swapaxes(parts, 0, 1).reshape(1, width).astype(F32)
 
         gain32 = jnp.where(first, vector(own, 0), vector(beside, 0))
@@ -319,24 +364,20 @@
 
     unit, values = run_backward(pick, resid, own, beside, columns, scale32, weighted, value_row)
 
-    with jax.named_scope("factor"):
+    teacher = lax.dynamic_index_in_dim(grades[0], lax.axis_index("yh"), 0, keepdims=True)
+    teacher = jnp.pad(teacher.astype(F32), ((0, 0), (0, head_size - CANDS)))
+
+    give = run_term(1 - pick, normed, unit, values, value_half, arrived, teacher, seg_local)
+    with jax.named_scope("reduce"):
+        got = lax.ppermute(give, "c", SWAP)
+        keep = run_term(pick, normed, unit, values, value_half, arrived, teacher, seg_local)
+        both = (keep.astype(F32) + got.astype(F32)).astype(BF16)
         stats = jnp.sum(arrived, axis=0)
-        sums, counts = stats[0, :cand_count], stats[1, :cand_count]
-        cand_score = sums / counts
-        teacher = lax.dynamic_index_in_dim(grade_rows, lax.axis_index("yh"), 0, keepdims=False)
-        teacher = teacher.astype(F32)
-        log_teacher = teacher - jnp.log(jnp.sum(jnp.exp(teacher)))
+        cand_score = stats[0, :CANDS] / stats[1, :CANDS]
+        grade = teacher[0, :CANDS]
+        log_teacher = grade - jnp.log(jnp.sum(jnp.exp(grade)))
         log_student = cand_score - jnp.log(jnp.sum(jnp.exp(cand_score)))
         own_loss = jnp.sum(jnp.exp(log_teacher) * (log_teacher - log_student))
-        grad_cand = (jnp.exp(log_student) - jnp.exp(log_teacher)) / counts
-        member = (seg_local == jnp.arange(cand_count, dtype=jnp.int32)).astype(F32)
-        factor = jnp.sum(member * grad_cand, axis=-1, keepdims=True)
-
-    give = run_term(1 - pick, normed, unit, values, value_half, factor, BF16)
-    with jax.named_scope("reduce"):
-        got = lax.ppermute(give, "c", SWAP)
-        keep = run_term(pick, normed, unit, values, value_half, factor, F32)
-        both = (keep + got.astype(F32)).astype(BF16)
         loss_hi = own_loss.astype(BF16)
         loss_lo = (own_loss - loss_hi.astype(F32)).astype(BF16)
         loss_row = jnp.pad(jnp.stack([loss_hi, loss_lo])[None, :], ((0, 7), (0, head_size - 2)))

time: 162 us -> 159 us (0.981)
  other arithmetic: 7.03 us -> 5.23 us
    convert_element_type x1 -> x2, other arithmetic: 2 us -> 0.35 us  [the longest x1 0.34 us: shards(): both = (keep.astype(F32) + got.astype(F32)).astype(BF16)]
  transfers between devices with their start and end apart: 4 -> 4, of which waited for: 2 -> 2; matrix products, arithmetic and copies ran while one was open for 1% -> 2% of each run, Pallas kernels for 5% -> 5%
where the time goes in v7:
time: 159 us
  blocking collectives  105 us (66%)
  starting transfers between devices  16.8 us (11%)
  Pallas kernels  16.6 us (10%)
  waiting for transfers between devices  9.29 us (6%)
  other arithmetic  5.23 us (3%)
  between operations  3.61 us (2%)
  local copies, waits for them, and re-layouts  1.83 us (1%)
    all_to_all x1, blocking collectives, shards(): own = lax.all_to_all(spread, XB, 0, 0)  35.7 us
    all_to_all x1, blocking collectives, shards(): came = lax.all_to_all(sent.reshape(8, 8 * rows, head_size), XB, 0, 0)  20.8 us
    all_to_all x1, blocking collectives, shards(): came = lax.all_to_all(part, Z, 0, 0).astype(F32)  16.4 us
    all_to_all x1, blocking collectives, shards(): lax.all_to_all(jnp.broadcast_to(block, (8,) + block.shape), Y, 0, 0)  15.9 us
    all_to_all x1, blocking collectives, shards(): came = lax.all_to_all(part, Y, 0, 0)  10.7 us
    all_to_all x1, waiting for transfers between devices, shards(): arrived = lax.all_to_all(stats, ('yl', 'x', 'zh'), 0, 0)  7.53 us
    all_to_all x1, starting transfers between devices, shards(): arrived = lax.all_to_all(stats, ('yl', 'x', 'zh'), 0, 0)  6.2 us
    ppermute x1, starting transfers between devices, shards(): beside = lax.ppermute(own, 'c', SWAP)  6.19 us
  transfers between devices with their start and end apart: 4, of which 2 were waited for; matrix products, arithmetic and copies ran while one was open for 2% of the time, Pallas kernels for 5%

profile of v7, /device:TPU:1, one launch (start us, length us, event | category | flops | bytes accessed | tf_op | source)
XLA Modules:
  0.0 158.5 jit_solution(16331109163764834817)
XLA Ops:
  0.6 0.7 broadcast_select_fusion.1
  1.4 0.7 broadcast_select_fusion.2
  2.1 0.7 collective-permute-start
  2.8 0.0 collective-permute-done
  2.9 15.9 %all_to_all.30 = bf16[8,88,128]{2,1,0:T(8,128)(2,1)S(1)} all-to-all(bf16[8,88,128]{2,1,0:T(8,128)(2,1)S(1)} %broadcast_in_dim.30), channel_id=1, replica_groups=mesh['yh'=4,'yl'=2,'x'=4,'zh'=2,'za'=3,'zb'=2,'c'=2] {'yh','yl'}, dimensions={0} | all-to-all | bytes 360448 | tf_op jit(solution)/shard_map/gather/all_to_all | solution.py:333
  18.8 0.2 broadcast_in_dim.31
  19.0 0.0 copy-start.1
  19.0 35.7 %all_to_all.31.own_ref = bf16[8,656,128]{2,1,0:T(8,128)(2,1)S(1)} all-to-all(bf16[8,656,128]{2,1,0:T(8,128)(2,1)S(1)} %broadcast_in_dim.31), channel_id=1, replica_groups=mesh['yh'=4,'yl'=2,'x'=4,'zh'=2,'za'=3,'zb'=2,'c'=2] {'x','zb'}, dimensions={0} | all-to-all | bytes 2686976 | tf_op jit(solution)/shard_map/gather/all_to_all | solution.py:342
  54.7 0.0 copy-start.2
  54.7 0.0 copy-start
  54.7 6.2 %collective-permute-start.1 = (bf16[8,656,128]{2,1,0:T(8,128)(2,1)S(1)}, bf16[8,656,128]{2,1,0:T(8,128)(2,1)S(1)}, u32[]{:S(2)}, u32[]{:S(2)}) collective-permute-start(bf16[8,656,128]{2,1,0:T(8,128)(2,1)S(1)} %all_to_all.31.own_ref), channel_id=1, source_target_pairs={{0,1},{1,0},{2,3},{3,2},{4,5},{5,4},{6,7},{7,6},{8,9},{9,8},{10,11... | collective-permute-start | bytes 4030472 | tf_op jit(solution)/shard_map/gather/ppermute | solution.py:345
  60.9 0.0 copy-done.1
  60.9 0.6 multiply_reduce_fusion
  61.5 0.1 copy.58.root_ref
  61.7 0.0 copy-done.2
  61.7 0.1 copy.59.segment_ref
  61.9 1.8 %collective-permute-done.1.beside_ref = bf16[8,656,128]{2,1,0:T(8,128)(2,1)S(1)} collective-permute-done((bf16[8,656,128]{2,1,0:T(8,128)(2,1)S(1)}, bf16[8,656,128]{2,1,0:T(8,128)(2,1)S(1)}, u32[]{:S(2)}, u32[]{:S(2)}) %collective-permute-start.1) | collective-permute-done | bytes 1343520 | tf_op jit(solution)/shard_map/gather/ppermute | solution.py:345
  63.6 0.1 fusion.8
  63.8 0.1 select_n.96.gain_ref
  63.9 0.1 select_n.100.scale_ref
  64.0 0.1 mul.16.weighted_ref
  64.1 0.0 copy-done
  64.1 0.0 copy-start.3
  64.1 6.1 %forward.1 = (bf16[256,5120]{1,0:T(8,128)(2,1)}, bf16[256,5120]{1,0:T(8,128)(2,1)}, bf16[256,128]{1,0:T(8,128)(2,1)S(1)}, f32[256,128]{1,0:T(8,128)S(1)}, f32[16,8,128]{2,1,0:T(8,128)}) custom-call(s32[1]{0:T(128)} %bitcast.core_ref.pick_ref, bf16[256,5120]{1,0:T(8,128)(2,1)} %bitcast.61, f32[256,1]{1,0:T(8,128)S(1)} %copy.58.root_ref, ...), custom_call_target="tpu_custom_call" | custom-call | flops 671088640 | bytes 15728640 | tf_op jit(solution)/shard_map/forward/pallas_call | solution.py:227
  70.2 6.2 %all-to-all-start.2 = ((f32[16,8,128]{2,1,0:T(8,128)}), f32[16,8,128]{2,1,0:T(8,128)S(1)}, u32[]{:S(2)}, u32[]{:S(2)}) async-start(f32[16,8,128]{2,1,0:T(8,128)} %get-tuple-element.20), calls=%async_computation.2 | async-start | bytes 131072 | tf_op jit(solution)/shard_map/stats/all_to_all | solution.py:363
  76.4 0.0 copy-done.3
  76.4 4.6 %backward.1 = (bf16[256,5120]{1,0:T(8,128)(2,1)}, f32[256,128]{1,0:T(8,128)S(1)}) custom-call(s32[1]{0:T(128)} %bitcast.core_ref.pick_ref, bf16[256,5120]{1,0:T(8,128)(2,1)} %get-tuple-element.15.resid_ref, bf16[8,656,128]{2,1,0:T(8,128)(2,1)S(1)} %all_to_all.31.own_ref, bf16[8,656,128]{2,1,0:T(8,128)(2,1)S(1)} %collective-permute-done.1.beside_ref, ...), custom_call_target="tpu_custom_call" | custom-call | flops 335544320 | bytes 10485760 | tf_op jit(solution)/shard_map/backward/pallas_call | solution.py:258
  81.1 7.5 %all-to-all-done.2.arrived_ref = f32[16,8,128]{2,1,0:T(8,128)S(1)} async-done(((f32[16,8,128]{2,1,0:T(8,128)}), f32[16,8,128]{2,1,0:T(8,128)S(1)}, u32[]{:S(2)}, u32[]{:S(2)}) %all-to-all-start.2) | async-done | bytes 65568 | tf_op jit(solution)/shard_map/stats/all_to_all | solution.py:363
  88.6 2.9 %term.3 = bf16[5120,128]{1,0:T(8,128)(2,1)S(1)} custom-call(s32[1]{0:T(128)S(6)} %sub.27.pick_ref, bf16[256,5120]{1,0:T(8,128)(2,1)} %get-tuple-element.14.normed_ref, bf16[256,5120]{1,0:T(8,128)(2,1)} %get-tuple-element.17.unit_ref, f32[256,128]{1,0:T(8,128)S(1)} %get-tuple-element.18.values_ref, bf16[256,128]{1,0:T(8,128)(2,1)S(1)} %get-tuple-element.19.half_ref, ...), custom_call_target="tpu_custom_call" | custom-call | flops 335544320 | bytes 5242880 | tf_op jit(solution)/shard_map/term/pallas_call | solution.py:280
  91.6 3.7 %collective-permute-start.2 = (bf16[5120,128]{1,0:T(8,128)(2,1)S(1)}, bf16[5120,128]{1,0:T(8,128)(2,1)S(1)}, u32[]{:S(2)}, u32[]{:S(2)}) collective-permute-start(bf16[5120,128]{1,0:T(8,128)(2,1)S(1)} %term.3), channel_id=1, source_target_pairs={{0,1},{1,0},{2,3},{3,2},{4,5},{5,4},{6,7},{7,6},{8,9},{9,8},{10,11... | collective-permute-start | bytes 3932168 | tf_op jit(solution)/shard_map/reduce/ppermute | solution.py:372
  95.3 0.6 exponential_reduce_fusion.1
  96.6 0.6 exponential_reduce_fusion
  97.9 0.6 fusion.7
  99.8 0.1 maximum_bitcast_fusion
  99.9 2.9 %term.2 = bf16[5120,128]{1,0:T(8,128)(2,1)S(1)} custom-call(s32[1]{0:T(128)} %bitcast.core_ref.pick_ref, bf16[256,5120]{1,0:T(8,128)(2,1)} %get-tuple-element.14.normed_ref, bf16[256,5120]{1,0:T(8,128)(2,1)} %get-tuple-element.17.unit_ref, f32[256,128]{1,0:T(8,128)S(1)} %get-tuple-element.18.values_ref, bf16[256,128]{1,0:T(8,128)(2,1)S(1)} %get-tuple-element.19.half_ref, ...), custom_call_target="tpu_custom_call" | custom-call | flops 335544320 | bytes 5242880 | tf_op jit(solution)/shard_map/reduce/term/pallas_call | solution.py:280
  102.9 0.0 collective-permute-done.2
  102.9 0.3 add_convert_fusion
  103.2 0.1 copy.62
  103.4 20.8 %all_to_all.32 = bf16[8,640,128]{2,1,0:T(8,128)(2,1)S(1)} all-to-all(bf16[8,640,128]{2,1,0:T(8,128)(2,1)S(1)} %bitcast.62), channel_id=1, replica_groups=mesh['yh'=4,'yl'=2,'x'=4,'zh'=2,'za'=3,'zb'=2,'c'=2] {'x','zb'}, dimensions={0} | all-to-all | bytes 2621440 | tf_op jit(solution)/shard_map/reduce/all_to_all | solution.py:387
  124.2 0.2 reduce_sum.92
  124.4 10.7 %all_to_all.33 = bf16[8,88,128]{2,1,0:T(8,128)(2,1)S(1)} all-to-all(bf16[8,88,128]{2,1,0:T(8,128)(2,1)S(1)} %pad_maximum_fusion), channel_id=1, replica_groups=mesh['yh'=4,'yl'=2,'x'=4,'zh'=2,'za'=3,'zb'=2,'c'=2] {'yh','yl'}, dimensions={0} | all-to-all | bytes 360448 | tf_op jit(solution)/shard_map/reduce/all_to_all | solution.py:390
  135.1 0.1 copy.68
  135.2 0.5 convert_reduce_fusion.1
  135.8 16.4 %all_to_all.34 = bf16[12,40,128]{2,1,0:T(8,128)(2,1)S(1)} all-to-all(bf16[12,40,128]{2,1,0:T(8,128)(2,1)S(1)} %bitcast.67), channel_id=1, replica_groups=mesh['yh'=4,'yl'=2,'x'=4,'zh'=2,'za'=3,'zb'=2,'c'=2] {'zh','za','zb'}, dimensions={0} | all-to-all | bytes 245760 | tf_op jit(solution)/shard_map/reduce/all_to_all | solution.py:397
  152.3 5.6 %all_gather.3 = f32[2,80,128]{2,1,0:T(8,128)S(1)} all-gather(f32[1,80,128]{2,1,0:T(8,128)S(1)} %bitcast.71), channel_id=1, replica_groups=mesh['yh'=4,'yl'=2,'x'=4,'zh'=2,'za'=3,'zb'=2,'c'=2] {'c'}, dimensions={0}, use_global_device_ids=true | all-gather | bytes 122880 | tf_op jit(solution)/shard_map/reduce/all_gather | solution.py:399
  157.9 0.6 slice_bitcast_fusion
  (20 shorter events, 0.3 us)
Async XLA Ops:
  2.1 0.7 collective-permute-start
  19.0 41.9 %copy-start.1 = (bf16[1,256,5120]{2,1,0:T(8,128)(2,1)S(1)}, bf16[1,256,5120]{2,1,0:T(8,128)(2,1)}, u32[]{:S(2)}) copy-start(bf16[1,256,5120]{2,1,0:T(8,128)(2,1)} %param.10) | copy-start | bytes 7864324
  54.7 7.0 %copy-start.2 = (s32[1,256]{1,0:T(1,128)S(1)}, s32[1,256]{1,0:T(1,128)}, u32[]{:S(2)}) copy-start(s32[1,256]{1,0:T(1,128)} %param.11) | copy-start | bytes 3076
  54.7 9.3 %copy-start = (f32[128]{0:T(128)S(1)}, f32[128]{0:T(128)}, u32[]{:S(2)}) copy-start(f32[128]{0:T(128)} %param.14) | copy-start | bytes 1540
  54.7 8.9 %collective-permute-start.1 = (bf16[8,656,128]{2,1,0:T(8,128)(2,1)S(1)}, bf16[8,656,128]{2,1,0:T(8,128)(2,1)S(1)}, u32[]{:S(2)}, u32[]{:S(2)}) collective-permute-start(bf16[8,656,128]{2,1,0:T(8,128)(2,1)S(1)} %all_to_all.31.own_ref), channel_id=1, source_target_pairs={{0,1},{1,0},{2,3},{3,2},{4,5},{5,4},{6,7},{7,6},{8,9},{9,8},{10,11... | collective-permute-start | bytes 4030472 | tf_op jit(solution)/shard_map/gather/ppermute | solution.py:345
  64.1 12.3 %copy-start.3 = (s32[1,4,20]{2,1,0:T(4,128)S(1)}, s32[1,4,20]{2,1,0:T(4,128)}, u32[]{:S(2)}) copy-start(s32[1,4,20]{2,1,0:T(4,128)} %param.12) | copy-start | bytes 964
  70.2 18.4 %all-to-all-start.2 = ((f32[16,8,128]{2,1,0:T(8,128)}), f32[16,8,128]{2,1,0:T(8,128)S(1)}, u32[]{:S(2)}, u32[]{:S(2)}) async-start(f32[16,8,128]{2,1,0:T(8,128)} %get-tuple-element.20), calls=%async_computation.2 | async-start | bytes 131072 | tf_op jit(solution)/shard_map/stats/all_to_all | solution.py:363
  91.6 11.3 %collective-permute-start.2 = (bf16[5120,128]{1,0:T(8,128)(2,1)S(1)}, bf16[5120,128]{1,0:T(8,128)(2,1)S(1)}, u32[]{:S(2)}, u32[]{:S(2)}) collective-permute-start(bf16[5120,128]{1,0:T(8,128)(2,1)S(1)} %term.3), channel_id=1, source_target_pairs={{0,1},{1,0},{2,3},{3,2},{4,5},{5,4},{6,7},{7,6},{8,9},{9,8},{10,11... | collective-permute-start | bytes 3932168 | tf_op jit(solution)/shard_map/reduce/ppermute | solution.py:372

commit v8 on v7

--- a/solution.py
+++ b/solution.py
@@ -184,7 +184,9 @@
     grad_cand = (jnp.exp(log_student) - jnp.exp(log_teacher)) / counts
     places = lax.broadcasted_iota(jnp.int32, (segment_ref.shape[0], 128), 1)
     member = segment_ref[...] == places
-    return jnp.sum(jnp.where(member, grad_cand, 0.0), axis=1, keepdims=True)
+    factor = jnp.sum(jnp.where(member, grad_cand, 0.0), axis=1, keepdims=True)
+    shares = jnp.exp(log_teacher) * (log_teacher - log_student)
+    return factor, jnp.sum(jnp.where(real, shares, 0.0), axis=1, keepdims=True)
 
 
 def term_kernel(
@@ -197,11 +199,16 @@
     teacher_ref,
     segment_ref,
     term_ref,
+    loss_ref,
     small_ref,
 ):
     @pl.when(pl.program_id(0) == 0)
     def _():
-        factor = list_factor(arrived_ref, teacher_ref, segment_ref)
+        factor, loss = list_factor(arrived_ref, teacher_ref, segment_ref)
+        high = jnp.broadcast_to(loss, loss_ref.shape).astype(BF16).astype(F32)
+        lanes = lax.broadcasted_iota(jnp.int32, loss_ref.shape, 1)
+        low = jnp.where(lanes == 1, loss - high, 0.0)
+        loss_ref[...] = jnp.where(lanes == 0, high, low)
         side = jnp.where(pick_ref[0] == 0, values_ref[...], half_ref[...].astype(F32))
         small_ref[...] = (factor * side).T.astype(BF16)
 
@@ -279,7 +286,10 @@
     whole = lambda j, pick: (0, 0)
     return pl.pallas_call(
         term_kernel,
-        out_shape=jax.ShapeDtypeStruct((width, head), BF16),
+        out_shape=(
+            jax.ShapeDtypeStruct((width, head), BF16),
+            jax.ShapeDtypeStruct((8, 128), F32),
+        ),
         grid_spec=pltpu.PrefetchScalarGridSpec(
             num_scalar_prefetch=1,
             grid=(width // tile,),
@@ -292,7 +302,10 @@
                 pl.BlockSpec((1, 128), whole),
                 pl.BlockSpec((tokens, 1), whole),
             ],
-            out_specs=pl.BlockSpec((tile, head), lambda j, pick: (j, 0)),
+            out_specs=(
+                pl.BlockSpec((tile, head), lambda j, pick: (j, 0)),
+                pl.BlockSpec((8, 128), whole),
+            ),
             scratch_shapes=[pltpu.VMEM((head, tokens), BF16)],
         ),
         compiler_params=pltpu.CompilerParams(vmem_limit_bytes=TERM_LIMIT),
@@ -367,21 +380,13 @@
     teacher = lax.dynamic_index_in_dim(grades[0], lax.axis_index("yh"), 0, keepdims=True)
     teacher = jnp.pad(teacher.astype(F32), ((0, 0), (0, head_size - CANDS)))
 
-    give = run_term(1 - pick, normed, unit, values, value_half, arrived, teacher, seg_local)
+    give, loss_row = run_term(1 - pick, normed, unit, values, value_half, arrived, teacher, seg_local)
     with jax.named_scope("reduce"):
         got = lax.ppermute(give, "c", SWAP)
-        keep = run_term(pick, normed, unit, values, value_half, arrived, teacher, seg_local)
+        keep, _ = run_term(pick, normed, unit, values, value_half, arrived, teacher, seg_local)
         both = (keep.astype(F32) + got.astype(F32)).astype(BF16)
-        stats = jnp.sum(arrived, axis=0)
-        cand_score = stats[0, :CANDS] / stats[1, :CANDS]
-        grade = teacher[0, :CANDS]
-        log_teacher = grade - jnp.log(jnp.sum(jnp.exp(grade)))
-        log_student = cand_score - jnp.log(jnp.sum(jnp.exp(cand_score)))
-        own_loss = jnp.sum(jnp.exp(log_teacher) * (log_teacher - log_student))
-        loss_hi = own_loss.astype(BF16)
-        loss_lo = (own_loss - loss_hi.astype(F32)).astype(BF16)
-        loss_row = jnp.pad(jnp.stack([loss_hi, loss_lo])[None, :], ((0, 7), (0, head_size - 2)))
-        both, loss_row = lax.optimization_barrier((both, jnp.broadcast_to(loss_row, (8, 8, head_size))))
+        loss_row = jnp.broadcast_to(loss_row.astype(BF16), (8, 8, head_size))
+        both, loss_row = lax.optimization_barrier((both, loss_row))
         half = rows // 2
         sent = both.reshape(8, 4, 2, 2, half, head_size).transpose(1, 3, 0, 2, 4, 5)
         came = lax.all_to_all(sent.reshape(8, 8 * rows, head_size), XB, 0, 0)

time: 159 us -> 155 us (0.975)
  between operations: 3.61 us -> 0.91 us
  waiting for transfers between devices: 9.29 us -> 6.92 us
    reduce_sum x4 -> x0, other arithmetic: 1.87 us -> none  [the longest x1 0.62 us: shards(): log_student = cand_score - jnp.log(jnp.sum(jnp.exp(cand_score)))]
    ppermute x1, waiting for transfers between devices: 1.75 us -> 0.01 us  [shards(): beside = lax.ppermute(own, 'c', SWAP)]
    reduce_sum x1, other arithmetic: 0.6 us -> 2.35 us  [shards(): jnp.mean(tokens32 * tokens32, axis=-1, keepdims=True) + EPSILON]
  transfers between devices with their start and end apart: 4 -> 4, of which waited for: 2 -> 1; matrix products, arithmetic and copies ran while one was open for 2% -> 2% of each run, Pallas kernels for 5% -> 5%
where the time goes in v8:
time: 155 us; the launch traced here: 154 us
  blocking collectives  105 us (68%)
  Pallas kernels  17.2 us (11%)
  starting transfers between devices  16.6 us (11%)
  waiting for transfers between devices  6.92 us (4%)
  other arithmetic  5.72 us (4%)
  local copies, waits for them, and re-layouts  1.82 us (1%)
    all_to_all x1, blocking collectives, shards(): own = lax.all_to_all(spread, XB, 0, 0)  35.5 us
    all_to_all x1, blocking collectives, shards(): came = lax.all_to_all(sent.reshape(8, 8 * rows, head_size), XB, 0, 0)  20.8 us
    all_to_all x1, blocking collectives, shards(): came = lax.all_to_all(part, Z, 0, 0).astype(F32)  16.4 us
    all_to_all x1, blocking collectives, shards(): lax.all_to_all(jnp.broadcast_to(block, (8,) + block.shape), Y, 0, 0)  15.9 us
    all_to_all x1, blocking collectives, shards(): came = lax.all_to_all(part, Y, 0, 0)  10.7 us
    all_to_all x1, waiting for transfers between devices, shards(): arrived = lax.all_to_all(stats, ('yl', 'x', 'zh'), 0, 0)  6.91 us
    pallas_call x2, Pallas kernels, run_term(): pl.pallas_call(term_kernel, out_shape=(jax.ShapeDtypeStruct((width, head)...  6.47 us
    all_to_all x1, starting transfers between devices, shards(): arrived = lax.all_to_all(stats, ('yl', 'x', 'zh'), 0, 0)  6.22 us
  transfers between devices with their start and end apart: 4, of which 1 were waited for; matrix products, arithmetic and copies ran while one was open for 2% of the time, Pallas kernels for 5%

profile of v8, /device:TPU:1, one launch (start us, length us, event | category | flops | bytes accessed | tf_op | source)
XLA Modules:
  0.0 154.1 jit_solution(8036120881336935856)
XLA Ops:
  0.6 0.7 broadcast_select_fusion.1
  1.4 0.7 broadcast_select_fusion.2
  2.1 0.7 collective-permute-start
  2.8 0.0 collective-permute-done
  2.9 15.9 %all_to_all.30 = bf16[8,88,128]{2,1,0:T(8,128)(2,1)S(1)} all-to-all(bf16[8,88,128]{2,1,0:T(8,128)(2,1)S(1)} %broadcast_in_dim.27), channel_id=1, replica_groups=mesh['yh'=4,'yl'=2,'x'=4,'zh'=2,'za'=3,'zb'=2,'c'=2] {'yh','yl'}, dimensions={0} | all-to-all | bytes 360448 | tf_op jit(solution)/shard_map/gather/all_to_all | solution.py:346
  18.8 0.2 broadcast_in_dim.28
  19.0 0.0 copy-start.1
  19.0 35.5 %all_to_all.31.own_ref = bf16[8,656,128]{2,1,0:T(8,128)(2,1)S(1)} all-to-all(bf16[8,656,128]{2,1,0:T(8,128)(2,1)S(1)} %broadcast_in_dim.28), channel_id=1, replica_groups=mesh['yh'=4,'yl'=2,'x'=4,'zh'=2,'za'=3,'zb'=2,'c'=2] {'x','zb'}, dimensions={0} | all-to-all | bytes 2686976 | tf_op jit(solution)/shard_map/gather/all_to_all | solution.py:355
  54.5 6.1 %collective-permute-start.1 = (bf16[8,656,128]{2,1,0:T(8,128)(2,1)S(1)}, bf16[8,656,128]{2,1,0:T(8,128)(2,1)S(1)}, u32[]{:S(2)}, u32[]{:S(2)}) collective-permute-start(bf16[8,656,128]{2,1,0:T(8,128)(2,1)S(1)} %all_to_all.31.own_ref), channel_id=1, source_target_pairs={{0,1},{1,0},{2,3},{3,2},{4,5},{5,4},{6,7},{7,6},{8,9},{9,8},{10,11... | collective-permute-start | bytes 4030472 | tf_op jit(solution)/shard_map/gather/ppermute | solution.py:358
  60.5 0.0 copy-done.1
  60.5 0.1 copy.59.segment_ref
  60.7 0.0 copy-start
  60.7 2.3 %multiply_reduce_fusion = f32[256]{0:T(256)S(1)} fusion(bf16[1,256,5120]{2,1,0:T(8,128)(2,1)} %param.10), kind=kLoop, calls=%fused_computation | loop fusion | flops 3931904 | bytes 2622464 | tf_op jit(solution)/shard_map/gather/reduce_sum | solution.py:357
  63.1 0.1 copy.58.root_ref
  63.2 0.0 collective-permute-done.1.beside_ref
  63.2 0.1 fusion.6
  63.4 0.1 mul.13.weighted_ref
  63.5 0.1 select_n.100.scale_ref
  63.6 0.1 select_n.96.gain_ref
  63.7 0.0 copy-done
  63.7 6.1 %forward.1 = (bf16[256,5120]{1,0:T(8,128)(2,1)}, bf16[256,5120]{1,0:T(8,128)(2,1)}, bf16[256,128]{1,0:T(8,128)(2,1)S(1)}, f32[256,128]{1,0:T(8,128)S(1)}, f32[16,8,128]{2,1,0:T(8,128)}) custom-call(s32[1]{0:T(128)} %bitcast.core_ref.pick_ref, bf16[256,5120]{1,0:T(8,128)(2,1)} %bitcast.46, f32[256,1]{1,0:T(8,128)S(1)} %copy.58.root_ref, ...), custom_call_target="tpu_custom_call" | custom-call | flops 671088640 | bytes 15728640 | tf_op jit(solution)/shard_map/forward/pallas_call | solution.py:234
  69.8 6.2 %all-to-all-start.2 = ((f32[16,8,128]{2,1,0:T(8,128)}), f32[16,8,128]{2,1,0:T(8,128)S(1)}, u32[]{:S(2)}, u32[]{:S(2)}) async-start(f32[16,8,128]{2,1,0:T(8,128)} %get-tuple-element.23), calls=%async_computation.2 | async-start | bytes 131072 | tf_op jit(solution)/shard_map/stats/all_to_all | solution.py:376
  76.0 0.7 convert_bitcast_fusion
  76.7 4.6 %backward.1 = (bf16[256,5120]{1,0:T(8,128)(2,1)}, f32[256,128]{1,0:T(8,128)S(1)}) custom-call(s32[1]{0:T(128)} %bitcast.core_ref.pick_ref, bf16[256,5120]{1,0:T(8,128)(2,1)} %get-tuple-element.18.resid_ref, bf16[8,656,128]{2,1,0:T(8,128)(2,1)S(1)} %all_to_all.31.own_ref, bf16[8,656,128]{2,1,0:T(8,128)(2,1)S(1)} %collective-permute-done.1.beside_ref, ...), custom_call_target="tpu_custom_call" | custom-call | flops 335544320 | bytes 10485760 | tf_op jit(solution)/shard_map/backward/pallas_call | solution.py:265
  81.4 6.9 %all-to-all-done.2.arrived_ref = f32[16,8,128]{2,1,0:T(8,128)S(1)} async-done(((f32[16,8,128]{2,1,0:T(8,128)}), f32[16,8,128]{2,1,0:T(8,128)S(1)}, u32[]{:S(2)}, u32[]{:S(2)}) %all-to-all-start.2) | async-done | bytes 65568 | tf_op jit(solution)/shard_map/stats/all_to_all | solution.py:376
  88.3 2.9 %term.3 = (bf16[5120,128]{1,0:T(8,128)(2,1)S(1)}, f32[8,128]{1,0:T(8,128)S(1)}) custom-call(s32[1]{0:T(128)S(6)} %sub.3.pick_ref, bf16[256,5120]{1,0:T(8,128)(2,1)} %get-tuple-element.17.normed_ref, bf16[256,5120]{1,0:T(8,128)(2,1)} %get-tuple-element.20.unit_ref, f32[256,128]{1,0:T(8,128)S(1)} %get-tuple-element.21.values_ref, ...), custom_call_target="tpu_custom_call" | custom-call | flops 335544320 | bytes 5242880 | tf_op jit(solution)/shard_map/term/pallas_call | solution.py:287
  91.2 3.7 %collective-permute-start.2 = (bf16[5120,128]{1,0:T(8,128)(2,1)S(1)}, bf16[5120,128]{1,0:T(8,128)(2,1)S(1)}, u32[]{:S(2)}, u32[]{:S(2)}) collective-permute-start(bf16[5120,128]{1,0:T(8,128)(2,1)S(1)} %get-tuple-element.25), channel_id=1, source_target_pairs={{0,1},{1,0},{2,3},{3,2},{4,5},{5,4},{6,7},{7,6},{8,9},{9,8},{10,11... | collective-permute-start | bytes 3932168 | tf_op jit(solution)/shard_map/reduce/ppermute | solution.py:385
  94.9 3.5 %term.2 = (bf16[5120,128]{1,0:T(8,128)(2,1)S(1)}, f32[8,128]{1,0:T(8,128)}) custom-call(s32[1]{0:T(128)} %bitcast.core_ref.pick_ref, bf16[256,5120]{1,0:T(8,128)(2,1)} %get-tuple-element.17.normed_ref, bf16[256,5120]{1,0:T(8,128)(2,1)} %get-tuple-element.20.unit_ref, f32[256,128]{1,0:T(8,128)S(1)} %get-tuple-element.21.values_ref, ...), custom_call_target="tpu_custom_call" | custom-call | flops 335544320 | bytes 5242880 | tf_op jit(solution)/shard_map/reduce/term/pallas_call | solution.py:287
  98.4 0.0 collective-permute-done.2
  98.5 0.3 add_convert_fusion
  98.8 0.1 copy.62
  98.9 20.8 %all_to_all.32 = bf16[8,640,128]{2,1,0:T(8,128)(2,1)S(1)} all-to-all(bf16[8,640,128]{2,1,0:T(8,128)(2,1)S(1)} %bitcast.47), channel_id=1, replica_groups=mesh['yh'=4,'yl'=2,'x'=4,'zh'=2,'za'=3,'zb'=2,'c'=2] {'x','zb'}, dimensions={0} | all-to-all | bytes 2621440 | tf_op jit(solution)/shard_map/reduce/all_to_all | solution.py:392
  119.8 0.2 reduce_sum.52
  120.0 10.7 %all_to_all.33 = bf16[8,88,128]{2,1,0:T(8,128)(2,1)S(1)} all-to-all(bf16[8,88,128]{2,1,0:T(8,128)(2,1)S(1)} %pad_maximum_fusion), channel_id=1, replica_groups=mesh['yh'=4,'yl'=2,'x'=4,'zh'=2,'za'=3,'zb'=2,'c'=2] {'yh','yl'}, dimensions={0} | all-to-all | bytes 360448 | tf_op jit(solution)/shard_map/reduce/all_to_all | solution.py:395
  130.7 0.1 copy.68
  130.8 0.5 convert_reduce_fusion.1
  131.4 16.4 %all_to_all.34 = bf16[12,40,128]{2,1,0:T(8,128)(2,1)S(1)} all-to-all(bf16[12,40,128]{2,1,0:T(8,128)(2,1)S(1)} %bitcast.52), channel_id=1, replica_groups=mesh['yh'=4,'yl'=2,'x'=4,'zh'=2,'za'=3,'zb'=2,'c'=2] {'zh','za','zb'}, dimensions={0} | all-to-all | bytes 245760 | tf_op jit(solution)/shard_map/reduce/all_to_all | solution.py:402
  147.8 5.6 %all_gather.3 = f32[2,80,128]{2,1,0:T(8,128)S(1)} all-gather(f32[1,80,128]{2,1,0:T(8,128)S(1)} %bitcast.56), channel_id=1, replica_groups=mesh['yh'=4,'yl'=2,'x'=4,'zh'=2,'za'=3,'zb'=2,'c'=2] {'c'}, dimensions={0}, use_global_device_ids=true | all-gather | bytes 122880 | tf_op jit(solution)/shard_map/reduce/all_gather | solution.py:404
  153.4 0.6 slice_bitcast_fusion
  (18 shorter events, 0.2 us)
Async XLA Ops:
  2.1 0.7 collective-permute-start
  19.0 41.5 %copy-start.1 = (s32[1,256]{1,0:T(1,128)S(1)}, s32[1,256]{1,0:T(1,128)}, u32[]{:S(2)}) copy-start(s32[1,256]{1,0:T(1,128)} %param.11) | copy-start | bytes 3076
  54.5 8.8 %collective-permute-start.1 = (bf16[8,656,128]{2,1,0:T(8,128)(2,1)S(1)}, bf16[8,656,128]{2,1,0:T(8,128)(2,1)S(1)}, u32[]{:S(2)}, u32[]{:S(2)}) collective-permute-start(bf16[8,656,128]{2,1,0:T(8,128)(2,1)S(1)} %all_to_all.31.own_ref), channel_id=1, source_target_pairs={{0,1},{1,0},{2,3},{3,2},{4,5},{5,4},{6,7},{7,6},{8,9},{9,8},{10,11... | collective-permute-start | bytes 4030472 | tf_op jit(solution)/shard_map/gather/ppermute | solution.py:358
  60.7 3.0 %copy-start = (f32[128]{0:T(128)S(1)}, f32[128]{0:T(128)}, u32[]{:S(2)}) copy-start(f32[128]{0:T(128)} %param.14) | copy-start | bytes 1540
  69.8 18.5 %all-to-all-start.2 = ((f32[16,8,128]{2,1,0:T(8,128)}), f32[16,8,128]{2,1,0:T(8,128)S(1)}, u32[]{:S(2)}, u32[]{:S(2)}) async-start(f32[16,8,128]{2,1,0:T(8,128)} %get-tuple-element.23), calls=%async_computation.2 | async-start | bytes 131072 | tf_op jit(solution)/shard_map/stats/all_to_all | solution.py:376
  91.2 7.2 %collective-permute-start.2 = (bf16[5120,128]{1,0:T(8,128)(2,1)S(1)}, bf16[5120,128]{1,0:T(8,128)(2,1)S(1)}, u32[]{:S(2)}, u32[]{:S(2)}) collective-permute-start(bf16[5120,128]{1,0:T(8,128)(2,1)S(1)} %get-tuple-element.25), channel_id=1, source_target_pairs={{0,1},{1,0},{2,3},{3,2},{4,5},{5,4},{6,7},{7,6},{8,9},{9,8},{10,11... | collective-permute-start | bytes 3932168 | tf_op jit(solution)/shard_map/reduce/ppermute | solution.py:385
